TPU v7x, 32 devices: a whole 2x2x4 slice. The times are simulated.
32 devices in a mesh: row: 8 (over z, y), col: 4 (over x, core).
Axes of the slice: x: 2, y: 2, z: 4, core: 2. Of those that a mesh axis runs over, the one named last changes fastest.
Arguments:
- feat_in: bfloat16 [256, 256, 256], P('row', 'col'), may hold values from -6 to 6
- conv_weight: bfloat16 [2304, 256], P('col'), may hold values from -0.125 to 0.125
- conv_bias: float32 [256], replicated, may hold values from -4 to 4
- proj_weight: bfloat16 [256, 768], replicated, may hold values from -0.375 to 0.375
- qkv_weight: bfloat16 [768, 2304], P('row'), may hold values from -2 to 2
- tissue: int32 [128, 128], P('row', 'col'), may hold values from 0 to 1, as said below
- phase: int32 [128, 128], P('row', 'col'), may hold values from 0 to 3, as said below
Outputs:
- attended: bfloat16 [128, 128, 768], P('row', 'col')
Inputs may be any that keep to these rules, and one draw needn't show every extreme that they name: Within each column strip, phase is the token column plus an offset drawn for each token row, modulo 4. In each device's block of tokens, every phase holds at least one tissue token.
All inputs are finite; a program needn't handle non-finite values.
Results may differ from a plain program's by a relative error of at most 0.0065.
Values may be sent and summed in bfloat16 or wider, within the bound.
No kernel may reach another device: no remote copies, remote signals or barrier semaphores. Data moves between devices by JAX's collectives and lax.ppermute only.
A program may use at most 64 MiB of HBM per device.

v0:
```python
import jax
import jax.numpy as jnp
from jax import lax
from jax.sharding import PartitionSpec as P

HD = 64
DILATION_STEP = 4


def partner(array, axis, apart):
    return lax.ppermute(array, axis, [(i, i ^ 1 << apart) for i in range(lax.axis_size(axis))])


def shifted(array, axis, by):
    length = lax.axis_size(axis)
    pairs = [(i, i + by) for i in range(length) if 0 <= i + by < length]
    return lax.ppermute(array, axis, pairs)


def layer_norm(values):
    centred = values - jnp.mean(values, axis=-1, keepdims=True)
    spread_rows = jnp.mean(centred * centred, axis=-1, keepdims=True)
    return centred * lax.rsqrt(spread_rows + 1e-05)


def fold_rows(operand, piece):
    return jnp.dot(operand, piece, preferred_element_type=jnp.float32)


def split_pair(buffer, bit, mine):
    slots = buffer.shape[0]
    view = buffer.reshape((slots >> bit + 1, 2, 1 << bit) + buffer.shape[1:])
    keep = jnp.where(mine == 0, view[:, 0], view[:, 1])
    send = jnp.where(mine == 0, view[:, 1], view[:, 0])
    return (keep, send)


def join_pair(keep, got, mine, shape):
    first = jnp.where(mine == 0, keep, got)
    second = jnp.where(mine == 0, got, keep)
    return jnp.stack([first, second], axis=1).reshape(shape)


def route_sender(payload, flags):
    mine_index = lax.axis_index("row")
    for bit in range(flag_bits(flags)):
        mine = mine_index >> bit & 1
        keep_a, send_a = split_pair(payload, bit, mine)
        keep_b, send_b = split_pair(flags, bit, mine)
        got_a, got_b = partner((send_a, send_b), "row", bit)
        payload = join_pair(keep_a, got_a, mine, payload.shape)
        flags = join_pair(keep_b, got_b, mine, flags.shape)
    return (payload, flags)


def route_back(payload):
    mine_index = lax.axis_index("row")
    for bit in range(flag_bits(payload)):
        mine = mine_index >> bit & 1
        keep_a, send_a = split_pair(payload, bit, mine)
        got_a = partner(send_a, "row", bit)
        payload = join_pair(keep_a, got_a, mine, payload.shape)
    return payload


def flag_bits(buffer):
    return buffer.shape[0].bit_length() - 1


def attend(queries, keys_all, values_all, key_live, query_live):
    row_count = queries.shape[0]
    model_width = queries.shape[1]
    head_count = model_width // HD
    query_heads = queries.reshape(row_count, head_count, HD).transpose(1, 0, 2)
    key_heads = keys_all.reshape(keys_all.shape[0], head_count, HD).transpose(1, 0, 2)
    value_heads = values_all.reshape(values_all.shape[0], head_count, HD).transpose(1, 0, 2)
    allowed = (key_live > 0.5)[None, :]

    def one_head(operands):
        query_head, key_head, value_head = operands
        scores = jnp.einsum(
            "qd,kd->qk", query_head, key_head, preferred_element_type=jnp.float32
        ) * HD ** (-0.5)
        scores = jnp.where(allowed, scores, -1e30)
        top_score = jnp.max(scores, axis=1, keepdims=True)
        weights = jnp.where(allowed, jnp.exp(scores - top_score), 0.0)
        denominator = jnp.sum(weights, axis=1, keepdims=True)
        return (
            jnp.dot(weights.astype(jnp.bfloat16), value_head, preferred_element_type=jnp.float32)
            / denominator
        )

    stacked = lax.map(one_head, (query_heads, key_heads, value_heads))
    merged = stacked.transpose(1, 0, 2).reshape(row_count, model_width)
    return (merged * query_live.astype(jnp.float32)[:, None]).astype(jnp.bfloat16)


def local(feat_in, conv_weight, conv_bias, proj_weight, qkv_weight, tissue, phase):
    in_rows, in_cols, channels = feat_in.shape
    out_rows = in_rows // 2
    out_cols = in_cols // 2
    token_count = out_rows * out_cols
    band_count = lax.axis_size("row")
    owner_labels = 2 * DILATION_STEP
    capacity = token_count // owner_labels
    model_width = qkv_weight.shape[0] * band_count
    left_edge = shifted(feat_in[:, in_cols - 1 :, :], "col", 1)
    widened = jnp.concatenate([left_edge, feat_in], axis=1)
    upper_edge = shifted(widened[in_rows - 1 :], "row", 1)
    padded = jnp.concatenate([upper_edge, widened], axis=0)
    windows = []
    for row_tap in range(3):
        for col_tap in range(3):
            window = padded[
                row_tap : row_tap + in_rows - 1 : 2, col_tap : col_tap + in_cols - 1 : 2, :
            ]
            windows.append(window.reshape(token_count, channels))
    patches = jnp.concatenate(windows, axis=1)
    conv_sum = fold_rows(patches, lax.all_gather(conv_weight, "col", axis=0, tiled=True))
    features = jax.nn.gelu(conv_sum + conv_bias).astype(jnp.bfloat16)
    tokens_bf = layer_norm(
        jnp.dot(features, proj_weight, preferred_element_type=jnp.float32)
    ).astype(jnp.bfloat16)
    phase_labels = phase.reshape(token_count)
    indicator_matrix = (
        phase_labels[:, None] == jnp.arange(DILATION_STEP, dtype=jnp.int32)[None, :]
    ).astype(jnp.int32)
    ranking = jnp.sum(
        (jnp.cumsum(indicator_matrix, axis=0) - indicator_matrix) * indicator_matrix, axis=1
    )
    target = (2 * phase_labels + ranking // capacity) * capacity + ranking % capacity
    inverse = (
        jnp.zeros((token_count,), jnp.int32)
        .at[target]
        .set(jnp.arange(token_count, dtype=jnp.int32))
    )
    tissue_flag = tissue.reshape(token_count).astype(jnp.bfloat16)
    flag_out = tissue_flag[inverse].reshape(owner_labels, capacity)
    qkv_local = fold_rows(tokens_bf, lax.all_gather(qkv_weight, "row", axis=0, tiled=True)).astype(
        jnp.bfloat16
    )
    arrived, arrived_flag = route_sender(
        qkv_local[inverse].reshape(owner_labels, capacity, 3 * model_width), flag_out
    )
    arrived_qkv = arrived.reshape(token_count, 3 * model_width)
    query_flag = arrived_flag.reshape(token_count)
    keys_values = arrived_qkv[:, model_width:]
    partner_kv, partner_flag = partner((keys_values, query_flag), "row", 0)
    joined_kv = jnp.concatenate([keys_values, partner_kv], axis=0)
    key_flag = jnp.concatenate([query_flag, partner_flag], axis=0)
    attended_rows = attend(
        arrived_qkv[:, :model_width],
        joined_kv[:, :model_width],
        joined_kv[:, model_width:],
        key_flag,
        query_flag,
    )
    returned = route_back(attended_rows.reshape(owner_labels, capacity, model_width))
    outputs = returned.reshape(token_count, model_width)[target]
    return outputs.reshape(out_rows, out_cols, model_width)


def solution(mesh):
    in_specs = (
        P("row", "col", None),
        P("col", None),
        P(),
        P(),
        P("row", None),
        P("row", "col"),
        P("row", "col"),
    )
    out_specs = P("row", "col", None)
    return jax.shard_map(local, mesh=mesh, in_specs=in_specs, out_specs=out_specs, check_vma=False)
```

profile of v0, /device:TPU:0, one launch (start us, length us, event | category | flops | bytes accessed | tf_op | source)
XLA Modules:
  0.0 370.1 jit_solution(18356025018190672156)
XLA Ops:
  9.0 2.4 collective-permute-start.4
  15.4 2.4 scatter_custom_fusion
  17.9 8.8 %slice.137 = bf16[16,32,256]{2,1,0:T(8,128)(2,1)} slice(bf16[32,64,256]{2,1,0:T(8,128)(2,1)} %param.9), slice={[0:31:2], [0:63:2], [0:256:1]} | slice | bytes 524288 | tf_op jit(solution)/shard_map/slice | solution.py:114
  28.9 4.3 %collective-permute-start.5 = (bf16[1,65,256]{2,1,0:T(8,128)(2,1)S(1)}, bf16[1,65,256]{2,1,0:T(8,128)(2,1)S(1)}, u32[]{:S(2)}, u32[]{:S(2)}) collective-permute-start(bf16[1,65,256]{2,1,0:T(8,128)(2,1)S(1)} %fusion.51), channel_id=1, source_target_pairs={{0,4},{4,8},{8,12},{12,16},{16,20},{20,24},{24,28},{1,5},{5,9},{9,... | collective-permute-start | bytes 99848 | tf_op jit(solution)/shard_map/ppermute | solution.py:17
  33.8 5.1 %slice.136 = bf16[16,32,256]{2,1,0:T(8,128)(2,1)} slice(bf16[32,65,256]{2,1,0:T(8,128)(2,1)S(1)} %pad_maximum_fusion.2), slice={[0:31:2], [0:63:2], [0:256:1]} | slice | bytes 524288 | tf_op jit(solution)/shard_map/slice | solution.py:114
  38.8 5.0 %slice.139 = bf16[16,32,256]{2,1,0:T(8,128)(2,1)} slice(bf16[32,65,256]{2,1,0:T(8,128)(2,1)S(1)} %pad_maximum_fusion.2), slice={[1:32:2], [0:63:2], [0:256:1]} | slice | bytes 524288 | tf_op jit(solution)/shard_map/slice | solution.py:114
  44.6 5.1 %slice.133 = bf16[16,32,256]{2,1,0:T(8,128)(2,1)} slice(bf16[33,65,256]{2,1,0:T(8,128)(2,1)S(1)} %maximum_maximum_fusion), slice={[0:31:2], [0:63:2], [0:256:1]} | slice | bytes 524288 | tf_op jit(solution)/shard_map/slice | solution.py:114
  50.9 1.7 constant_dynamic-update-slice_fusion.8
  58.7 3.5 fusion.67
  63.3 33.2 %all-gather.5.cloned.1.call-done = bf16[768,2304]{1,0:T(8,128)(2,1)} async-done(((bf16[96,2304]{1,0:T(8,128)(2,1)}), bf16[768,2304]{1,0:T(8,128)(2,1)}) %all-gather.5.cloned.1.call-update) | async-done | bytes 3538960 | tf_op jit(solution)/shard_map/all_gather | solution.py:139
  96.5 4.5 %convolution_convert_fusion = bf16[512,2304]{1,0:T(8,128)(2,1)S(1)} fusion(bf16[768,2304]{1,0:T(8,128)(2,1)} %all-gather.5.cloned.1.call-done, f32[512,768]{1,0:T(8,128)} %copy-done.4, f32[512]{0:T(512)S(1)} %add_rsqrt_fusion, f32[512]{0:T(512)S(1)} %broadcast_multiply_fusion.1), kind=kOutput, calls=%fused_computation.28 | convolution fusion | flops 1814298624 | bytes 7475200 | tf_op jit(solution)/shard_map/dot_general | solution.py:27
  101.1 3.4 gather_fusion.1
  104.5 2.9 fusion.23
  108.0 26.5 %collective-permute-done.6 = bf16[4,1,64,2304]{3,2,0,1:T(8,128)(2,1)} collective-permute-done((bf16[4,1,64,2304]{3,2,0,1:T(8,128)(2,1)}, bf16[4,1,64,2304]{3,2,0,1:T(8,128)(2,1)}, u32[]{:S(2)}, u32[]{:S(2)}) %collective-permute-start.6) | collective-permute-done | bytes 1179680 | tf_op jit(solution)/shard_map/ppermute | solution.py:11
  138.3 25.2 %collective-permute-done.7 = bf16[2,2,64,2304]{3,2,1,0:T(8,128)(2,1)} collective-permute-done((bf16[2,2,64,2304]{3,2,1,0:T(8,128)(2,1)}, bf16[2,2,64,2304]{3,2,1,0:T(8,128)(2,1)}, u32[]{:S(2)}, u32[]{:S(2)}) %collective-permute-start.7) | collective-permute-done | bytes 1179680 | tf_op jit(solution)/shard_map/ppermute | solution.py:11
  166.4 2.9 collective-permute-start.8
  169.4 3.5 gather_fusion
  173.0 45.9 %collective-permute-done.8 = bf16[1,4,64,2304]{3,2,1,0:T(8,128)(2,1)} collective-permute-done((bf16[1,4,64,2304]{3,2,1,0:T(8,128)(2,1)}, bf16[1,4,64,2304]{3,2,1,0:T(8,128)(2,1)}, u32[]{:S(2)}, u32[]{:S(2)}) %collective-permute-start.8) | collective-permute-done | bytes 1179680 | tf_op jit(solution)/shard_map/ppermute | solution.py:11
  222.2 1.8 collective-permute-start
  224.0 32.9 %collective-permute-done = bf16[4,1,64]{2,0,1:T(4,128)(2,1)S(1)} collective-permute-done((bf16[4,1,64]{2,0,1:T(4,128)(2,1)S(1)}, bf16[4,1,64]{2,0,1:T(4,128)(2,1)S(1)}, u32[]{:S(2)}, u32[]{:S(2)}) %collective-permute-start) | collective-permute-done | bytes 544 | tf_op jit(solution)/shard_map/ppermute | solution.py:11
  256.9 2.4 collective-permute-start.1
  259.3 1.5 collective-permute-done.1
  260.9 3.4 collective-permute-start.2
  264.3 1.5 collective-permute-done.2
  266.4 3.2 collective-permute-done.3
  270.8 2.0 pad_maximum_fusion.3
  272.9 1.7 copy.108
  275.3 41.6 %while.10 = (s32[]{:T(128)}, f32[12,512,64]{1,2,0:T(8,128)}, pred[1,1024]{1,0:T(4,128)(4,1)S(1)}, bf16[12,512,64]{1,2,0:T(8,128)(2,1)}, bf16[12,1024,64]{1,2,0:T...) while((s32[]{:T(128)}, f32[12,512,64]{1,2,0:T(8,128)}, ...), condition=%wide.region_9.10_spmd, body=%wide.region_6.9_spmd.sunk | while | flops 141065216 | bytes 6767702 | solution.py:93
  275.3 1.5 fusion.79
  278.8 1.5 fusion.79
  282.2 1.5 fusion.79
  285.7 1.5 fusion.79
  289.2 1.5 fusion.79
  292.7 1.5 fusion.79
  296.1 1.5 fusion.79
  303.1 1.5 fusion.79
  306.5 1.5 fusion.79
  310.0 1.5 fusion.79
  313.5 1.5 fusion.79
  316.9 3.6 reshape.533
  321.6 3.7 %broadcast_select_fusion.1 = (bf16[4,1,1,64,768]{3,1,0,4,2:T(2,128)(2,1)S(1)}, bf16[4,1,1,64,768]{3,1,0,4,2:T(2,128)(2,1)S(1)}) fusion(pred[]{:T(512)S(6)} %eq.28, bf16[4,2,1,64,768]{3,1,0,4,2:T(2,128)(2,1)S(1)} %multiply_convert_fusion), kind=kLoop, calls=%fused_computation.33 | loop fusion | flops 393216 | bytes 1572865 | tf_op jit(solution)/shard_map/jit(_where)/select_n | solution.py:33
  325.3 2.7 copy.114
  329.7 6.4 %collective-permute-done.10 = bf16[4,1,64,768]{3,2,0,1:T(8,128)(2,1)S(1)} collective-permute-done((bf16[4,1,64,768]{3,2,0,1:T(8,128)(2,1)}, bf16[4,1,64,768]{3,2,0,1:T(8,128)(2,1)S(1)}, u32[]{:S(2)}, u32[]{:S(2)}) %collective-permute-start.10) | collective-permute-done | bytes 393248 | tf_op jit(solution)/shard_map/ppermute | solution.py:11
  336.2 2.1 collective-permute-start.11
  338.3 8.7 %collective-permute-done.11 = bf16[2,2,64,768]{3,2,1,0:T(8,128)(2,1)S(1)} collective-permute-done((bf16[2,2,64,768]{3,2,1,0:T(8,128)(2,1)S(1)}, bf16[2,2,64,768]{3,2,1,0:T(8,128)(2,1)S(1)}, u32[]{:S(2)}, u32[]{:S(2)}) %collective-permute-start.11) | collective-permute-done | bytes 393248 | tf_op jit(solution)/shard_map/ppermute | solution.py:11
  347.3 3.0 collective-permute-start.12
  350.4 10.0 %collective-permute-done.12 = bf16[1,4,64,768]{3,2,1,0:T(8,128)(2,1)S(1)} collective-permute-done((bf16[1,4,64,768]{3,2,1,0:T(8,128)(2,1)S(1)}, bf16[1,4,64,768]{3,2,1,0:T(8,128)(2,1)S(1)}, u32[]{:S(2)}, u32[]{:S(2)}) %collective-permute-start.12) | collective-permute-done | bytes 393248 | tf_op jit(solution)/shard_map/ppermute | solution.py:11
  360.5 2.7 gather_fusion.2
  (148 shorter events, 60.1 us)
Async XLA Ops:
  6.5 52.2 %copy-start = (bf16[256,768]{1,0:T(8,128)(2,1)S(1)}, bf16[256,768]{1,0:T(8,128)(2,1)}, u32[]{:S(2)}) copy-start(bf16[256,768]{1,0:T(8,128)(2,1)} %param.12) | copy-start | bytes 1179652
  6.5 20.1 %copy-start.3 = (bf16[32,64,256]{2,1,0:T(8,128)(2,1)S(1)}, bf16[32,64,256]{2,1,0:T(8,128)(2,1)}, u32[]{:S(2)}) copy-start(bf16[32,64,256]{2,1,0:T(8,128)(2,1)} %param.9) | copy-start | bytes 3145732
  6.5 52.2 %all-gather.3.cloned.1.call-start = ((), (), s32[]{:S(2)}) async-start(), calls=%async_computation | async-start | bytes 1474560 | tf_op jit(solution)/shard_map/all_gather | solution.py:119
  7.3 89.3 %all-gather.5.cloned.1.call-start = ((), (), s32[]{:S(2)}) async-start(), calls=%async_computation.1 | async-start | bytes 3981312 | tf_op jit(solution)/shard_map/all_gather | solution.py:139
  9.0 19.9 %collective-permute-start.4 = (bf16[32,1,256]{2,1,0:T(2,128)(2,1)S(1)}, bf16[32,1,256]{2,1,0:T(2,128)(2,1)S(1)}, u32[]{:S(2)}, u32[]{:S(2)}) collective-permute-start(bf16[32,1,256]{2,1,0:T(2,128)(2,1)S(1)} %slice.131), channel_id=1, source_target_pairs={{0,1},{1,2},{2,3},{4,5},{5,6},{6,7},{8,9},{9,10},{10,11},{12,13},{... | collective-permute-start | bytes 49160 | tf_op jit(solution)/shard_map/ppermute | solution.py:17
  28.9 15.0 %collective-permute-start.5 = (bf16[1,65,256]{2,1,0:T(8,128)(2,1)S(1)}, bf16[1,65,256]{2,1,0:T(8,128)(2,1)S(1)}, u32[]{:S(2)}, u32[]{:S(2)}) collective-permute-start(bf16[1,65,256]{2,1,0:T(8,128)(2,1)S(1)} %fusion.51), channel_id=1, source_target_pairs={{0,4},{4,8},{8,12},{12,16},{16,20},{20,24},{24,28},{1,5},{5,9},{9,... | collective-permute-start | bytes 99848 | tf_op jit(solution)/shard_map/ppermute | solution.py:17
  44.6 9.5 %copy-start.7 = (bf16[16,32,256]{2,1,0:T(8,128)(2,1)S(1)}, bf16[16,32,256]{2,1,0:T(8,128)(2,1)}, u32[]{:S(2)}) copy-start(bf16[16,32,256]{2,1,0:T(8,128)(2,1)} %slice.136) | copy-start | bytes 786436
  49.7 5.2 %copy-start.5 = (bf16[16,32,256]{2,1,0:T(8,128)(2,1)S(1)}, bf16[16,32,256]{2,1,0:T(8,128)(2,1)}, u32[]{:S(2)}) copy-start(bf16[16,32,256]{2,1,0:T(8,128)(2,1)} %slice.137) | copy-start | bytes 786436
  50.8 5.5 %copy-start.6 = (bf16[16,32,256]{2,1,0:T(8,128)(2,1)S(1)}, bf16[16,32,256]{2,1,0:T(8,128)(2,1)}, u32[]{:S(2)}) copy-start(bf16[16,32,256]{2,1,0:T(8,128)(2,1)} %slice.139) | copy-start | bytes 786436
  54.1 4.6 %copy-start.9 = (f32[256]{0:T(256)S(1)}, f32[256]{0:T(256)}, u32[]{:S(2)}) copy-start(f32[256]{0:T(256)} %param.11) | copy-start | bytes 3076
  62.2 1.1 copy-start.4
  104.5 30.0 %copy-start.2 = (bf16[512,2304]{1,0:T(8,128)(2,1)S(1)}, bf16[512,2304]{1,0:T(8,128)(2,1)}, u32[]{:S(2)}) copy-start(bf16[512,2304]{1,0:T(8,128)(2,1)} %gather_fusion.1) | copy-start | bytes 7077892
  107.4 27.1 %collective-permute-start.6 = (bf16[4,1,64,2304]{3,2,0,1:T(8,128)(2,1)}, bf16[4,1,64,2304]{3,2,0,1:T(8,128)(2,1)}, u32[]{:S(2)}, u32[]{:S(2)}) collective-permute-start(bf16[4,1,64,2304]{3,2,0,1:T(8,128)(2,1)} %fusion.23), channel_id=1, source_target_pairs={{0,4},{4,0},{8,12},{12,8},{16,20},{20,16},{24,28},{28,24},{1,5},{5... | collective-permute-start | bytes 3538952 | tf_op jit(solution)/shard_map/ppermute | solution.py:11
  137.3 26.1 %collective-permute-start.7 = (bf16[2,2,64,2304]{3,2,1,0:T(8,128)(2,1)}, bf16[2,2,64,2304]{3,2,1,0:T(8,128)(2,1)}, u32[]{:S(2)}, u32[]{:S(2)}) collective-permute-start(bf16[2,2,64,2304]{3,2,1,0:T(8,128)(2,1)} %select_bitcast_fusion.1), channel_id=1, source_target_pairs={{0,8},{4,12},{8,0},{12,4},{16,24},{20,28},{24,16},{28,20},{1,9},{5... | collective-permute-start | bytes 3538952 | tf_op jit(solution)/shard_map/ppermute | solution.py:11
  165.2 4.1 %copy-start.8 = (s32[16,32]{1,0:T(8,128)S(1)}, s32[16,32]{1,0:T(8,128)}, u32[]{:S(2)}) copy-start(s32[16,32]{1,0:T(8,128)} %param.14) | copy-start | bytes 6148
  166.4 52.5 %collective-permute-start.8 = (bf16[1,4,64,2304]{3,2,1,0:T(8,128)(2,1)}, bf16[1,4,64,2304]{3,2,1,0:T(8,128)(2,1)}, u32[]{:S(2)}, u32[]{:S(2)}) collective-permute-start(bf16[1,4,64,2304]{3,2,1,0:T(8,128)(2,1)} %select_bitcast_fusion), channel_id=1, source_target_pairs={{0,16},{4,20},{8,24},{12,28},{16,0},{20,4},{24,8},{28,12},{1,17},{... | collective-permute-start | bytes 3538952 | tf_op jit(solution)/shard_map/ppermute | solution.py:11
  221.8 49.0 %collective-permute-start.9 = (bf16[512,1536]{1,0:T(8,128)(2,1)}, bf16[512,1536]{1,0:T(8,128)(2,1)}, u32[]{:S(2)}, u32[]{:S(2)}) collective-permute-start(bf16[512,1536]{1,0:T(8,128)(2,1)} %slice.180), channel_id=1, source_target_pairs={{0,4},{4,0},{8,12},{12,8},{16,20},{20,16},{24,28},{28,24},{1,5},{5... | collective-permute-start | bytes 4718600 | tf_op jit(solution)/shard_map/ppermute | solution.py:11
  222.2 34.7 %collective-permute-start = (bf16[4,1,64]{2,0,1:T(4,128)(2,1)S(1)}, bf16[4,1,64]{2,0,1:T(4,128)(2,1)S(1)}, u32[]{:S(2)}, u32[]{:S(2)}) collective-permute-start(bf16[4,1,64]{2,0,1:T(4,128)(2,1)S(1)} %bitcast.239), channel_id=1, source_target_pairs={{0,4},{4,0},{8,12},{12,8},{16,20},{20,16},{24,28},{28,24},{1,5},{5... | collective-permute-start | bytes 1544 | tf_op jit(solution)/shard_map/ppermute | solution.py:11
  256.9 4.0 %collective-permute-start.1 = (bf16[2,2,64]{2,1,0:T(2,128)(2,1)S(1)}, bf16[2,2,64]{2,1,0:T(2,128)(2,1)S(1)}, u32[]{:S(2)}, u32[]{:S(2)}) collective-permute-start(bf16[2,2,64]{2,1,0:T(2,128)(2,1)S(1)} %bitcast.240), channel_id=1, source_target_pairs={{0,8},{4,12},{8,0},{12,4},{16,24},{20,28},{24,16},{28,20},{1,9},{5... | collective-permute-start | bytes 1544 | tf_op jit(solution)/shard_map/ppermute | solution.py:11
  260.9 5.0 %collective-permute-start.2 = (bf16[1,4,64]{2,1,0:T(4,128)(2,1)S(1)}, bf16[1,4,64]{2,1,0:T(4,128)(2,1)S(1)}, u32[]{:S(2)}, u32[]{:S(2)}) collective-permute-start(bf16[1,4,64]{2,1,0:T(4,128)(2,1)S(1)} %select_bitcast_fusion.4), channel_id=1, source_target_pairs={{0,16},{4,20},{8,24},{12,28},{16,0},{20,4},{24,8},{28,12},{1,17},{... | collective-permute-start | bytes 1544 | tf_op jit(solution)/shard_map/ppermute | solution.py:11
  266.0 3.6 collective-permute-start.3
  328.1 8.0 %collective-permute-start.10 = (bf16[4,1,64,768]{3,2,0,1:T(8,128)(2,1)}, bf16[4,1,64,768]{3,2,0,1:T(8,128)(2,1)S(1)}, u32[]{:S(2)}, u32[]{:S(2)}) collective-permute-start(bf16[4,1,64,768]{3,2,0,1:T(8,128)(2,1)} %bitcast.55), channel_id=1, source_target_pairs={{0,4},{4,0},{8,12},{12,8},{16,20},{20,16},{24,28},{28,24},{1,5},{5... | collective-permute-start | bytes 1179656 | tf_op jit(solution)/shard_map/ppermute | solution.py:11
  336.2 10.8 %collective-permute-start.11 = (bf16[2,2,64,768]{3,2,1,0:T(8,128)(2,1)S(1)}, bf16[2,2,64,768]{3,2,1,0:T(8,128)(2,1)S(1)}, u32[]{:S(2)}, u32[]{:S(2)}) collective-permute-start(bf16[2,2,64,768]{3,2,1,0:T(8,128)(2,1)S(1)} %select_bitcast_fusion.3), channel_id=1, source_target_pairs={{0,8},{4,12},{8,0},{12,4},{16,24},{20,28},{24,16},{28,20},{1,9},{5... | collective-permute-start | bytes 1179656 | tf_op jit(solution)/shard_map/ppermute | solution.py:11
  347.3 13.0 %collective-permute-start.12 = (bf16[1,4,64,768]{3,2,1,0:T(8,128)(2,1)S(1)}, bf16[1,4,64,768]{3,2,1,0:T(8,128)(2,1)S(1)}, u32[]{:S(2)}, u32[]{:S(2)}) collective-permute-start(bf16[1,4,64,768]{3,2,1,0:T(8,128)(2,1)S(1)} %select_bitcast_fusion.2), channel_id=1, source_target_pairs={{0,16},{4,20},{8,24},{12,28},{16,0},{20,4},{24,8},{28,12},{1,17},{... | collective-permute-start | bytes 1179656 | tf_op jit(solution)/shard_map/ppermute | solution.py:11
  360.5 2.7 copy-start.1
Sparse Core Ops, SparseCore 0:
  8.9 20.1 all-gather.2
  31.3 65.1 all-gather.4
where the time goes:
time: 371 us; the launch traced here: 370 us
  waiting for transfers between devices  196 us (53%)
  local copies, waits for them, and re-layouts  63.7 us (17%)
  matrix products  41.6 us (11%)
  other arithmetic  29.8 us (8%)
  starting transfers between devices  24.7 us (7%)
  between operations  13.8 us (4%)
    ppermute x11, waiting for transfers between devices, partner(): lax.ppermute(array, axis, [(i, i ^ 1 << apart) for i in range(lax.axis_si...  162 us
    all_gather x1, waiting for transfers between devices, local(): lax.all_gather(qkv_weight, 'row', axis=0, tiled=True)  33.2 us
    slice x9, local copies, waits for them, and re-layouts, local(): padded[row_tap:row_tap + in_rows - 1:2, col_tap:col_tap + in_cols - 1:2, :]  27.2 us
    ppermute x11, starting transfers between devices, partner(): lax.ppermute(array, axis, [(i, i ^ 1 << apart) for i in range(lax.axis_si...  18.1 us
    dot_general x12, matrix products, one_head(): jnp.einsum('qd,kd->qk', query_head, key_head, preferred_element_type=jnp....  17.8 us
    dot_general x12, matrix products, one_head(): jnp.dot(weights.astype(jnp.bfloat16), value_head, preferred_element_type=...  15.8 us
    unnamed x29, local copies, waits for them, and re-layouts  7.92 us
    reduce_sum x12, other arithmetic, one_head(): denominator = jnp.sum(weights, axis=1, keepdims=True)  7.74 us
  transfers between devices with their start and end apart: 15, of which 11 were waited for; matrix products, arithmetic and copies ran while one was open for 15% of the time, Pallas kernels for 0%

commit v1 on v0

v1 whole, which is shorter than its diff:
```python
import functools
import math

import jax
import jax.numpy as jnp
from jax import lax
from jax.experimental import pallas as pl
from jax.experimental.pallas import tpu as pltpu
from jax.sharding import PartitionSpec as P

HD = 64
PHASES = 4
SEGMENT = 8
QBLOCK = 32
LANES = 128
BF16 = jnp.bfloat16
F32 = jnp.float32
NT = (((1,), (1,)), ((), ()))
TN = (((0,), (0,)), ((), ()))
VMEM = pltpu.VMEM
ANY = pl.ANY


def dot(a, b, dims=None):
    if dims is None:
        return jnp.dot(a, b, preferred_element_type=F32)
    return lax.dot_general(a, b, dims, preferred_element_type=F32)


def flip(array, axis, bits):
    return lax.ppermute(array, axis, [(i, i ^ bits) for i in range(lax.axis_size(axis))])


def shifted(array, axis):
    return lax.ppermute(array, axis, [(i, i + 1) for i in range(lax.axis_size(axis) - 1)])


def cornered(array):
    rows, cols = lax.axis_size("row"), lax.axis_size("col")
    pairs = [
        (i * cols + j, (i + 1) * cols + j + 1) for i in range(rows - 1) for j in range(cols - 1)
    ]
    return lax.ppermute(array, ("row", "col"), pairs)


def call(kernel, out_shape, in_spaces, out_spaces, scratch, args, cost, name):
    return pl.pallas_call(
        kernel,
        out_shape=out_shape,
        in_specs=[pl.BlockSpec(memory_space=s) for s in in_spaces],
        out_specs=(
            tuple(pl.BlockSpec(memory_space=s) for s in out_spaces)
            if isinstance(out_spaces, tuple)
            else pl.BlockSpec(memory_space=out_spaces)
        ),
        scratch_shapes=scratch,
        compiler_params=pltpu.CompilerParams(vmem_limit_bytes=40 * 1024 * 1024),
        cost_estimate=pl.CostEstimate(flops=cost[0], bytes_accessed=cost[1], transcendentals=0),
        name=name,
    )(*args)


def widen_kernel(x_ref, cls_ref, z_ref, pos_ref, wide):
    rows, cols, channels = x_ref.shape
    half = cols // 2
    tokens = cls_ref.shape[1]
    bucket = tokens // PHASES

    def one_row(r, carry):
        for c in range(channels // LANES):
            wide[r, c, pl.ds(0, 8), :] = jnp.zeros((8, LANES), F32)
            wide[r, c, pl.ds(8, cols), :] = x_ref[r, :, c * LANES : (c + 1) * LANES].astype(F32)
            for b in range(3):
                spot = b * channels + c * LANES
                z_ref[r % 2, r // 2, :, spot : spot + LANES] = wide[
                    r, c, pl.ds(7 + b, half, stride=2), :
                ].astype(BF16)
        return carry

    lax.fori_loop(0, rows, one_row, 0, unroll=2)

    classes = lax.broadcasted_iota(jnp.int32, (16, tokens), 0)
    cls = jnp.broadcast_to(cls_ref[...], (16, tokens))
    member = (classes == cls).astype(F32)
    earlier = (
        lax.broadcasted_iota(jnp.int32, (tokens, tokens), 0)
        < lax.broadcasted_iota(jnp.int32, (tokens, tokens), 1)
    ).astype(F32)
    rank = dot(member.astype(BF16), earlier.astype(BF16))
    odd = lax.rem(classes, 2) == 1
    live_before = jnp.where(odd & (classes - 1 == cls), 1.0, 0.0)
    start = (classes // 2 * bucket).astype(F32) + jnp.sum(live_before, axis=1, keepdims=True)
    place = jnp.sum(member * (rank + start), axis=0, keepdims=True).astype(jnp.int32)
    pos_ref[...] = jnp.broadcast_to(place, pos_ref.shape)


def conv_kernel(
    z_ref, w0, w1, w2, w3, left_ref, up_ref, corner_ref, bias_ref, proj_ref, pos_ref,
    out_ref, weight, edge, sems,
):
    out_rows, out_cols, wide = z_ref.shape[1:]
    channels = wide // 3
    tokens = out_rows * out_cols
    shard = w0.shape[0]
    mine = lax.axis_index("col")
    copies = []
    for j, ref in enumerate((w0, w1, w2, w3)):
        spot = pl.multiple_of((mine ^ j) * shard, 64)
        copies.append(pltpu.make_async_copy(ref, weight.at[pl.ds(spot, shard)], sems.at[j]))
        copies[-1].start()
    in_rows = left_ref.shape[0]
    corner = jnp.broadcast_to(corner_ref[...].astype(F32), (8, channels))
    halves = range(channels // LANES)
    for c in halves:
        few = slice(c * LANES, (c + 1) * LANES)
        edge[0, c, pl.ds(0, 8), :] = corner[:, few]
        edge[0, c, pl.ds(8, in_rows), :] = left_ref[:, few].astype(F32)
        edge[1, c, pl.ds(0, 8), :] = jnp.zeros((8, LANES), F32)
        edge[1, c, pl.ds(8, 2 * out_cols), :] = up_ref[:, few].astype(F32)

    def every_second(side, first, count):
        parts = [edge[side, c, pl.ds(first, count, stride=2), :] for c in halves]
        return jnp.concatenate(parts, axis=1).astype(BF16)

    lefts = [every_second(0, 7 + a, out_rows) for a in range(3)]
    ups = [every_second(1, 7 + b, out_cols) for b in range(3)]
    for copy in copies:
        copy.wait()
    even = z_ref[0].reshape(tokens, wide)
    odd = z_ref[1].reshape(tokens, wide)
    acc = dot(even, weight[wide : 2 * wide]) + dot(odd, weight[2 * wide : 3 * wide])
    above = dot(odd[: tokens - out_cols], weight[:wide])
    top = dot(jnp.concatenate(ups, axis=1), weight[:wide])
    acc = acc + jnp.concatenate([top, above], axis=0)
    side = sum(dot(lefts[a], weight[a * wide : a * wide + channels]) for a in range(3))
    grid = acc.reshape(out_rows, out_cols, channels)
    first = lax.broadcasted_iota(jnp.int32, grid.shape, 1) == 0
    grid = grid + jnp.where(first, side[:, None, :], 0.0)
    pre = grid.reshape(tokens, channels) + bias_ref[...]
    features = jax.nn.gelu(pre).astype(BF16)
    projected = dot(features, proj_ref[...])
    centred = projected - jnp.mean(projected, axis=1, keepdims=True)
    spread = jnp.mean(centred * centred, axis=1, keepdims=True)
    scaled = (features.astype(F32) * lax.rsqrt(spread + 1e-05)).astype(BF16)
    chosen = (
        lax.broadcasted_iota(jnp.int32, (tokens, tokens), 0)
        == jnp.broadcast_to(pos_ref[0:1], (tokens, tokens))
    ).astype(F32)
    out_ref[...] = dot(chosen.astype(BF16), scaled).astype(BF16)


def merge_kernel(ordered, *refs):
    pieces, (proj_ref, out_ref) = refs[:SEGMENT], refs[SEGMENT:]
    depth = pieces[0].shape[0]
    mine = 0 if ordered else lax.rem(lax.axis_index("row"), SEGMENT)
    mean = jnp.mean(proj_ref[...].astype(F32), axis=0, keepdims=True)
    total = None
    for j, piece in enumerate(pieces):
        spot = pl.multiple_of((mine ^ j) * depth, 32)
        part = proj_ref[pl.ds(spot, depth), :].astype(F32) - mean
        high = part.astype(BF16)
        low = (part - high.astype(F32)).astype(BF16)
        term = dot(piece[...], high, TN) + dot(piece[...], low, TN)
        total = term if total is None else total + term
    out_ref[...] = total.astype(BF16)


def query_kernel(f_ref, m0, m1, m2, m3, q_ref, v_ref, merged, sems):
    shard = m0.shape[0]
    width = 4 * shard // 3
    heads = width // HD
    blocks = q_ref.shape[0]
    mine = lax.axis_index("col")
    copies = []
    for j, ref in enumerate((m0, m1, m2, m3)):
        spot = pl.multiple_of((mine ^ j) * shard, 64)
        copies.append(pltpu.make_async_copy(ref, merged.at[pl.ds(spot, shard)], sems.at[j]))
        copies[-1].start()
    for copy in copies:
        copy.wait()
    f = f_ref[...]
    factor = math.log2(math.e) / math.sqrt(HD)
    lanes = lax.broadcasted_iota(jnp.int32, (1, 2 * HD), 1)
    for pair in range(heads // 2):
        both = slice(pair * 2 * HD, (pair + 1) * 2 * HD)
        queries = dot(f, merged[both], NT).astype(BF16).astype(F32)
        keys = merged[width + pair * 2 * HD : width + (pair + 1) * 2 * HD]
        for h in range(2):
            one = jnp.where(lanes // HD == h, queries, 0.0).astype(BF16)
            wide = (dot(one, keys) * factor).astype(BF16)
            q_ref[:, 2 * pair + h] = wide.reshape(blocks, QBLOCK, wide.shape[1])
    v_ref[...] = merged[2 * width :]


def attend_kernel(counts_ref, q_ref, v_ref, pos_ref, live_ref, *refs):
    items, (out_ref, rows32, keys, mixed) = refs[:SEGMENT], refs[SEGMENT:]
    blocks, heads, qblock, channels = q_ref.shape
    tokens = items[0].shape[0]
    bucket = tokens // PHASES
    per_phase = blocks // PHASES
    group = SEGMENT * bucket
    mine = lax.rem(lax.axis_index("row"), SEGMENT)
    step = 256
    halves = range(channels // LANES)

    for p in range(PHASES):
        filled = 0
        for j in range(SEGMENT):
            for c in halves:
                rows32[c, pl.ds(filled, bucket), :] = items[j][
                    p * bucket : (p + 1) * bucket, c * LANES : (c + 1) * LANES
                ].astype(F32)
            filled = filled + counts_ref[mine ^ j, p]
        for c in halves:
            rows32[c, pl.ds(filled, step), :] = jnp.zeros((step, LANES), F32)
        own = counts_ref[mine, p]
        block_count = (own + qblock - 1) // qblock

        for width in range(step, group + 1, step):

            @pl.when((filled > width - step) & (filled <= width))
            def _():
                for c in halves:
                    keys[0:width, c * LANES : (c + 1) * LANES] = rows32[c, 0:width, :].astype(BF16)
                bias = jnp.where(
                    lax.broadcasted_iota(jnp.int32, (1, width), 1) < filled, 0.0, -1e30
                )

                def one_block(b, carry):
                    spot = p * per_phase + b
                    for part in range(3):
                        few = slice(part * heads // 3, (part + 1) * heads // 3)
                        q = q_ref[spot, few].reshape(heads // 3 * qblock, channels)
                        k = keys[0:width, :]
                        scores = dot(q, k, NT) + bias
                        weights = jnp.exp2(scores - jnp.max(scores, axis=1, keepdims=True))
                        total = jnp.sum(weights, axis=1, keepdims=True)
                        mix = dot(weights.astype(BF16), k) / total
                        mixed[spot, few] = mix.astype(BF16).reshape(heads // 3, qblock, channels)
                    return carry

                lax.fori_loop(0, block_count, one_block, 0)

        def no_block(b, carry):
            mixed[p * per_phase + b] = jnp.zeros((heads, qblock, channels), BF16)
            return carry

        lax.fori_loop(block_count, per_phase, no_block, 0)

    heads_out = []
    for h in range(heads):
        heads_out.append(
            dot(mixed[:, h].reshape(tokens, channels), v_ref[h * HD : (h + 1) * HD], NT)
        )
    ordered = jnp.concatenate(heads_out, axis=1).astype(BF16)
    chosen = (
        (
            lax.broadcasted_iota(jnp.int32, (tokens, tokens), 0)
            == jnp.broadcast_to(pos_ref[0:1], (tokens, tokens))
        )
        & (jnp.broadcast_to(live_ref[...], (tokens, tokens)) > 0)
    ).astype(F32)
    out_ref[...] = dot(chosen.astype(BF16), ordered, TN).astype(BF16)


def local(feat_in, conv_weight, conv_bias, proj_weight, qkv_weight, tissue, phase):
    in_rows, in_cols, channels = feat_in.shape
    out_rows, out_cols = in_rows // 2, in_cols // 2
    tokens = out_rows * out_cols
    row_count, col_count = lax.axis_size("row"), lax.axis_size("col")
    depth, out_width = qkv_weight.shape
    width = out_width // 3
    heads = width // HD
    share = out_width // col_count

    weight_x = flip(conv_weight, "col", 2)
    weight_core = flip(conv_weight, "col", 1)
    left = shifted(feat_in[:, in_cols - 1, :], "col")
    up = shifted(feat_in[in_rows - 1], "row")
    corner = cornered(feat_in[in_rows - 1, in_cols - 1 :, :])
    weight_far = flip(weight_x, "col", 1)

    qkv_mine = lax.dynamic_slice(
        qkv_weight, (0, lax.axis_index("col") * share), (depth, share)
    )
    ordered = row_count != SEGMENT
    if ordered:
        whole = lax.all_gather(qkv_mine, "row", axis=0, tiled=True)
        pieces = list(whole.reshape(SEGMENT, width // SEGMENT, share))
    else:
        z_pieces = [qkv_mine] + [flip(qkv_mine, "row", 2 * k) for k in (1, 2, 3)]
        y_pieces = flip(jnp.concatenate(z_pieces, axis=0), "row", 1)
        pieces = []
        for k in range(4):
            pieces += [z_pieces[k], y_pieces[k * depth : (k + 1) * depth]]

    live = tissue.reshape(1, tokens)
    cls = phase.reshape(1, tokens) * 2 + (1 - live)
    here = (phase[None] == jnp.arange(PHASES, dtype=jnp.int32)[:, None, None]) & (tissue[None] > 0)
    own_counts = jnp.sum(here.astype(jnp.int32), axis=(1, 2)).reshape(1, PHASES)
    groups = [
        [s * SEGMENT + i for i in range(SEGMENT)] for s in range(row_count // SEGMENT)
    ]
    counts = lax.all_gather(own_counts, "row", axis=0, tiled=True, axis_index_groups=groups)

    z, pos = call(
        widen_kernel,
        (
            jax.ShapeDtypeStruct((2, out_rows, out_cols, 3 * channels), BF16),
            jax.ShapeDtypeStruct((8, tokens), jnp.int32),
        ),
        [VMEM, VMEM],
        (VMEM, VMEM),
        [VMEM((in_rows, channels // LANES, in_cols + 8, LANES), F32)],
        (feat_in, cls),
        (1 << 24, 5 << 20),
        "widen",
    )
    mine = call(
        conv_kernel,
        jax.ShapeDtypeStruct((tokens, channels), BF16),
        [VMEM, ANY, ANY, ANY, ANY, VMEM, VMEM, VMEM, VMEM, VMEM, VMEM],
        VMEM,
        [
            VMEM((9 * channels, channels), BF16),
            VMEM((2, channels // LANES, in_cols + 8, LANES), F32),
            pltpu.SemaphoreType.DMA((4,)),
        ],
        (
            z, conv_weight, weight_core, weight_x, weight_far, left, up, corner,
            conv_bias.reshape(1, channels), proj_weight, pos,
        ),
        (1 << 30, 6 << 20),
        "conv",
    )

    z_items = [mine] + [flip(mine, "row", 2 * k) for k in (1, 2, 3)]
    items = []
    for item in z_items:
        items += [item, flip(item, "row", 1)]

    merged = call(
        functools.partial(merge_kernel, ordered),
        jax.ShapeDtypeStruct((share, channels), BF16),
        [VMEM] * (SEGMENT + 1),
        VMEM,
        [],
        (*pieces, proj_weight.T),
        (1 << 28, 2 << 20),
        "merge",
    )
    merged_x = flip(merged, "col", 2)
    merged_core = flip(merged, "col", 1)
    merged_far = flip(merged_x, "col", 1)
    blocks = tokens // QBLOCK
    queries, values = call(
        query_kernel,
        (
            jax.ShapeDtypeStruct((blocks, heads, QBLOCK, channels), BF16),
            jax.ShapeDtypeStruct((width, channels), BF16),
        ),
        [VMEM, ANY, ANY, ANY, ANY],
        (VMEM, VMEM),
        [VMEM((out_width, channels), BF16), pltpu.SemaphoreType.DMA((4,))],
        (mine, merged, merged_core, merged_x, merged_far),
        (1 << 30, 6 << 20),
        "queries",
    )
    group = SEGMENT * tokens // PHASES
    attended = call(
        attend_kernel,
        jax.ShapeDtypeStruct((tokens, width), BF16),
        [pltpu.SMEM] + [VMEM] * (4 + SEGMENT),
        VMEM,
        [
            VMEM((channels // LANES, group + 256, LANES), F32),
            VMEM((group, channels), BF16),
            VMEM((blocks, heads, QBLOCK, channels), BF16),
        ],
        (counts, queries, values, pos, live, *items),
        (4 << 30, 8 << 20),
        "attend",
    )
    return attended.reshape(out_rows, out_cols, width)


def solution(mesh):
    in_specs = (
        P("row", "col", None),
        P("col", None),
        P(),
        P(),
        P("row", None),
        P("row", "col"),
        P("row", "col"),
    )
    out_specs = P("row", "col", None)
    return jax.shard_map(local, mesh=mesh, in_specs=in_specs, out_specs=out_specs, check_vma=False)
```

time: 371 us -> 102 us (0.27)
  the two profiles are of different devices: /device:TPU:0 before, /device:TPU:16 now
where the time goes in v1:
time: 102 us
  waiting for transfers between devices  28.4 us (28%)
  Pallas kernels  26.2 us (26%)
  starting transfers between devices  24.4 us (24%)
  blocking collectives  11.3 us (11%)
  local copies, waits for them, and re-layouts  8.79 us (9%)
  other arithmetic  1.7 us (2%)
    ppermute x17, waiting for transfers between devices, flip(): lax.ppermute(array, axis, [(i, i ^ bits) for i in range(lax.axis_size(axi...  28.4 us
    pallas_call x5, Pallas kernels, call(): pl.pallas_call(kernel, out_shape=out_shape, in_specs=[pl.BlockSpec(memory...  26.2 us
    ppermute x17, starting transfers between devices, flip(): lax.ppermute(array, axis, [(i, i ^ bits) for i in range(lax.axis_size(axi...  17.3 us
    unnamed x1, blocking collectives  11.3 us
    ppermute x2, starting transfers between devices, shifted(): lax.ppermute(array, axis, [(i, i + 1) for i in range(lax.axis_size(axis)...  5.83 us
    unnamed x21, local copies, waits for them, and re-layouts  4.23 us
  transfers between devices with their start and end apart: 20, of which 6 were waited for; matrix products, arithmetic and copies ran while one was open for 8% of the time, Pallas kernels for 7%

profile of v1, /device:TPU:16, one launch (start us, length us, event | category | flops | bytes accessed | tf_op | source)
XLA Modules:
  0.0 101.8 jit_solution(1053158346759936858)
XLA Ops:
  0.0 1.0 copy-done
  1.0 0.1 constant_dynamic-slice_fusion.refs_0_
  1.1 1.6 %collective-permute-start.6 = (bf16[96,576]{1,0:T(8,128)(2,1)S(1)}, bf16[96,576]{1,0:T(8,128)(2,1)S(1)}, u32[]{:S(2)}, u32[]{:S(2)}) collective-permute-start(bf16[96,576]{1,0:T(8,128)(2,1)S(1)} %constant_dynamic-slice_fusion.refs_0_), channel_id=1, source_target_pairs={{0,8},{4,12},{8,0},{12,4},{16,24},{20,28},{24,16},{28,20},{1,9},{5... | collective-permute-start | bytes 331784 | tf_op jit(solution)/shard_map/ppermute | solution.py:31
  2.8 0.3 collective-permute-start.7
  3.1 1.6 %collective-permute-start.8 = (bf16[96,576]{1,0:T(8,128)(2,1)S(1)}, bf16[96,576]{1,0:T(8,128)(2,1)S(1)}, u32[]{:S(2)}, u32[]{:S(2)}) collective-permute-start(bf16[96,576]{1,0:T(8,128)(2,1)S(1)} %constant_dynamic-slice_fusion.refs_0_), channel_id=1, source_target_pairs={{0,24},{4,28},{8,16},{12,20},{16,8},{20,12},{24,0},{28,4},{1,25},{... | collective-permute-start | bytes 331784 | tf_op jit(solution)/shard_map/ppermute | solution.py:31
  4.7 1.5 %collective-permute-start.1 = (bf16[576,256]{1,0:T(8,128)(2,1)}, bf16[576,256]{1,0:T(8,128)(2,1)S(1)}, u32[]{:S(2)}, u32[]{:S(2)}) collective-permute-start(bf16[576,256]{1,0:T(8,128)(2,1)} %w0.1), channel_id=1, source_target_pairs={{0,2},{1,3},{2,0},{3,1},{4,6},{5,7},{6,4},{7,5},{8,10},{9,11},{10,... | collective-permute-start | bytes 884744 | tf_op jit(solution)/shard_map/ppermute | solution.py:31
  6.2 0.8 slice_bitcast_fusion
  6.9 0.7 broadcast_multiply_fusion
  7.6 0.9 slice.21
  8.6 0.8 reshape.47.live_ref
  9.4 0.1 mul.22
  9.4 2.4 %collective-permute-start.3 = (bf16[32,256]{1,0:T(8,128)(2,1)S(1)}, bf16[32,256]{1,0:T(8,128)(2,1)S(1)}, u32[]{:S(2)}, u32[]{:S(2)}) collective-permute-start(bf16[32,256]{1,0:T(8,128)(2,1)S(1)} %bitcast.13), channel_id=1, source_target_pairs={{0,1},{1,2},{2,3},{4,5},{5,6},{6,7},{8,9},{9,10},{10,11},{12,13},{... | collective-permute-start | bytes 49160 | tf_op jit(solution)/shard_map/ppermute | solution.py:35
  11.9 0.2 collective-permute-done.7.refs_4_
  12.1 3.4 %collective-permute-start.4 = (bf16[64,256]{1,0:T(8,128)(2,1)S(1)}, bf16[64,256]{1,0:T(8,128)(2,1)S(1)}, u32[]{:S(2)}, u32[]{:S(2)}) collective-permute-start(bf16[64,256]{1,0:T(8,128)(2,1)S(1)} %slice_bitcast_fusion), channel_id=1, source_target_pairs={{0,4},{4,8},{8,12},{12,16},{16,20},{20,24},{24,28},{1,5},{5,9},{9,... | collective-permute-start | bytes 98312 | tf_op jit(solution)/shard_map/ppermute | solution.py:35
  15.5 0.8 pad_maximum_fusion
  16.3 3.3 %collective-permute-start.9 = (bf16[384,576]{1,0:T(8,128)(2,1)}, bf16[384,576]{1,0:T(8,128)(2,1)}, u32[]{:S(2)}, u32[]{:S(2)}) collective-permute-start(bf16[384,576]{1,0:T(8,128)(2,1)} %pad_maximum_fusion), channel_id=1, source_target_pairs={{0,4},{4,0},{8,12},{12,8},{16,20},{20,16},{24,28},{28,24},{1,5},{5... | collective-permute-start | bytes 1327112 | tf_op jit(solution)/shard_map/ppermute | solution.py:31
  19.7 0.1 collective-permute-start.2
  19.7 0.7 slice_bitcast_fusion.1
  20.4 1.2 %copy.13 = bf16[256,768]{0,1:T(8,128)(2,1)S(1)} copy(bf16[256,768]{1,0:T(8,128)(2,1)} %proj_ref.1) | data formatting | bytes 786432 | tf_op args[3]
  21.6 0.0 copy-start.1
  21.6 1.2 %copy-done.1 = bf16[32,64,256]{2,1,0:T(8,128)(2,1)S(1)} copy-done((bf16[32,64,256]{2,1,0:T(8,128)(2,1)S(1)}, bf16[32,64,256]{2,1,0:T(8,128)(2,1)}, u32[]{:S(2)}) %copy-start.1) | copy-done | bytes 1048600
  22.8 0.7 widen.1
  23.5 0.0 copy-start.5
  23.5 0.0 copy-start.7
  23.5 0.0 copy-start.6
  23.6 6.6 %collective-permute-done.9 = bf16[384,576]{1,0:T(8,128)(2,1)} collective-permute-done((bf16[384,576]{1,0:T(8,128)(2,1)}, bf16[384,576]{1,0:T(8,128)(2,1)}, u32[]{:S(2)}, u32[]{:S(2)}) %collective-permute-start.9) | collective-permute-done | bytes 442400 | tf_op jit(solution)/shard_map/ppermute | solution.py:31
  30.1 1.3 %collective-permute-start.5 = (bf16[1,256]{1,0:T(2,128)(2,1)S(1)}, bf16[1,256]{1,0:T(2,128)(2,1)S(1)}, u32[]{:S(2)}, u32[]{:S(2)}) collective-permute-start(bf16[1,256]{1,0:T(2,128)(2,1)S(1)} %slice_bitcast_fusion.1), channel_id=1, source_target_pairs={{0,5},{1,6},{2,7},{4,9},{5,10},{6,11},{8,13},{9,14},{10,15},{12,17... | collective-permute-start | bytes 1544 | tf_op jit(solution)/shard_map/ppermute | solution.py:43
  31.4 1.1 %fusion.1 = (bf16[96,576]{1,0:T(8,128)(2,1)S(1)}, bf16[96,576]{1,0:T(8,128)(2,1)S(1)}, bf16[96,576]{1,0:T(8,128)(2,1)S(1)}, bf16[96,576]{1,0:T(8,128)(2,1)S(1)}) fusion(bf16[384,576]{1,0:T(8,128)(2,1)} %collective-permute-done.9), kind=kLoop, calls=%fused_computation.11 | loop fusion | bytes 884736 | tf_op jit(solution)/shard_map/slice | solution.py:295
  32.6 1.5 %merge.1.m0 = bf16[576,256]{1,0:T(8,128)(2,1)S(1)} custom-call(bf16[96,576]{1,0:T(8,128)(2,1)S(1)} %constant_dynamic-slice_fusion.refs_0_, bf16[96,576]{1,0:T(8,128)(2,1)S(1)} %get-tuple-element.16.refs_1_, bf16[96,576]{1,0:T(8,128)(2,1)S(1)} %collective-permute-done.6.refs_2_, bf16[96,576]{1,0:T(8,128)(2,1)S(1)} %get-tuple-element.15.refs_3_, ...), custom_call_target="tpu_custom_call" | custom-call | flops 268435456 | bytes 2097152 | tf_op jit(solution)/shard_map/merge/pallas_call | solution.py:47
  34.1 3.1 %collective-permute-start.11 = (bf16[576,256]{1,0:T(8,128)(2,1)S(1)}, bf16[576,256]{1,0:T(8,128)(2,1)S(1)}, u32[]{:S(2)}, u32[]{:S(2)}) collective-permute-start(bf16[576,256]{1,0:T(8,128)(2,1)S(1)} %merge.1.m0), channel_id=1, source_target_pairs={{0,2},{1,3},{2,0},{3,1},{4,6},{5,7},{6,4},{7,5},{8,10},{9,11},{10,... | collective-permute-start | bytes 884744 | tf_op jit(solution)/shard_map/ppermute | solution.py:31
  37.3 2.6 %conv.1.f_ref.refs_0_ = bf16[512,256]{1,0:T(8,128)(2,1)S(1)} custom-call(bf16[2,16,32,768]{3,2,1,0:T(8,128)(2,1)S(1)} %get-tuple-element.9.z_ref, bf16[576,256]{1,0:T(8,128)(2,1)S(1)} %copy-done.3, bf16[576,256]{1,0:T(8,128)(2,1)S(1)} %collective-permute-done.w1, bf16[576,256]{1,0:T(8,128)(2,1)S(1)} %collective-permute-done.1.w2, ...), custom_call_target="tpu_custom_call" | custom-call | flops 1073741824 | bytes 6291456 | tf_op jit(solution)/shard_map/conv/pallas_call | solution.py:47
  39.9 1.9 %collective-permute-start.14 = (bf16[512,256]{1,0:T(8,128)(2,1)S(1)}, bf16[512,256]{1,0:T(8,128)(2,1)S(1)}, u32[]{:S(2)}, u32[]{:S(2)}) collective-permute-start(bf16[512,256]{1,0:T(8,128)(2,1)S(1)} %conv.1.f_ref.refs_0_), channel_id=1, source_target_pairs={{0,8},{4,12},{8,0},{12,4},{16,24},{20,28},{24,16},{28,20},{1,9},{5... | collective-permute-start | bytes 786440 | tf_op jit(solution)/shard_map/ppermute | solution.py:31
  41.8 1.7 %collective-permute-start.18 = (bf16[512,256]{1,0:T(8,128)(2,1)S(1)}, bf16[512,256]{1,0:T(8,128)(2,1)S(1)}, u32[]{:S(2)}, u32[]{:S(2)}) collective-permute-start(bf16[512,256]{1,0:T(8,128)(2,1)S(1)} %conv.1.f_ref.refs_0_), channel_id=1, source_target_pairs={{0,24},{4,28},{8,16},{12,20},{16,8},{20,12},{24,0},{28,4},{1,25},{... | collective-permute-start | bytes 786440 | tf_op jit(solution)/shard_map/ppermute | solution.py:31
  43.5 1.6 %collective-permute-done.11.m2 = bf16[576,256]{1,0:T(8,128)(2,1)S(1)} collective-permute-done((bf16[576,256]{1,0:T(8,128)(2,1)S(1)}, bf16[576,256]{1,0:T(8,128)(2,1)S(1)}, u32[]{:S(2)}, u32[]{:S(2)}) %collective-permute-start.11) | collective-permute-done | bytes 294944 | tf_op jit(solution)/shard_map/ppermute | solution.py:31
  45.0 0.2 collective-permute-start.13
  45.3 0.6 collective-permute-start.12
  45.9 5.7 %collective-permute-done.14.refs_2_ = bf16[512,256]{1,0:T(8,128)(2,1)S(1)} collective-permute-done((bf16[512,256]{1,0:T(8,128)(2,1)S(1)}, bf16[512,256]{1,0:T(8,128)(2,1)S(1)}, u32[]{:S(2)}, u32[]{:S(2)}) %collective-permute-start.14) | collective-permute-done | bytes 262176 | tf_op jit(solution)/shard_map/ppermute | solution.py:31
  51.6 7.9 %collective-permute-done.16.refs_4_ = bf16[512,256]{1,0:T(8,128)(2,1)S(1)} collective-permute-done((bf16[512,256]{1,0:T(8,128)(2,1)S(1)}, bf16[512,256]{1,0:T(8,128)(2,1)S(1)}, u32[]{:S(2)}, u32[]{:S(2)}) %collective-permute-start.16) | collective-permute-done | bytes 262176 | tf_op jit(solution)/shard_map/ppermute | solution.py:31
  59.5 0.9 collective-permute-start.17
  60.5 6.4 %collective-permute-done.18.refs_6_ = bf16[512,256]{1,0:T(8,128)(2,1)S(1)} collective-permute-done((bf16[512,256]{1,0:T(8,128)(2,1)S(1)}, bf16[512,256]{1,0:T(8,128)(2,1)S(1)}, u32[]{:S(2)}, u32[]{:S(2)}) %collective-permute-start.18) | collective-permute-done | bytes 262176 | tf_op jit(solution)/shard_map/ppermute | solution.py:31
  66.9 0.4 collective-permute-start.19
  67.3 0.6 dynamic-slice
  68.5 0.2 convert_reduce_fusion
  68.7 0.2 dynamic-update-slice
  68.9 11.3 %all-reduce = s32[32]{0:T(128)S(1)} all-reduce(s32[32]{0:T(128)S(1)} %dynamic-update-slice), channel_id=2, replica_groups={{0,4,8,12,16,20,24,28},{1,5,9,13,17,21,25,29},{2,6,10,14,18,22,26,30},{..., use_global_device_ids=true, to_apply=%add | all-reduce | flops 32 | bytes 256
  80.2 0.1 reshape.50.counts_ref
  80.3 2.0 %queries.1 = (bf16[16,12,32,256]{3,2,1,0:T(8,128)(2,1)S(1)}, bf16[768,256]{1,0:T(8,128)(2,1)S(1)}) custom-call(bf16[512,256]{1,0:T(8,128)(2,1)S(1)} %conv.1.f_ref.refs_0_, bf16[576,256]{1,0:T(8,128)(2,1)S(1)} %merge.1.m0, bf16[576,256]{1,0:T(8,128)(2,1)S(1)} %collective-permute-done.10.m1, bf16[576,256]{1,0:T(8,128)(2,1)S(1)} %collective-permute-done.11.m2, ...), custom_call_target="tpu_custom_call" | custom-call | flops 1073741824 | bytes 6291456 | tf_op jit(solution)/shard_map/queries/pallas_call | solution.py:47
  82.4 19.4 %attend.1 = bf16[512,768]{1,0:T(8,128)(2,1)} custom-call(s32[8,4]{1,0:T(8,128)S(1)} %reshape.50.counts_ref, bf16[16,12,32,256]{3,2,1,0:T(8,128)(2,1)S(1)} %get-tuple-element.11.q_ref, bf16[768,256]{1,0:T(8,128)(2,1)S(1)} %get-tuple-element.12.v_ref, s32[8,512]{1,0:T(8,128)S(1)} %get-tuple-element.10.pos_ref, s32[1,512]{1,0:T(1,128)S(1)} %reshape.47.live_ref, ...), custom_call_target="tpu_custom_call" | custom-call | flops 4294967296 | bytes 8388608 | tf_op jit(solution)/shard_map/attend/pallas_call | solution.py:47
  (32 shorter events, 0.1 us)
Async XLA Ops:
  0.0 1.0 copy-start
  0.0 37.3 %copy-start.3 = (bf16[576,256]{1,0:T(8,128)(2,1)S(1)}, bf16[576,256]{1,0:T(8,128)(2,1)}, u32[]{:S(2)}) copy-start(bf16[576,256]{1,0:T(8,128)(2,1)} %w0.1) | copy-start | bytes 884740
  0.0 37.3 %copy-start.2 = (bf16[256,768]{1,0:T(8,128)(2,1)S(1)}, bf16[256,768]{1,0:T(8,128)(2,1)}, u32[]{:S(2)}) copy-start(bf16[256,768]{1,0:T(8,128)(2,1)} %proj_ref.1) | copy-start | bytes 1179652
  0.0 37.3 %copy-start.4 = (f32[256]{0:T(256)S(1)}, f32[256]{0:T(256)}, u32[]{:S(2)}) copy-start(f32[256]{0:T(256)} %param.9) | copy-start | bytes 3076
  1.1 8.3 %collective-permute-start.6 = (bf16[96,576]{1,0:T(8,128)(2,1)S(1)}, bf16[96,576]{1,0:T(8,128)(2,1)S(1)}, u32[]{:S(2)}, u32[]{:S(2)}) collective-permute-start(bf16[96,576]{1,0:T(8,128)(2,1)S(1)} %constant_dynamic-slice_fusion.refs_0_), channel_id=1, source_target_pairs={{0,8},{4,12},{8,0},{12,4},{16,24},{20,28},{24,16},{28,20},{1,9},{5... | collective-permute-start | bytes 331784 | tf_op jit(solution)/shard_map/ppermute | solution.py:31
  2.8 9.3 %collective-permute-start.7 = (bf16[96,576]{1,0:T(8,128)(2,1)S(1)}, bf16[96,576]{1,0:T(8,128)(2,1)S(1)}, u32[]{:S(2)}, u32[]{:S(2)}) collective-permute-start(bf16[96,576]{1,0:T(8,128)(2,1)S(1)} %constant_dynamic-slice_fusion.refs_0_), channel_id=1, source_target_pairs={{0,16},{4,20},{8,24},{12,28},{16,0},{20,4},{24,8},{28,12},{1,17},{... | collective-permute-start | bytes 331784 | tf_op jit(solution)/shard_map/ppermute | solution.py:31
  3.1 12.4 %collective-permute-start.8 = (bf16[96,576]{1,0:T(8,128)(2,1)S(1)}, bf16[96,576]{1,0:T(8,128)(2,1)S(1)}, u32[]{:S(2)}, u32[]{:S(2)}) collective-permute-start(bf16[96,576]{1,0:T(8,128)(2,1)S(1)} %constant_dynamic-slice_fusion.refs_0_), channel_id=1, source_target_pairs={{0,24},{4,28},{8,16},{12,20},{16,8},{20,12},{24,0},{28,4},{1,25},{... | collective-permute-start | bytes 331784 | tf_op jit(solution)/shard_map/ppermute | solution.py:31
  4.7 15.0 %collective-permute-start.1 = (bf16[576,256]{1,0:T(8,128)(2,1)}, bf16[576,256]{1,0:T(8,128)(2,1)S(1)}, u32[]{:S(2)}, u32[]{:S(2)}) collective-permute-start(bf16[576,256]{1,0:T(8,128)(2,1)} %w0.1), channel_id=1, source_target_pairs={{0,2},{1,3},{2,0},{3,1},{4,6},{5,7},{6,4},{7,5},{8,10},{9,11},{10,... | collective-permute-start | bytes 884744 | tf_op jit(solution)/shard_map/ppermute | solution.py:31
  6.2 31.1 %collective-permute-start = (bf16[576,256]{1,0:T(8,128)(2,1)}, bf16[576,256]{1,0:T(8,128)(2,1)S(1)}, u32[]{:S(2)}, u32[]{:S(2)}) collective-permute-start(bf16[576,256]{1,0:T(8,128)(2,1)} %w0.1), channel_id=1, source_target_pairs={{0,1},{1,0},{2,3},{3,2},{4,5},{5,4},{6,7},{7,6},{8,9},{9,8},{10,11... | collective-permute-start | bytes 884744 | tf_op jit(solution)/shard_map/ppermute | solution.py:31
  9.4 27.8 %collective-permute-start.3 = (bf16[32,256]{1,0:T(8,128)(2,1)S(1)}, bf16[32,256]{1,0:T(8,128)(2,1)S(1)}, u32[]{:S(2)}, u32[]{:S(2)}) collective-permute-start(bf16[32,256]{1,0:T(8,128)(2,1)S(1)} %bitcast.13), channel_id=1, source_target_pairs={{0,1},{1,2},{2,3},{4,5},{5,6},{6,7},{8,9},{9,10},{10,11},{12,13},{... | collective-permute-start | bytes 49160 | tf_op jit(solution)/shard_map/ppermute | solution.py:35
  12.1 25.2 %collective-permute-start.4 = (bf16[64,256]{1,0:T(8,128)(2,1)S(1)}, bf16[64,256]{1,0:T(8,128)(2,1)S(1)}, u32[]{:S(2)}, u32[]{:S(2)}) collective-permute-start(bf16[64,256]{1,0:T(8,128)(2,1)S(1)} %slice_bitcast_fusion), channel_id=1, source_target_pairs={{0,4},{4,8},{8,12},{12,16},{16,20},{20,24},{24,28},{1,5},{5,9},{9,... | collective-permute-start | bytes 98312 | tf_op jit(solution)/shard_map/ppermute | solution.py:35
  16.3 13.8 %collective-permute-start.9 = (bf16[384,576]{1,0:T(8,128)(2,1)}, bf16[384,576]{1,0:T(8,128)(2,1)}, u32[]{:S(2)}, u32[]{:S(2)}) collective-permute-start(bf16[384,576]{1,0:T(8,128)(2,1)} %pad_maximum_fusion), channel_id=1, source_target_pairs={{0,4},{4,0},{8,12},{12,8},{16,20},{20,16},{24,28},{28,24},{1,5},{5... | collective-permute-start | bytes 1327112 | tf_op jit(solution)/shard_map/ppermute | solution.py:31
  19.7 17.6 %collective-permute-start.2 = (bf16[576,256]{1,0:T(8,128)(2,1)S(1)}, bf16[576,256]{1,0:T(8,128)(2,1)S(1)}, u32[]{:S(2)}, u32[]{:S(2)}) collective-permute-start(bf16[576,256]{1,0:T(8,128)(2,1)S(1)} %collective-permute-done.1.w2), channel_id=1, source_target_pairs={{0,1},{1,0},{2,3},{3,2},{4,5},{5,4},{6,7},{7,6},{8,9},{9,8},{10,11... | collective-permute-start | bytes 884744 | tf_op jit(solution)/shard_map/ppermute | solution.py:31
  21.6 1.2 %copy-start.1 = (bf16[32,64,256]{2,1,0:T(8,128)(2,1)S(1)}, bf16[32,64,256]{2,1,0:T(8,128)(2,1)}, u32[]{:S(2)}) copy-start(bf16[32,64,256]{2,1,0:T(8,128)(2,1)} %x_ref.1) | copy-start | bytes 3145732
  23.5 43.7 %copy-start.5 = (s32[16,32]{1,0:T(8,128)S(1)}, s32[16,32]{1,0:T(8,128)}, u32[]{:S(2)}) copy-start(s32[16,32]{1,0:T(8,128)} %param.12) | copy-start | bytes 6148
  23.5 43.7 %copy-start.7 = (u32[32]{0:T(128)S(1)}, u32[32]{0:T(128)}, u32[]{:S(2)}) copy-start(u32[32]{0:T(128)} %constant.17) | copy-start | bytes 388
  23.5 45.0 %copy-start.6 = (s32[16,32]{1,0:T(8,128)S(1)}, s32[16,32]{1,0:T(8,128)}, u32[]{:S(2)}) copy-start(s32[16,32]{1,0:T(8,128)} %param.13) | copy-start | bytes 6148
  30.1 3.9 %collective-permute-start.5 = (bf16[1,256]{1,0:T(2,128)(2,1)S(1)}, bf16[1,256]{1,0:T(2,128)(2,1)S(1)}, u32[]{:S(2)}, u32[]{:S(2)}) collective-permute-start(bf16[1,256]{1,0:T(2,128)(2,1)S(1)} %slice_bitcast_fusion.1), channel_id=1, source_target_pairs={{0,5},{1,6},{2,7},{4,9},{5,10},{6,11},{8,13},{9,14},{10,15},{12,17... | collective-permute-start | bytes 1544 | tf_op jit(solution)/shard_map/ppermute | solution.py:43
  34.1 11.0 %collective-permute-start.11 = (bf16[576,256]{1,0:T(8,128)(2,1)S(1)}, bf16[576,256]{1,0:T(8,128)(2,1)S(1)}, u32[]{:S(2)}, u32[]{:S(2)}) collective-permute-start(bf16[576,256]{1,0:T(8,128)(2,1)S(1)} %merge.1.m0), channel_id=1, source_target_pairs={{0,2},{1,3},{2,0},{3,1},{4,6},{5,7},{6,4},{7,5},{8,10},{9,11},{10,... | collective-permute-start | bytes 884744 | tf_op jit(solution)/shard_map/ppermute | solution.py:31
  37.2 8.1 %collective-permute-start.10 = (bf16[576,256]{1,0:T(8,128)(2,1)S(1)}, bf16[576,256]{1,0:T(8,128)(2,1)S(1)}, u32[]{:S(2)}, u32[]{:S(2)}) collective-permute-start(bf16[576,256]{1,0:T(8,128)(2,1)S(1)} %merge.1.m0), channel_id=1, source_target_pairs={{0,1},{1,0},{2,3},{3,2},{4,5},{5,4},{6,7},{7,6},{8,9},{9,8},{10,11... | collective-permute-start | bytes 884744 | tf_op jit(solution)/shard_map/ppermute | solution.py:31
  39.9 11.7 %collective-permute-start.14 = (bf16[512,256]{1,0:T(8,128)(2,1)S(1)}, bf16[512,256]{1,0:T(8,128)(2,1)S(1)}, u32[]{:S(2)}, u32[]{:S(2)}) collective-permute-start(bf16[512,256]{1,0:T(8,128)(2,1)S(1)} %conv.1.f_ref.refs_0_), channel_id=1, source_target_pairs={{0,8},{4,12},{8,0},{12,4},{16,24},{20,28},{24,16},{28,20},{1,9},{5... | collective-permute-start | bytes 786440 | tf_op jit(solution)/shard_map/ppermute | solution.py:31
  41.8 17.8 %collective-permute-start.16 = (bf16[512,256]{1,0:T(8,128)(2,1)S(1)}, bf16[512,256]{1,0:T(8,128)(2,1)S(1)}, u32[]{:S(2)}, u32[]{:S(2)}) collective-permute-start(bf16[512,256]{1,0:T(8,128)(2,1)S(1)} %conv.1.f_ref.refs_0_), channel_id=1, source_target_pairs={{0,16},{4,20},{8,24},{12,28},{16,0},{20,4},{24,8},{28,12},{1,17},{... | collective-permute-start | bytes 786440 | tf_op jit(solution)/shard_map/ppermute | solution.py:31
  41.8 25.1 %collective-permute-start.18 = (bf16[512,256]{1,0:T(8,128)(2,1)S(1)}, bf16[512,256]{1,0:T(8,128)(2,1)S(1)}, u32[]{:S(2)}, u32[]{:S(2)}) collective-permute-start(bf16[512,256]{1,0:T(8,128)(2,1)S(1)} %conv.1.f_ref.refs_0_), channel_id=1, source_target_pairs={{0,24},{4,28},{8,16},{12,20},{16,8},{20,12},{24,0},{28,4},{1,25},{... | collective-permute-start | bytes 786440 | tf_op jit(solution)/shard_map/ppermute | solution.py:31
  45.0 37.3 %collective-permute-start.13 = (bf16[512,256]{1,0:T(8,128)(2,1)S(1)}, bf16[512,256]{1,0:T(8,128)(2,1)S(1)}, u32[]{:S(2)}, u32[]{:S(2)}) collective-permute-start(bf16[512,256]{1,0:T(8,128)(2,1)S(1)} %conv.1.f_ref.refs_0_), channel_id=1, source_target_pairs={{0,4},{4,0},{8,12},{12,8},{16,20},{20,16},{24,28},{28,24},{1,5},{5... | collective-permute-start | bytes 786440 | tf_op jit(solution)/shard_map/ppermute | solution.py:31
  45.3 35.0 %collective-permute-start.12 = (bf16[576,256]{1,0:T(8,128)(2,1)S(1)}, bf16[576,256]{1,0:T(8,128)(2,1)S(1)}, u32[]{:S(2)}, u32[]{:S(2)}) collective-permute-start(bf16[576,256]{1,0:T(8,128)(2,1)S(1)} %collective-permute-done.11.m2), channel_id=1, source_target_pairs={{0,1},{1,0},{2,3},{3,2},{4,5},{5,4},{6,7},{7,6},{8,9},{9,8},{10,11... | collective-permute-start | bytes 884744 | tf_op jit(solution)/shard_map/ppermute | solution.py:31
  51.6 30.7 %collective-permute-start.15 = (bf16[512,256]{1,0:T(8,128)(2,1)S(1)}, bf16[512,256]{1,0:T(8,128)(2,1)S(1)}, u32[]{:S(2)}, u32[]{:S(2)}) collective-permute-start(bf16[512,256]{1,0:T(8,128)(2,1)S(1)} %collective-permute-done.14.refs_2_), channel_id=1, source_target_pairs={{0,4},{4,0},{8,12},{12,8},{16,20},{20,16},{24,28},{28,24},{1,5},{5... | collective-permute-start | bytes 786440 | tf_op jit(solution)/shard_map/ppermute | solution.py:31
  59.5 22.8 %collective-permute-start.17 = (bf16[512,256]{1,0:T(8,128)(2,1)S(1)}, bf16[512,256]{1,0:T(8,128)(2,1)}, u32[]{:S(2)}, u32[]{:S(2)}) collective-permute-start(bf16[512,256]{1,0:T(8,128)(2,1)S(1)} %collective-permute-done.16.refs_4_), channel_id=1, source_target_pairs={{0,4},{4,0},{8,12},{12,8},{16,20},{20,16},{24,28},{28,24},{1,5},{5... | collective-permute-start | bytes 786440 | tf_op jit(solution)/shard_map/ppermute | solution.py:31
  66.9 15.5 %collective-permute-start.19 = (bf16[512,256]{1,0:T(8,128)(2,1)S(1)}, bf16[512,256]{1,0:T(8,128)(2,1)}, u32[]{:S(2)}, u32[]{:S(2)}) collective-permute-start(bf16[512,256]{1,0:T(8,128)(2,1)S(1)} %collective-permute-done.18.refs_6_), channel_id=1, source_target_pairs={{0,4},{4,0},{8,12},{12,8},{16,20},{20,16},{24,28},{28,24},{1,5},{5... | collective-permute-start | bytes 786440 | tf_op jit(solution)/shard_map/ppermute | solution.py:31

commit v2 on v1

v2 whole, which is shorter than its diff:
```python
import functools
import math

import jax
import jax.numpy as jnp
from jax import lax
from jax.experimental import pallas as pl
from jax.experimental.pallas import tpu as pltpu
from jax.sharding import PartitionSpec as P

HD = 64
PHASES = 4
SEGMENT = 8
LANES = 128
BF16 = jnp.bfloat16
F32 = jnp.float32
NT = (((1,), (1,)), ((), ()))
TN = (((0,), (0,)), ((), ()))
VMEM = pltpu.VMEM
ANY = pl.ANY


def dot(a, b, dims=None):
    if dims is None:
        return jnp.dot(a, b, preferred_element_type=F32)
    return lax.dot_general(a, b, dims, preferred_element_type=F32)


def flip(array, axis, bits):
    return lax.ppermute(array, axis, [(i, i ^ bits) for i in range(lax.axis_size(axis))])


def shifted(array, axis):
    return lax.ppermute(array, axis, [(i, i + 1) for i in range(lax.axis_size(axis) - 1)])


HOPS = (1, 3, 0, 2)


def ring(array):
    pairs = []
    for i in range(lax.axis_size("row")):
        z, y = i % SEGMENT // 2, i % 2
        pairs.append((i, i // SEGMENT * SEGMENT + 2 * HOPS[z] + y))
    return lax.ppermute(array, "row", pairs)


def behind(z):
    found = [z]
    for _ in range(len(HOPS) - 1):
        z = found[-1]
        found.append(jnp.where(z == 0, 2, jnp.where(z == 1, 0, jnp.where(z == 2, 3, 1))))
    return found


def call(kernel, out_shape, in_spaces, out_spaces, scratch, args, name):
    return pl.pallas_call(
        kernel,
        out_shape=out_shape,
        in_specs=[pl.BlockSpec(memory_space=s) for s in in_spaces],
        out_specs=(
            tuple(pl.BlockSpec(memory_space=s) for s in out_spaces)
            if isinstance(out_spaces, tuple)
            else pl.BlockSpec(memory_space=out_spaces)
        ),
        scratch_shapes=scratch,
        compiler_params=pltpu.CompilerParams(vmem_limit_bytes=40 * 1024 * 1024),
        cost_estimate=pl.CostEstimate(flops=0, bytes_accessed=0, transcendentals=0),
        name=name,
    )(*args)


def prepare_kernel(
    x_ref, tissue_ref, phase_ref, left_ref, z_ref, sort_ref, back_ref, wide
):
    rows, cols, channels = x_ref.shape
    out_rows, out_cols = tissue_ref.shape
    half = cols // 2
    tokens = out_rows * out_cols
    bucket = tokens // PHASES
    left_ref[...] = x_ref[:, cols - 1, :]
    def one_row(r, carry):
        for c in range(channels // LANES):
            wide[r, c, pl.ds(0, 8), :] = jnp.zeros((8, LANES), F32)
            wide[r, c, pl.ds(8, cols), :] = x_ref[r, :, c * LANES : (c + 1) * LANES].astype(F32)
            for b in range(3):
                spot = b * channels + c * LANES
                z_ref[r % 2, r // 2, :, spot : spot + LANES] = wide[
                    r, c, pl.ds(7 + b, half, stride=2), :
                ].astype(BF16)
        return carry

    lax.fori_loop(0, rows, one_row, 0, unroll=2)

    def iota(shape, axis):
        return lax.broadcasted_iota(jnp.int32, shape, axis)

    labels = (phase_ref[...] * 2 + 1 - tissue_ref[...]).astype(F32).astype(BF16)
    spread = (iota((out_cols, tokens), 0) == lax.rem(iota((out_cols, tokens), 1), out_cols)).astype(F32)
    along = dot(labels, spread.astype(BF16))
    in_row = iota((out_rows, tokens), 0) == iota((out_rows, tokens), 1) // out_cols
    cls = jnp.sum(jnp.where(in_row, along, 0.0), axis=0, keepdims=True).astype(jnp.int32)
    classes = iota((16, tokens), 0)
    cls = jnp.broadcast_to(cls, (16, tokens))
    member = (classes == cls).astype(F32)
    earlier = (iota((tokens, tokens), 0) < iota((tokens, tokens), 1)).astype(F32)
    rank = dot(member.astype(BF16), earlier.astype(BF16))
    odd = lax.rem(classes, 2) == 1
    live_before = jnp.where(odd & (classes - 1 == cls), 1.0, 0.0)
    start = (classes // 2 * bucket).astype(F32) + jnp.sum(live_before, axis=1, keepdims=True)
    place = jnp.sum(member * (rank + start), axis=0, keepdims=True)
    place = jnp.broadcast_to(place, (LANES, tokens))
    sort_ref[...] = (
        iota((tokens, tokens), 0) == jnp.broadcast_to(place[0:1].astype(jnp.int32), (tokens, tokens))
    ).astype(F32).astype(BF16)
    column = place.T[:, 0:1].astype(jnp.int32)
    back_ref[...] = (iota((tokens, tokens), 1) == column).astype(F32).astype(BF16)


def conv_kernel(
    z_hbm, w0, w1, w2, w3, proj_hbm, sort_hbm, left_ref, up_ref, bias_ref,
    out_ref, z_ref, weight, proj_ref, sort_ref, edge, sems,
):
    out_rows, out_cols, wide = z_ref.shape[1:]
    channels = wide // 3
    tokens = out_rows * out_cols
    shard = w0.shape[0]
    mine = lax.axis_index("col")
    copies = [pltpu.make_async_copy(z_hbm, z_ref, sems.at[4])]
    for j, ref in enumerate((w0, w1, w2, w3)):
        spot = pl.multiple_of((mine ^ j) * shard, 64)
        copies.append(pltpu.make_async_copy(ref, weight.at[pl.ds(spot, shard)], sems.at[j]))
    later = [
        pltpu.make_async_copy(proj_hbm, proj_ref, sems.at[5]),
        pltpu.make_async_copy(sort_hbm, sort_ref, sems.at[6]),
    ]
    for copy in copies + later:
        copy.start()
    in_rows = left_ref.shape[0]
    corner = up_ref[0:16].astype(F32)
    halves = range(channels // LANES)
    for c in halves:
        few = slice(c * LANES, (c + 1) * LANES)
        edge[0, c, pl.ds(0, 8), :] = corner[8:16, few]
        edge[0, c, pl.ds(8, in_rows), :] = left_ref[:, few].astype(F32)
        edge[1, c, pl.ds(0, 8), :] = jnp.zeros((8, LANES), F32)
        edge[1, c, pl.ds(8, 2 * out_cols), :] = up_ref[16:, few].astype(F32)

    def every_second(side, first, count):
        parts = [edge[side, c, pl.ds(first, count, stride=2), :] for c in halves]
        return jnp.concatenate(parts, axis=1).astype(BF16)

    lefts = [every_second(0, 7 + a, out_rows) for a in range(3)]
    ups = [every_second(1, 7 + b, out_cols) for b in range(3)]
    for copy in copies:
        copy.wait()
    even = z_ref[0].reshape(tokens, wide)
    odd = z_ref[1].reshape(tokens, wide)
    acc = dot(even, weight[wide : 2 * wide]) + dot(odd, weight[2 * wide : 3 * wide])
    above = dot(odd[: tokens - out_cols], weight[:wide])
    top = dot(jnp.concatenate(ups, axis=1), weight[:wide])
    acc = acc + jnp.concatenate([top, above], axis=0)
    side = sum(dot(lefts[a], weight[a * wide : a * wide + channels]) for a in range(3))
    grid = acc.reshape(out_rows, out_cols, channels)
    first = lax.broadcasted_iota(jnp.int32, grid.shape, 1) == 0
    grid = grid + jnp.where(first, side[:, None, :], 0.0)
    pre = grid.reshape(tokens, channels) + bias_ref[...]
    features = jax.nn.gelu(pre).astype(BF16)
    for copy in later:
        copy.wait()
    projected = dot(features, proj_ref[...])
    centred = projected - jnp.mean(projected, axis=1, keepdims=True)
    spread = jnp.mean(centred * centred, axis=1, keepdims=True)
    scaled = (features.astype(F32) * lax.rsqrt(spread + 1e-05)).astype(BF16)
    out_ref[...] = dot(sort_ref[...], scaled).astype(BF16)


def merge_kernel(ordered, *refs):
    pieces, (proj_ref, out_ref, counts_ref) = refs[:-3], refs[-3:]
    share = out_ref.shape[0]
    depth, lanes = pieces[0].shape
    mine = lax.rem(lax.axis_index("row"), SEGMENT)
    if ordered:
        order = range(SEGMENT)
    else:
        order = [2 * z + lax.rem(mine, 2) for z in behind(mine // 2)]
    mean = jnp.mean(proj_ref[...].astype(F32), axis=0, keepdims=True)
    total = None
    for piece, j in zip(pieces, order):
        spot = pl.multiple_of(j * depth, 32)
        part = proj_ref[pl.ds(spot, depth), :].astype(F32) - mean
        high = part.astype(BF16)
        low = (part - high.astype(F32)).astype(BF16)
        term = dot(piece[...], high, TN) + dot(piece[...], low, TN)
        total = term if total is None else total + term
    out_ref[...] = total[:share].astype(out_ref.dtype)
    rows = [piece[0:16, lanes - LANES :].astype(F32)[0:1] for piece in pieces]
    rows += [jnp.zeros((16 - len(rows), LANES), F32)]
    counts_ref[...] = jnp.concatenate(rows, axis=0).astype(BF16)


def join_kernel(mine_ref, got_ref, my_counts, got_counts, out_ref, counts_ref):
    out_ref[...] = (mine_ref[...] + got_ref[...].astype(F32)).astype(BF16)
    a, b = my_counts[...].astype(F32), got_counts[...].astype(F32)
    rows = [side[k : k + 1] for k in range(SEGMENT // 2) for side in (a, b)]
    counts_ref[...] = jnp.concatenate(rows, axis=0).astype(jnp.int32)


def query_kernel(f_ref, m0, m1, m2, m3, q_ref, v_ref, merged, sems):
    shard = m0.shape[0]
    width = 4 * shard // 3
    heads = width // HD
    blocks, _, bucket, _ = q_ref.shape
    mine = lax.axis_index("col")
    copies = []
    for j, ref in enumerate((m0, m1, m2, m3)):
        spot = pl.multiple_of((mine ^ j) * shard, 64)
        copies.append(pltpu.make_async_copy(ref, merged.at[pl.ds(spot, shard)], sems.at[j]))
        copies[-1].start()
    for copy in copies:
        copy.wait()
    f = f_ref[...]
    factor = math.log2(math.e) / math.sqrt(HD)
    lanes = lax.broadcasted_iota(jnp.int32, (1, 2 * HD), 1)
    for pair in range(heads // 2):
        both = slice(pair * 2 * HD, (pair + 1) * 2 * HD)
        queries = dot(f, merged[both], NT).astype(BF16).astype(F32)
        keys = merged[width + pair * 2 * HD : width + (pair + 1) * 2 * HD]
        for h in range(2):
            one = jnp.where(lanes // HD == h, queries, 0.0).astype(BF16)
            wide = (dot(one, keys) * factor).astype(BF16)
            q_ref[:, 2 * pair + h] = wide.reshape(blocks, bucket, wide.shape[1])
    v_ref[...] = merged[2 * width :].astype(F32).T.astype(BF16)


def attend_kernel(spare, counts_ref, q_hbm, v_hbm, back_hbm, *refs):
    items = refs[:SEGMENT]
    out_ref, rows32, keys, keys_t, mixed, q_ref, v_ref, back_ref, sems = refs[SEGMENT:]
    phases, heads, bucket, channels = q_ref.shape
    tokens = phases * bucket
    group = SEGMENT * bucket
    halves = range(channels // LANES)
    parts = 6
    share = heads // parts
    copies = [
        pltpu.make_async_copy(a, b, sems.at[i])
        for i, (a, b) in enumerate(((q_hbm, q_ref), (v_hbm, v_ref), (back_hbm, back_ref)))
    ]
    for copy in copies:
        copy.start()
    fills = []
    for p in range(phases):
        filled = 0
        for j in range(SEGMENT):
            for c in halves:
                rows32[p, c, pl.ds(filled, bucket), :] = items[j][
                    p * bucket : (p + 1) * bucket, c * LANES : (c + 1) * LANES
                ].astype(F32)
            filled = filled + counts_ref[j, spare + p]
        for c in halves:
            rows32[p, c, pl.ds(filled, group // 2), :] = jnp.zeros((group // 2, LANES), F32)
        fills.append(filled)
    most = functools.reduce(jnp.maximum, fills)
    for copy in copies:
        copy.wait()
    for width in (group // 2, group):

        @pl.when((most > width - group // 2) & (most <= width))
        def _():
            for p in range(phases):
                if width == group:

                    @pl.when(fills[p] < group // 2)
                    def _(p=p):
                        for c in halves:
                            rows32[p, c, group // 2 : group, :] = jnp.zeros((group // 2, LANES), F32)

                for c in halves:
                    some = rows32[p, c, 0:width, :]
                    keys[p, 0:width, c * LANES : (c + 1) * LANES] = some.astype(BF16)
                    keys_t[p, c * LANES : (c + 1) * LANES, 0:width] = some.T.astype(BF16)
                bias = jnp.where(
                    lax.broadcasted_iota(jnp.int32, (1, width), 1) < fills[p], 0.0, -1e30
                )
                for part in range(parts):
                    few = slice(part * share, (part + 1) * share)
                    q = q_ref[p, few].reshape(share * bucket, channels)
                    scores = dot(q, keys_t[p, :, 0:width]) + bias
                    weights = jnp.exp2(scores - jnp.max(scores, axis=1, keepdims=True))
                    total = jnp.sum(weights, axis=1, keepdims=True)
                    mix = dot(weights.astype(BF16), keys[p, 0:width, :]) * (1.0 / total)
                    mixed[p, few] = mix.astype(BF16).reshape(share, bucket, channels)

    outs = []
    lane = lax.broadcasted_iota(jnp.int32, (1, LANES), 1)
    for pair in range(heads // 2):
        some = v_ref[:, pair * LANES : (pair + 1) * LANES]
        a = dot(mixed[:, 2 * pair].reshape(tokens, channels), some)
        b = dot(mixed[:, 2 * pair + 1].reshape(tokens, channels), some)
        outs.append(jnp.where(lane < HD, a, b))
    spot = lax.broadcasted_iota(jnp.int32, (bucket, 1), 0)
    live = jnp.concatenate([spot < counts_ref[0, spare + p] for p in range(phases)], axis=0)
    ordered = jnp.where(live, jnp.concatenate(outs, axis=1), 0.0).astype(BF16)
    out_ref[...] = dot(back_ref[...], ordered).astype(BF16)


def local(feat_in, conv_weight, conv_bias, proj_weight, qkv_weight, tissue, phase):
    in_rows, in_cols, channels = feat_in.shape
    out_rows, out_cols = in_rows // 2, in_cols // 2
    tokens = out_rows * out_cols
    row_count, col_count = lax.axis_size("row"), lax.axis_size("col")
    depth, out_width = qkv_weight.shape
    width = out_width // 3
    heads = width // HD
    share = out_width // col_count

    weight_x = flip(conv_weight, "col", 2)
    weight_core = flip(conv_weight, "col", 1)
    weight_far = flip(weight_x, "col", 1)
    left, z, sort, back = call(
        prepare_kernel,
        (
            jax.ShapeDtypeStruct((in_rows, channels), BF16),
            jax.ShapeDtypeStruct((2, out_rows, out_cols, 3 * channels), BF16),
            jax.ShapeDtypeStruct((tokens, tokens), BF16),
            jax.ShapeDtypeStruct((tokens, tokens), BF16),
        ),
        [VMEM] * 3,
        (VMEM,) * 4,
        [VMEM((in_rows, channels // LANES, in_cols + 8, LANES), F32)],
        (feat_in, tissue, phase),
        "prepare",
    )
    left = shifted(left, "col")
    up = shifted(jnp.concatenate([left[in_rows - 16 :], feat_in[in_rows - 1]], axis=0), "row")

    here = (phase[None] == jnp.arange(PHASES, dtype=jnp.int32)[:, None, None]) & (tissue[None] > 0)
    own_counts = jnp.sum(here.astype(F32), axis=(1, 2)).astype(BF16)
    qkv_mine = lax.dynamic_slice(
        qkv_weight, (0, lax.axis_index("col") * share), (depth, share)
    )
    lanes = -share % LANES
    if lanes < PHASES:
        lanes += LANES
    beside = jnp.broadcast_to(jnp.pad(own_counts, (0, lanes - PHASES))[None], (depth, lanes))
    qkv_mine = jnp.concatenate([qkv_mine, beside], axis=1)
    spare = share % LANES
    ordered = row_count != SEGMENT
    if ordered:
        whole = lax.all_gather(qkv_mine, "row", axis=0, tiled=True)
        pieces = list(whole.reshape(SEGMENT, width // SEGMENT, share + lanes))
        groups = [
            [s * SEGMENT + i for i in range(SEGMENT)] for s in range(row_count // SEGMENT)
        ]
        spot = lax.rem(lax.axis_index("row"), SEGMENT)
        y = lax.rem(spot, 2)
        order = jnp.stack([2 * z_from + side for z_from in behind(spot // 2) for side in (y, 1 - y)])
        counts = lax.all_gather(own_counts, "row", axis_index_groups=groups)[order]
        counts = jnp.pad(counts.astype(jnp.int32), ((0, 0), (spare, LANES - spare - PHASES)))
    else:
        pieces = [qkv_mine]
        for _ in range(3):
            pieces.append(ring(pieces[-1]))
        z, *pieces = lax.optimization_barrier((z, *pieces))

    mine = call(
        conv_kernel,
        jax.ShapeDtypeStruct((tokens, channels), BF16),
        [ANY] * 7 + [VMEM] * 3,
        VMEM,
        [
            VMEM(z.shape, BF16),
            VMEM((9 * channels, channels), BF16),
            VMEM(proj_weight.shape, BF16),
            VMEM((tokens, tokens), BF16),
            VMEM((2, channels // LANES, in_cols + 8, LANES), F32),
            pltpu.SemaphoreType.DMA((7,)),
        ],
        (
            z, conv_weight, weight_core, weight_x, weight_far, proj_weight, sort, left, up,
            conv_bias.reshape(1, channels),
        ),
        "conv",
    )

    items = []
    item = mine
    for step in range(4):
        if step < 3:
            later, beside = ring(item), flip(item, "row", 1)
            later, beside = lax.optimization_barrier((later, beside))
        else:
            later, beside = None, flip(item, "row", 1)
        items += [item, beside]
        item = later

    merged, counts_mine = call(
        functools.partial(merge_kernel, ordered),
        (
            jax.ShapeDtypeStruct((share, channels), BF16 if ordered else F32),
            jax.ShapeDtypeStruct((16, LANES), BF16),
        ),
        [VMEM] * (len(pieces) + 1),
        (VMEM, VMEM),
        [],
        (*pieces, proj_weight.T),
        "merge",
    )
    if not ordered:
        got = flip(jnp.concatenate([merged.astype(BF16), jnp.pad(counts_mine, ((0, 0), (0, channels - LANES)))], axis=0), "row", 1)
        merged, counts = call(
            join_kernel,
            (
                jax.ShapeDtypeStruct((share, channels), BF16),
                jax.ShapeDtypeStruct((SEGMENT, LANES), jnp.int32),
            ),
            [VMEM] * 4,
            (VMEM, VMEM),
            [],
            (merged, got[:share], counts_mine, got[share:, :LANES]),
            "join",
        )
    merged_x = flip(merged, "col", 2)
    merged_core = flip(merged, "col", 1)
    merged_far = flip(merged_x, "col", 1)
    bucket = tokens // PHASES
    queries, values = call(
        query_kernel,
        (
            jax.ShapeDtypeStruct((PHASES, heads, bucket, channels), BF16),
            jax.ShapeDtypeStruct((channels, width), BF16),
        ),
        [VMEM, ANY, ANY, ANY, ANY],
        (VMEM, VMEM),
        [VMEM((out_width, channels), BF16), pltpu.SemaphoreType.DMA((4,))],
        (mine, merged, merged_core, merged_x, merged_far),
        "queries",
    )
    group = SEGMENT * bucket
    attended = call(
        functools.partial(attend_kernel, spare),
        jax.ShapeDtypeStruct((tokens, width), BF16),
        [pltpu.SMEM, ANY, ANY, ANY] + [VMEM] * SEGMENT,
        VMEM,
        [
            VMEM((PHASES, channels // LANES, group + group // 2, LANES), F32),
            VMEM((PHASES, group, channels), BF16),
            VMEM((PHASES, channels, group), BF16),
            VMEM(queries.shape, BF16),
            VMEM(queries.shape, BF16),
            VMEM(values.shape, BF16),
            VMEM((tokens, tokens), BF16),
            pltpu.SemaphoreType.DMA((3,)),
        ],
        (counts, queries, values, back, *items),
        "attend",
    )
    return attended.reshape(out_rows, out_cols, width)


def solution(mesh):
    in_specs = (
        P("row", "col", None),
        P("col", None),
        P(),
        P(),
        P("row", None),
        P("row", "col"),
        P("row", "col"),
    )
    out_specs = P("row", "col", None)
    return jax.shard_map(local, mesh=mesh, in_specs=in_specs, out_specs=out_specs, check_vma=False)
```

time: 102 us -> 76 us (0.75)
  the two profiles are of different devices: /device:TPU:16 before, /device:TPU:0 now
where the time goes in v2:
time: 76 us; the launch traced here: 75.6 us
  waiting for transfers between devices  29.5 us (39%)
  starting transfers between devices  22.4 us (29%)
  Pallas kernels  16.1 us (21%)
  local copies, waits for them, and re-layouts  5.56 us (7%)
  other arithmetic  1.68 us (2%)
    ppermute x11, waiting for transfers between devices, flip(): lax.ppermute(array, axis, [(i, i ^ bits) for i in range(lax.axis_size(axi...  18.5 us
    pallas_call x6, Pallas kernels, call(): pl.pallas_call(kernel, out_shape=out_shape, in_specs=[pl.BlockSpec(memory...  16.1 us
    ppermute x6, starting transfers between devices, ring(): return lax.ppermute(array, 'row', pairs)  10.9 us
    ppermute x6, waiting for transfers between devices, ring(): return lax.ppermute(array, 'row', pairs)  10 us
    ppermute x2, starting transfers between devices, shifted(): lax.ppermute(array, axis, [(i, i + 1) for i in range(lax.axis_size(axis)...  5.83 us
    ppermute x11, starting transfers between devices, flip(): lax.ppermute(array, axis, [(i, i ^ bits) for i in range(lax.axis_size(axi...  5.71 us
    unnamed x17, local copies, waits for them, and re-layouts  5.43 us
  transfers between devices with their start and end apart: 19, of which 12 were waited for; matrix products, arithmetic and copies ran while one was open for 3% of the time, Pallas kernels for 6%

profile of v2, /device:TPU:0, one launch (start us, length us, event | category | flops | bytes accessed | tf_op | source)
XLA Modules:
  0.0 75.6 jit_solution(2786157339446635259)
XLA Ops:
  0.0 2.9 %collective-permute-start.5 = (bf16[576,256]{1,0:T(8,128)(2,1)}, bf16[576,256]{1,0:T(8,128)(2,1)S(1)}, u32[]{:S(2)}, u32[]{:S(2)}) collective-permute-start(bf16[576,256]{1,0:T(8,128)(2,1)} %w0.1), channel_id=1, source_target_pairs={{0,2},{1,3},{2,0},{3,1},{4,6},{5,7},{6,4},{7,5},{8,10},{9,11},{10,... | collective-permute-start | bytes 884744 | tf_op jit(solution)/shard_map/ppermute | solution.py:30
  2.9 0.7 broadcast_compare_fusion
  3.6 0.8 %convert_reduce_fusion = bf16[4]{0:T(256)(128)(2,1)S(1)} fusion(s32[16,32]{1,0:T(8,128)} %phase_ref.1, pred[16,32]{1,0:T(8,128)(4,1)S(1)} %broadcast_compare_fusion), kind=kLoop, calls=%fused_computation.6 | loop fusion | flops 8188 | bytes 2568 | tf_op jit(solution)/shard_map/reduce_sum | solution.py:338
  4.5 0.1 fusion.3
  4.5 0.1 constant_dynamic-slice_fusion
  4.7 1.6 %collective-permute-start = (bf16[96,640]{1,0:T(8,128)(2,1)S(1)}, bf16[96,640]{1,0:T(8,128)(2,1)S(1)}, u32[]{:S(2)}, u32[]{:S(2)}) collective-permute-start(bf16[96,640]{1,0:T(8,128)(2,1)S(1)} %pad_maximum_fusion.refs_0_), channel_id=1, source_target_pairs={{0,8},{4,12},{8,24},{12,28},{16,0},{20,4},{24,16},{28,20},{1,9},{5... | collective-permute-start | bytes 368648 | tf_op jit(solution)/shard_map/ppermute | solution.py:45
  6.3 0.0 collective-permute-start.4
  6.3 1.2 %copy-done.3 = bf16[32,64,256]{2,1,0:T(8,128)(2,1)S(1)} copy-done((bf16[32,64,256]{2,1,0:T(8,128)(2,1)S(1)}, bf16[32,64,256]{2,1,0:T(8,128)(2,1)}, u32[]{:S(2)}) %copy-start.3) | copy-done | bytes 1048600
  7.5 0.7 copy-done.5
  8.2 0.7 copy-done.6
  8.9 1.2 %prepare.1 = (bf16[32,256]{1,0:T(8,128)(2,1)S(1)}, bf16[2,16,32,768]{3,2,1,0:T(8,128)(2,1)S(1)}, bf16[512,512]{1,0:T(8,128)(2,1)S(1)}, bf16[512,512]{1,0:T(8,128)(2,1)S(1)}) custom-call(bf16[32,64,256]{2,1,0:T(8,128)(2,1)S(1)} %copy-done.3, s32[16,32]{1,0:T(8,128)S(1)} %copy-done.5, s32[16,32]{1,0:T(8,128)S(1)} %copy-done.6), custom_call_target="tpu_custom_call" | custom-call | tf_op jit(solution)/shard_map/prepare/pallas_call | solution.py:57
  10.1 2.4 %collective-permute-start.7 = (bf16[32,256]{1,0:T(8,128)(2,1)S(1)}, bf16[32,256]{1,0:T(8,128)(2,1)S(1)}, u32[]{:S(2)}, u32[]{:S(2)}) collective-permute-start(bf16[32,256]{1,0:T(8,128)(2,1)S(1)} %get-tuple-element.36), channel_id=1, source_target_pairs={{0,1},{1,2},{2,3},{4,5},{5,6},{6,7},{8,9},{9,10},{10,11},{12,13},{... | collective-permute-start | bytes 49160 | tf_op jit(solution)/shard_map/ppermute | solution.py:34
  12.5 0.0 collective-permute-done.refs_1_
  12.6 2.6 %collective-permute-start.1 = (bf16[96,640]{1,0:T(8,128)(2,1)S(1)}, bf16[96,640]{1,0:T(8,128)(2,1)S(1)}, u32[]{:S(2)}, u32[]{:S(2)}) collective-permute-start(bf16[96,640]{1,0:T(8,128)(2,1)S(1)} %collective-permute-done.refs_1_), channel_id=1, source_target_pairs={{0,8},{4,12},{8,24},{12,28},{16,0},{20,4},{24,16},{28,20},{1,9},{5... | collective-permute-start | bytes 368648 | tf_op jit(solution)/shard_map/ppermute | solution.py:45
  15.2 0.0 collective-permute-done.5.w2
  15.2 3.6 %collective-permute-done.1.refs_2_ = bf16[96,640]{1,0:T(8,128)(2,1)S(1)} collective-permute-done((bf16[96,640]{1,0:T(8,128)(2,1)S(1)}, bf16[96,640]{1,0:T(8,128)(2,1)S(1)}, u32[]{:S(2)}, u32[]{:S(2)}) %collective-permute-start.1) | collective-permute-done | bytes 122912 | tf_op jit(solution)/shard_map/ppermute | solution.py:45
  18.9 1.7 %collective-permute-start.2 = (bf16[96,640]{1,0:T(8,128)(2,1)S(1)}, bf16[96,640]{1,0:T(8,128)(2,1)S(1)}, u32[]{:S(2)}, u32[]{:S(2)}) collective-permute-start(bf16[96,640]{1,0:T(8,128)(2,1)S(1)} %collective-permute-done.1.refs_2_), channel_id=1, source_target_pairs={{0,8},{4,12},{8,24},{12,28},{16,0},{20,4},{24,16},{28,20},{1,9},{5... | collective-permute-start | bytes 368648 | tf_op jit(solution)/shard_map/ppermute | solution.py:45
  20.6 3.4 %collective-permute-start.8 = (bf16[80,256]{1,0:T(8,128)(2,1)S(1)}, bf16[80,256]{1,0:T(8,128)(2,1)S(1)}, u32[]{:S(2)}, u32[]{:S(2)}) collective-permute-start(bf16[80,256]{1,0:T(8,128)(2,1)S(1)} %pad_maximum_fusion.1), channel_id=1, source_target_pairs={{0,4},{4,8},{8,12},{12,16},{16,20},{20,24},{24,28},{1,5},{5,9},{9,... | collective-permute-start | bytes 122888 | tf_op jit(solution)/shard_map/ppermute | solution.py:34
  24.0 0.7 collective-permute-done.2.refs_3_
  24.7 1.0 %collective-permute-done.8.up_ref = bf16[80,256]{1,0:T(8,128)(2,1)S(1)} collective-permute-done((bf16[80,256]{1,0:T(8,128)(2,1)S(1)}, bf16[80,256]{1,0:T(8,128)(2,1)S(1)}, u32[]{:S(2)}, u32[]{:S(2)}) %collective-permute-start.8) | collective-permute-done | bytes 40992 | tf_op jit(solution)/shard_map/ppermute | solution.py:34
  25.7 0.0 collective-permute-done.4.w1
  25.7 1.0 %copy-done.1 = bf16[256,768]{1,0:T(8,128)(2,1)S(1)} copy-done((bf16[256,768]{1,0:T(8,128)(2,1)S(1)}, bf16[256,768]{1,0:T(8,128)(2,1)}, u32[]{:S(2)}) %copy-start.1) | copy-done | bytes 393240
  26.7 1.0 %copy-done.4 = bf16[576,256]{1,0:T(8,128)(2,1)S(1)} copy-done((bf16[576,256]{1,0:T(8,128)(2,1)S(1)}, bf16[576,256]{1,0:T(8,128)(2,1)}, u32[]{:S(2)}) %copy-start.4) | copy-done | bytes 294936
  27.6 0.7 copy-done.7
  28.3 3.0 %conv.1.f_ref.refs_0_ = bf16[512,256]{1,0:T(8,128)(2,1)S(1)} custom-call(bf16[2,16,32,768]{3,2,1,0:T(8,128)(2,1)S(1)} %get-tuple-element.34.z_hbm, bf16[576,256]{1,0:T(8,128)(2,1)S(1)} %copy-done.4, bf16[576,256]{1,0:T(8,128)(2,1)S(1)} %collective-permute-done.4.w1, bf16[576,256]{1,0:T(8,128)(2,1)S(1)} %collective-permute-done.5.w2, ...), custom_call_target="tpu_custom_call" | custom-call | tf_op jit(solution)/shard_map/conv/pallas_call | solution.py:57
  31.3 3.1 %collective-permute-start.12 = (bf16[512,256]{1,0:T(8,128)(2,1)S(1)}, bf16[512,256]{1,0:T(8,128)(2,1)S(1)}, u32[]{:S(2)}, u32[]{:S(2)}) collective-permute-start(bf16[512,256]{1,0:T(8,128)(2,1)S(1)} %conv.1.f_ref.refs_0_), channel_id=1, source_target_pairs={{0,8},{4,12},{8,24},{12,28},{16,0},{20,4},{24,16},{28,20},{1,9},{5... | collective-permute-start | bytes 786440 | tf_op jit(solution)/shard_map/ppermute | solution.py:45
  34.4 0.6 collective-permute-start.13
  35.0 0.2 copy.9
  35.2 1.0 %merge.1 = (f32[576,256]{1,0:T(8,128)S(1)}, bf16[16,128]{1,0:T(8,128)(2,1)S(1)}) custom-call(bf16[96,640]{1,0:T(8,128)(2,1)S(1)} %pad_maximum_fusion.refs_0_, bf16[96,640]{1,0:T(8,128)(2,1)S(1)} %collective-permute-done.refs_1_, bf16[96,640]{1,0:T(8,128)(2,1)S(1)} %collective-permute-done.1.refs_2_, bf16[96,640]{1,0:T(8,128)(2,1)S(1)} %collective-permute-done.2.refs_3_, ...), custom_call_target="tpu_custom_call" | custom-call | tf_op jit(solution)/shard_map/merge/pallas_call | solution.py:57
  36.2 1.5 %collective-permute-start.3 = (bf16[592,256]{1,0:T(8,128)(2,1)S(1)}, bf16[592,256]{1,0:T(8,128)(2,1)S(1)}, u32[]{:S(2)}, u32[]{:S(2)}) collective-permute-start(bf16[592,256]{1,0:T(8,128)(2,1)S(1)} %fusion.1), channel_id=1, source_target_pairs={{0,4},{4,0},{8,12},{12,8},{16,20},{20,16},{24,28},{28,24},{1,5},{5... | collective-permute-start | bytes 909320 | tf_op jit(solution)/shard_map/ppermute | solution.py:30
  37.7 1.4 %collective-permute-done.12.refs_2_ = bf16[512,256]{1,0:T(8,128)(2,1)S(1)} collective-permute-done((bf16[512,256]{1,0:T(8,128)(2,1)S(1)}, bf16[512,256]{1,0:T(8,128)(2,1)S(1)}, u32[]{:S(2)}, u32[]{:S(2)}) %collective-permute-start.12) | collective-permute-done | bytes 262176 | tf_op jit(solution)/shard_map/ppermute | solution.py:45
  39.1 4.6 %collective-permute-done.13.refs_1_ = bf16[512,256]{1,0:T(8,128)(2,1)S(1)} collective-permute-done((bf16[512,256]{1,0:T(8,128)(2,1)S(1)}, bf16[512,256]{1,0:T(8,128)(2,1)S(1)}, u32[]{:S(2)}, u32[]{:S(2)}) %collective-permute-start.13) | collective-permute-done | bytes 262176 | tf_op jit(solution)/shard_map/ppermute | solution.py:30
  43.6 0.7 collective-permute-start.14
  44.3 0.3 collective-permute-start.15
  44.6 5.0 %collective-permute-done.3 = bf16[592,256]{1,0:T(8,128)(2,1)S(1)} collective-permute-done((bf16[592,256]{1,0:T(8,128)(2,1)S(1)}, bf16[592,256]{1,0:T(8,128)(2,1)S(1)}, u32[]{:S(2)}, u32[]{:S(2)}) %collective-permute-start.3) | collective-permute-done | bytes 303136 | tf_op jit(solution)/shard_map/ppermute | solution.py:30
  49.6 0.1 join.1
  49.7 0.1 collective-permute-start.10
  49.8 1.1 %collective-permute-done.14.refs_4_ = bf16[512,256]{1,0:T(8,128)(2,1)S(1)} collective-permute-done((bf16[512,256]{1,0:T(8,128)(2,1)S(1)}, bf16[512,256]{1,0:T(8,128)(2,1)S(1)}, u32[]{:S(2)}, u32[]{:S(2)}) %collective-permute-start.14) | collective-permute-done | bytes 262176 | tf_op jit(solution)/shard_map/ppermute | solution.py:45
  50.9 1.5 %collective-permute-done.15.refs_3_ = bf16[512,256]{1,0:T(8,128)(2,1)S(1)} collective-permute-done((bf16[512,256]{1,0:T(8,128)(2,1)S(1)}, bf16[512,256]{1,0:T(8,128)(2,1)S(1)}, u32[]{:S(2)}, u32[]{:S(2)}) %collective-permute-start.15) | collective-permute-done | bytes 262176 | tf_op jit(solution)/shard_map/ppermute | solution.py:30
  52.4 1.1 %collective-permute-start.16 = (bf16[512,256]{1,0:T(8,128)(2,1)S(1)}, bf16[512,256]{1,0:T(8,128)(2,1)S(1)}, u32[]{:S(2)}, u32[]{:S(2)}) collective-permute-start(bf16[512,256]{1,0:T(8,128)(2,1)S(1)} %collective-permute-done.14.refs_4_), channel_id=1, source_target_pairs={{0,8},{4,12},{8,24},{12,28},{16,0},{20,4},{24,16},{28,20},{1,9},{5... | collective-permute-start | bytes 786440 | tf_op jit(solution)/shard_map/ppermute | solution.py:45
  53.5 0.3 collective-permute-start.17
  53.8 2.6 %collective-permute-done.10.m2 = bf16[576,256]{1,0:T(8,128)(2,1)S(1)} collective-permute-done((bf16[576,256]{1,0:T(8,128)(2,1)S(1)}, bf16[576,256]{1,0:T(8,128)(2,1)S(1)}, u32[]{:S(2)}, u32[]{:S(2)}) %collective-permute-start.10) | collective-permute-done | bytes 294944 | tf_op jit(solution)/shard_map/ppermute | solution.py:30
  56.5 3.2 %collective-permute-done.16.refs_6_ = bf16[512,256]{1,0:T(8,128)(2,1)S(1)} collective-permute-done((bf16[512,256]{1,0:T(8,128)(2,1)S(1)}, bf16[512,256]{1,0:T(8,128)(2,1)S(1)}, u32[]{:S(2)}, u32[]{:S(2)}) %collective-permute-start.16) | collective-permute-done | bytes 262176 | tf_op jit(solution)/shard_map/ppermute | solution.py:45
  59.7 0.5 collective-permute-done.17.refs_5_
  60.2 0.0 collective-permute-start.18
  60.2 2.0 %queries.1 = (bf16[4,12,128,256]{3,2,1,0:T(8,128)(2,1)S(1)}, bf16[256,768]{1,0:T(8,128)(2,1)S(1)}) custom-call(bf16[512,256]{1,0:T(8,128)(2,1)S(1)} %conv.1.f_ref.refs_0_, bf16[576,256]{1,0:T(8,128)(2,1)S(1)} %get-tuple-element.37.m0, bf16[576,256]{1,0:T(8,128)(2,1)S(1)} %collective-permute-done.9.m1, bf16[576,256]{1,0:T(8,128)(2,1)S(1)} %collective-permute-done.10.m2, ...), custom_call_target="tpu_custom_call" | custom-call | tf_op jit(solution)/shard_map/queries/pallas_call | solution.py:57
  62.2 4.3 %collective-permute-done.18.refs_7_ = bf16[512,256]{1,0:T(8,128)(2,1)S(1)} collective-permute-done((bf16[512,256]{1,0:T(8,128)(2,1)S(1)}, bf16[512,256]{1,0:T(8,128)(2,1)S(1)}, u32[]{:S(2)}, u32[]{:S(2)}) %collective-permute-start.18) | collective-permute-done | bytes 262176 | tf_op jit(solution)/shard_map/ppermute | solution.py:30
  66.5 8.9 %attend.1 = bf16[512,768]{1,0:T(8,128)(2,1)} custom-call(s32[8,128]{1,0:T(8,128)S(1)} %get-tuple-element.33.counts_ref, bf16[4,12,128,256]{3,2,1,0:T(8,128)(2,1)S(1)} %get-tuple-element.38.q_hbm, bf16[256,768]{1,0:T(8,128)(2,1)S(1)} %get-tuple-element.39.v_hbm, bf16[512,512]{1,0:T(8,128)(2,1)S(1)} %get-tuple-element.40.back_hbm, ...), custom_call_target="tpu_custom_call" | custom-call | tf_op jit(solution)/shard_map/attend/pallas_call | solution.py:57
  (25 shorter events, 0.2 us)
Async XLA Ops:
  0.0 4.5 %copy-start = (bf16[96,2304]{1,0:T(8,128)(2,1)S(1)}, bf16[96,2304]{1,0:T(8,128)(2,1)}, u32[]{:S(2)}) copy-start(bf16[96,2304]{1,0:T(8,128)(2,1)} %param.11) | copy-start | bytes 1327108
  0.0 35.0 %copy-start.2 = (bf16[256,768]{1,0:T(8,128)(2,1)S(1)}, bf16[256,768]{1,0:T(8,128)(2,1)}, u32[]{:S(2)}) copy-start(bf16[256,768]{1,0:T(8,128)(2,1)} %proj_hbm.1) | copy-start | bytes 1179652
  0.0 15.2 %collective-permute-start.5 = (bf16[576,256]{1,0:T(8,128)(2,1)}, bf16[576,256]{1,0:T(8,128)(2,1)S(1)}, u32[]{:S(2)}, u32[]{:S(2)}) collective-permute-start(bf16[576,256]{1,0:T(8,128)(2,1)} %w0.1), channel_id=1, source_target_pairs={{0,2},{1,3},{2,0},{3,1},{4,6},{5,7},{6,4},{7,5},{8,10},{9,11},{10,... | collective-permute-start | bytes 884744 | tf_op jit(solution)/shard_map/ppermute | solution.py:30
  4.7 7.9 %collective-permute-start = (bf16[96,640]{1,0:T(8,128)(2,1)S(1)}, bf16[96,640]{1,0:T(8,128)(2,1)S(1)}, u32[]{:S(2)}, u32[]{:S(2)}) collective-permute-start(bf16[96,640]{1,0:T(8,128)(2,1)S(1)} %pad_maximum_fusion.refs_0_), channel_id=1, source_target_pairs={{0,8},{4,12},{8,24},{12,28},{16,0},{20,4},{24,16},{28,20},{1,9},{5... | collective-permute-start | bytes 368648 | tf_op jit(solution)/shard_map/ppermute | solution.py:45
  6.3 19.3 %collective-permute-start.4 = (bf16[576,256]{1,0:T(8,128)(2,1)}, bf16[576,256]{1,0:T(8,128)(2,1)S(1)}, u32[]{:S(2)}, u32[]{:S(2)}) collective-permute-start(bf16[576,256]{1,0:T(8,128)(2,1)} %w0.1), channel_id=1, source_target_pairs={{0,1},{1,0},{2,3},{3,2},{4,5},{5,4},{6,7},{7,6},{8,9},{9,8},{10,11... | collective-permute-start | bytes 884744 | tf_op jit(solution)/shard_map/ppermute | solution.py:30
  6.3 1.2 %copy-start.3 = (bf16[32,64,256]{2,1,0:T(8,128)(2,1)S(1)}, bf16[32,64,256]{2,1,0:T(8,128)(2,1)}, u32[]{:S(2)}) copy-start(bf16[32,64,256]{2,1,0:T(8,128)(2,1)} %x_ref.1) | copy-start | bytes 3145732
  7.5 0.7 copy-start.5
  8.2 0.7 copy-start.6
  10.1 5.1 %collective-permute-start.7 = (bf16[32,256]{1,0:T(8,128)(2,1)S(1)}, bf16[32,256]{1,0:T(8,128)(2,1)S(1)}, u32[]{:S(2)}, u32[]{:S(2)}) collective-permute-start(bf16[32,256]{1,0:T(8,128)(2,1)S(1)} %get-tuple-element.36), channel_id=1, source_target_pairs={{0,1},{1,2},{2,3},{4,5},{5,6},{6,7},{8,9},{9,10},{10,11},{12,13},{... | collective-permute-start | bytes 49160 | tf_op jit(solution)/shard_map/ppermute | solution.py:34
  12.6 6.3 %collective-permute-start.1 = (bf16[96,640]{1,0:T(8,128)(2,1)S(1)}, bf16[96,640]{1,0:T(8,128)(2,1)S(1)}, u32[]{:S(2)}, u32[]{:S(2)}) collective-permute-start(bf16[96,640]{1,0:T(8,128)(2,1)S(1)} %collective-permute-done.refs_1_), channel_id=1, source_target_pairs={{0,8},{4,12},{8,24},{12,28},{16,0},{20,4},{24,16},{28,20},{1,9},{5... | collective-permute-start | bytes 368648 | tf_op jit(solution)/shard_map/ppermute | solution.py:45
  15.2 10.5 %collective-permute-start.6 = (bf16[576,256]{1,0:T(8,128)(2,1)S(1)}, bf16[576,256]{1,0:T(8,128)(2,1)S(1)}, u32[]{:S(2)}, u32[]{:S(2)}) collective-permute-start(bf16[576,256]{1,0:T(8,128)(2,1)S(1)} %collective-permute-done.5.w2), channel_id=1, source_target_pairs={{0,1},{1,0},{2,3},{3,2},{4,5},{5,4},{6,7},{7,6},{8,9},{9,8},{10,11... | collective-permute-start | bytes 884744 | tf_op jit(solution)/shard_map/ppermute | solution.py:30
  18.9 5.8 %collective-permute-start.2 = (bf16[96,640]{1,0:T(8,128)(2,1)S(1)}, bf16[96,640]{1,0:T(8,128)(2,1)S(1)}, u32[]{:S(2)}, u32[]{:S(2)}) collective-permute-start(bf16[96,640]{1,0:T(8,128)(2,1)S(1)} %collective-permute-done.1.refs_2_), channel_id=1, source_target_pairs={{0,8},{4,12},{8,24},{12,28},{16,0},{20,4},{24,16},{28,20},{1,9},{5... | collective-permute-start | bytes 368648 | tf_op jit(solution)/shard_map/ppermute | solution.py:45
  20.6 5.1 %collective-permute-start.8 = (bf16[80,256]{1,0:T(8,128)(2,1)S(1)}, bf16[80,256]{1,0:T(8,128)(2,1)S(1)}, u32[]{:S(2)}, u32[]{:S(2)}) collective-permute-start(bf16[80,256]{1,0:T(8,128)(2,1)S(1)} %pad_maximum_fusion.1), channel_id=1, source_target_pairs={{0,4},{4,8},{8,12},{12,16},{16,20},{20,24},{24,28},{1,5},{5,9},{9,... | collective-permute-start | bytes 122888 | tf_op jit(solution)/shard_map/ppermute | solution.py:34
  25.7 1.0 %copy-start.1 = (bf16[256,768]{1,0:T(8,128)(2,1)S(1)}, bf16[256,768]{1,0:T(8,128)(2,1)}, u32[]{:S(2)}) copy-start(bf16[256,768]{1,0:T(8,128)(2,1)} %proj_hbm.1) | copy-start | bytes 1179652
  26.7 1.0 %copy-start.4 = (bf16[576,256]{1,0:T(8,128)(2,1)S(1)}, bf16[576,256]{1,0:T(8,128)(2,1)}, u32[]{:S(2)}) copy-start(bf16[576,256]{1,0:T(8,128)(2,1)} %w0.1) | copy-start | bytes 884740
  27.6 0.7 copy-start.7
  31.3 7.8 %collective-permute-start.12 = (bf16[512,256]{1,0:T(8,128)(2,1)S(1)}, bf16[512,256]{1,0:T(8,128)(2,1)S(1)}, u32[]{:S(2)}, u32[]{:S(2)}) collective-permute-start(bf16[512,256]{1,0:T(8,128)(2,1)S(1)} %conv.1.f_ref.refs_0_), channel_id=1, source_target_pairs={{0,8},{4,12},{8,24},{12,28},{16,0},{20,4},{24,16},{28,20},{1,9},{5... | collective-permute-start | bytes 786440 | tf_op jit(solution)/shard_map/ppermute | solution.py:45
  34.4 9.2 %collective-permute-start.13 = (bf16[512,256]{1,0:T(8,128)(2,1)S(1)}, bf16[512,256]{1,0:T(8,128)(2,1)S(1)}, u32[]{:S(2)}, u32[]{:S(2)}) collective-permute-start(bf16[512,256]{1,0:T(8,128)(2,1)S(1)} %conv.1.f_ref.refs_0_), channel_id=1, source_target_pairs={{0,4},{4,0},{8,12},{12,8},{16,20},{20,16},{24,28},{28,24},{1,5},{5... | collective-permute-start | bytes 786440 | tf_op jit(solution)/shard_map/ppermute | solution.py:30
  36.2 13.4 %collective-permute-start.3 = (bf16[592,256]{1,0:T(8,128)(2,1)S(1)}, bf16[592,256]{1,0:T(8,128)(2,1)S(1)}, u32[]{:S(2)}, u32[]{:S(2)}) collective-permute-start(bf16[592,256]{1,0:T(8,128)(2,1)S(1)} %fusion.1), channel_id=1, source_target_pairs={{0,4},{4,0},{8,12},{12,8},{16,20},{20,16},{24,28},{28,24},{1,5},{5... | collective-permute-start | bytes 909320 | tf_op jit(solution)/shard_map/ppermute | solution.py:30
  43.6 7.3 %collective-permute-start.14 = (bf16[512,256]{1,0:T(8,128)(2,1)S(1)}, bf16[512,256]{1,0:T(8,128)(2,1)S(1)}, u32[]{:S(2)}, u32[]{:S(2)}) collective-permute-start(bf16[512,256]{1,0:T(8,128)(2,1)S(1)} %collective-permute-done.12.refs_2_), channel_id=1, source_target_pairs={{0,8},{4,12},{8,24},{12,28},{16,0},{20,4},{24,16},{28,20},{1,9},{5... | collective-permute-start | bytes 786440 | tf_op jit(solution)/shard_map/ppermute | solution.py:45
  44.3 8.1 %collective-permute-start.15 = (bf16[512,256]{1,0:T(8,128)(2,1)S(1)}, bf16[512,256]{1,0:T(8,128)(2,1)S(1)}, u32[]{:S(2)}, u32[]{:S(2)}) collective-permute-start(bf16[512,256]{1,0:T(8,128)(2,1)S(1)} %collective-permute-done.12.refs_2_), channel_id=1, source_target_pairs={{0,4},{4,0},{8,12},{12,8},{16,20},{20,16},{24,28},{28,24},{1,5},{5... | collective-permute-start | bytes 786440 | tf_op jit(solution)/shard_map/ppermute | solution.py:30
  49.7 6.8 %collective-permute-start.10 = (bf16[576,256]{1,0:T(8,128)(2,1)S(1)}, bf16[576,256]{1,0:T(8,128)(2,1)S(1)}, u32[]{:S(2)}, u32[]{:S(2)}) collective-permute-start(bf16[576,256]{1,0:T(8,128)(2,1)S(1)} %get-tuple-element.37.m0), channel_id=1, source_target_pairs={{0,2},{1,3},{2,0},{3,1},{4,6},{5,7},{6,4},{7,5},{8,10},{9,11},{10,... | collective-permute-start | bytes 884744 | tf_op jit(solution)/shard_map/ppermute | solution.py:30
  52.4 7.3 %collective-permute-start.16 = (bf16[512,256]{1,0:T(8,128)(2,1)S(1)}, bf16[512,256]{1,0:T(8,128)(2,1)S(1)}, u32[]{:S(2)}, u32[]{:S(2)}) collective-permute-start(bf16[512,256]{1,0:T(8,128)(2,1)S(1)} %collective-permute-done.14.refs_4_), channel_id=1, source_target_pairs={{0,8},{4,12},{8,24},{12,28},{16,0},{20,4},{24,16},{28,20},{1,9},{5... | collective-permute-start | bytes 786440 | tf_op jit(solution)/shard_map/ppermute | solution.py:45
  53.5 6.6 %collective-permute-start.17 = (bf16[512,256]{1,0:T(8,128)(2,1)S(1)}, bf16[512,256]{1,0:T(8,128)(2,1)S(1)}, u32[]{:S(2)}, u32[]{:S(2)}) collective-permute-start(bf16[512,256]{1,0:T(8,128)(2,1)S(1)} %collective-permute-done.14.refs_4_), channel_id=1, source_target_pairs={{0,4},{4,0},{8,12},{12,8},{16,20},{20,16},{24,28},{28,24},{1,5},{5... | collective-permute-start | bytes 786440 | tf_op jit(solution)/shard_map/ppermute | solution.py:30
  53.8 6.4 %collective-permute-start.9 = (bf16[576,256]{1,0:T(8,128)(2,1)S(1)}, bf16[576,256]{1,0:T(8,128)(2,1)S(1)}, u32[]{:S(2)}, u32[]{:S(2)}) collective-permute-start(bf16[576,256]{1,0:T(8,128)(2,1)S(1)} %get-tuple-element.37.m0), channel_id=1, source_target_pairs={{0,1},{1,0},{2,3},{3,2},{4,5},{5,4},{6,7},{7,6},{8,9},{9,8},{10,11... | collective-permute-start | bytes 884744 | tf_op jit(solution)/shard_map/ppermute | solution.py:30
  56.5 3.7 %collective-permute-start.11 = (bf16[576,256]{1,0:T(8,128)(2,1)S(1)}, bf16[576,256]{1,0:T(8,128)(2,1)S(1)}, u32[]{:S(2)}, u32[]{:S(2)}) collective-permute-start(bf16[576,256]{1,0:T(8,128)(2,1)S(1)} %collective-permute-done.10.m2), channel_id=1, source_target_pairs={{0,1},{1,0},{2,3},{3,2},{4,5},{5,4},{6,7},{7,6},{8,9},{9,8},{10,11... | collective-permute-start | bytes 884744 | tf_op jit(solution)/shard_map/ppermute | solution.py:30
  60.2 6.4 %collective-permute-start.18 = (bf16[512,256]{1,0:T(8,128)(2,1)S(1)}, bf16[512,256]{1,0:T(8,128)(2,1)S(1)}, u32[]{:S(2)}, u32[]{:S(2)}) collective-permute-start(bf16[512,256]{1,0:T(8,128)(2,1)S(1)} %collective-permute-done.16.refs_6_), channel_id=1, source_target_pairs={{0,4},{4,0},{8,12},{12,8},{16,20},{20,16},{24,28},{28,24},{1,5},{5... | collective-permute-start | bytes 786440 | tf_op jit(solution)/shard_map/ppermute | solution.py:30

commit v3 on v2

--- a/solution.py
+++ b/solution.py
@@ -53,7 +53,7 @@
     return found
 
 
-def call(kernel, out_shape, in_spaces, out_spaces, scratch, args, name):
+def call(kernel, out_shape, in_spaces, out_spaces, scratch, args, name, mib):
     return pl.pallas_call(
         kernel,
         out_shape=out_shape,
@@ -64,17 +64,17 @@
             else pl.BlockSpec(memory_space=out_spaces)
         ),
         scratch_shapes=scratch,
-        compiler_params=pltpu.CompilerParams(vmem_limit_bytes=40 * 1024 * 1024),
+        compiler_params=pltpu.CompilerParams(vmem_limit_bytes=mib * 1024 * 1024),
         cost_estimate=pl.CostEstimate(flops=0, bytes_accessed=0, transcendentals=0),
         name=name,
     )(*args)
 
 
 def prepare_kernel(
-    x_ref, tissue_ref, phase_ref, left_ref, z_ref, sort_ref, back_ref, wide
+    x_ref, label_ref, left_ref, z_ref, sort_ref, back_ref, wide
 ):
     rows, cols, channels = x_ref.shape
-    out_rows, out_cols = tissue_ref.shape
+    out_rows, out_cols = label_ref.shape
     half = cols // 2
     tokens = out_rows * out_cols
     bucket = tokens // PHASES
@@ -95,7 +95,7 @@
     def iota(shape, axis):
         return lax.broadcasted_iota(jnp.int32, shape, axis)
 
-    labels = (phase_ref[...] * 2 + 1 - tissue_ref[...]).astype(F32).astype(BF16)
+    labels = label_ref[...].astype(BF16)
     spread = (iota((out_cols, tokens), 0) == lax.rem(iota((out_cols, tokens), 1), out_cols)).astype(F32)
     along = dot(labels, spread.astype(BF16))
     in_row = iota((out_rows, tokens), 0) == iota((out_rows, tokens), 1) // out_cols
@@ -234,11 +234,20 @@
 
 
 def attend_kernel(spare, counts_ref, q_hbm, v_hbm, back_hbm, *refs):
-    items = refs[:SEGMENT]
-    out_ref, rows32, keys, keys_t, mixed, q_ref, v_ref, back_ref, sems = refs[SEGMENT:]
+    around, across = refs[:4], refs[4:8]
+    out_ref, rows32, keys, keys_t, mixed, q_ref, v_ref, back_ref, sems = refs[8:]
     phases, heads, bucket, channels = q_ref.shape
     tokens = phases * bucket
     group = SEGMENT * bucket
+
+    def part_of(j, p):
+        step, side = j // 2, j % 2
+        if side == 0:
+            return around[step], p * bucket
+        if step != 1 or 2 * p < phases:
+            return across[step], p * bucket
+        return around[2], tokens + (2 * p - phases) * bucket // 2
+
     halves = range(channels // LANES)
     parts = 6
     share = heads // parts
@@ -252,9 +261,10 @@
     for p in range(phases):
         filled = 0
         for j in range(SEGMENT):
+            source, first = part_of(j, p)
             for c in halves:
-                rows32[p, c, pl.ds(filled, bucket), :] = items[j][
-                    p * bucket : (p + 1) * bucket, c * LANES : (c + 1) * LANES
+                rows32[p, c, pl.ds(filled, bucket), :] = source[
+                    first : first + bucket, c * LANES : (c + 1) * LANES
                 ].astype(F32)
             filled = filled + counts_ref[j, spare + p]
         for c in halves:
@@ -317,6 +327,7 @@
     weight_x = flip(conv_weight, "col", 2)
     weight_core = flip(conv_weight, "col", 1)
     weight_far = flip(weight_x, "col", 1)
+    labels = (phase * 2 + 1 - tissue).astype(F32)
     left, z, sort, back = call(
         prepare_kernel,
         (
@@ -325,16 +336,17 @@
             jax.ShapeDtypeStruct((tokens, tokens), BF16),
             jax.ShapeDtypeStruct((tokens, tokens), BF16),
         ),
-        [VMEM] * 3,
+        [VMEM] * 2,
         (VMEM,) * 4,
         [VMEM((in_rows, channels // LANES, in_cols + 8, LANES), F32)],
-        (feat_in, tissue, phase),
+        (feat_in, labels),
         "prepare",
+        24,
     )
     left = shifted(left, "col")
     up = shifted(jnp.concatenate([left[in_rows - 16 :], feat_in[in_rows - 1]], axis=0), "row")
 
-    here = (phase[None] == jnp.arange(PHASES, dtype=jnp.int32)[:, None, None]) & (tissue[None] > 0)
+    here = labels[None] == 2.0 * jnp.arange(PHASES, dtype=F32)[:, None, None]
     own_counts = jnp.sum(here.astype(F32), axis=(1, 2)).astype(BF16)
     qkv_mine = lax.dynamic_slice(
         qkv_weight, (0, lax.axis_index("col") * share), (depth, share)
@@ -381,18 +393,20 @@
             conv_bias.reshape(1, channels),
         ),
         "conv",
-    )
-
-    items = []
-    item = mine
+        24,
+    )
+
+    half = tokens // 2
+    around, across = [mine], []
+    message = mine
     for step in range(4):
+        passed = flip(message[:half] if step == 1 else message[:tokens], "row", 1)
         if step < 3:
-            later, beside = ring(item), flip(item, "row", 1)
-            later, beside = lax.optimization_barrier((later, beside))
-        else:
-            later, beside = None, flip(item, "row", 1)
-        items += [item, beside]
-        item = later
+            message, passed = lax.optimization_barrier((ring(message[:tokens] if step == 2 else message), passed))
+            around.append(message)
+        across.append(passed)
+        if step == 0:
+            message = jnp.concatenate([message, passed[half:]], axis=0)
 
     merged, counts_mine = call(
         functools.partial(merge_kernel, ordered),
@@ -405,6 +419,7 @@
         [],
         (*pieces, proj_weight.T),
         "merge",
+        16,
     )
     if not ordered:
         got = flip(jnp.concatenate([merged.astype(BF16), jnp.pad(counts_mine, ((0, 0), (0, channels - LANES)))], axis=0), "row", 1)
@@ -419,6 +434,7 @@
             [],
             (merged, got[:share], counts_mine, got[share:, :LANES]),
             "join",
+            16,
         )
     merged_x = flip(merged, "col", 2)
     merged_core = flip(merged, "col", 1)
@@ -435,6 +451,7 @@
         [VMEM((out_width, channels), BF16), pltpu.SemaphoreType.DMA((4,))],
         (mine, merged, merged_core, merged_x, merged_far),
         "queries",
+        24,
     )
     group = SEGMENT * bucket
     attended = call(
@@ -452,8 +469,9 @@
             VMEM((tokens, tokens), BF16),
             pltpu.SemaphoreType.DMA((3,)),
         ],
-        (counts, queries, values, back, *items),
+        (counts, queries, values, back, *around, *across),
         "attend",
+        36,
     )
     return attended.reshape(out_rows, out_cols, width)
 

time: 76 us -> 74.2 us (0.976); the launches traced: 75.6 us -> 73 us
  waiting for transfers between devices: 29.5 us -> 26.4 us
  starting transfers between devices: 22.4 us -> 24.8 us
  local copies, waits for them, and re-layouts: 5.56 us -> 4.21 us
    ppermute x11, waiting for transfers between devices: 18.5 us -> 14.5 us  [flip(): lax.ppermute(array, axis, [(i, i ^ bits) for i in range(lax.axis_size(axi...]
    ppermute x11, starting transfers between devices: 5.71 us -> 7.54 us  [flip(): lax.ppermute(array, axis, [(i, i ^ bits) for i in range(lax.axis_size(axi...]
    unnamed x17 -> x13, local copies, waits for them, and re-layouts: 5.43 us -> 4.04 us
    ppermute x6, waiting for transfers between devices: 10 us -> 11 us  [ring(): return lax.ppermute(array, 'row', pairs)]
  transfers between devices with their start and end apart: 19 -> 19, of which waited for: 12 -> 12; matrix products, arithmetic and copies ran while one was open for 3% -> 2% of each run, Pallas kernels for 6% -> 6%
where the time goes in v3:
time: 74.2 us; the launch traced here: 73 us
  waiting for transfers between devices  26.4 us (36%)
  starting transfers between devices  24.8 us (33%)
  Pallas kernels  16.1 us (22%)
  local copies, waits for them, and re-layouts  4.21 us (6%)
  other arithmetic  1.1 us (1%)
    pallas_call x6, Pallas kernels, call(): pl.pallas_call(kernel, out_shape=out_shape, in_specs=[pl.BlockSpec(memory...  16.1 us
    ppermute x11, waiting for transfers between devices, flip(): lax.ppermute(array, axis, [(i, i ^ bits) for i in range(lax.axis_size(axi...  14.5 us
    ppermute x6, starting transfers between devices, ring(): return lax.ppermute(array, 'row', pairs)  11.4 us
    ppermute x6, waiting for transfers between devices, ring(): return lax.ppermute(array, 'row', pairs)  11 us
    ppermute x11, starting transfers between devices, flip(): lax.ppermute(array, axis, [(i, i ^ bits) for i in range(lax.axis_size(axi...  7.54 us
    ppermute x2, starting transfers between devices, shifted(): lax.ppermute(array, axis, [(i, i + 1) for i in range(lax.axis_size(axis)...  5.83 us
    unnamed x13, local copies, waits for them, and re-layouts  4.04 us
  transfers between devices with their start and end apart: 19, of which 12 were waited for; matrix products, arithmetic and copies ran while one was open for 2% of the time, Pallas kernels for 6%

profile of v3, /device:TPU:0, one launch (start us, length us, event | category | flops | bytes accessed | tf_op | source)
XLA Modules:
  0.0 73.0 jit_solution(17380663290406098073)
XLA Ops:
  0.0 2.9 %collective-permute-start.5 = (bf16[576,256]{1,0:T(8,128)(2,1)}, bf16[576,256]{1,0:T(8,128)(2,1)S(1)}, u32[]{:S(2)}, u32[]{:S(2)}) collective-permute-start(bf16[576,256]{1,0:T(8,128)(2,1)} %w0.1), channel_id=1, source_target_pairs={{0,2},{1,3},{2,0},{3,1},{4,6},{5,7},{6,4},{7,5},{8,10},{9,11},{10,... | collective-permute-start | bytes 884744 | tf_op jit(solution)/shard_map/ppermute | solution.py:30
  3.0 0.7 subtract_convert_fusion.label_ref
  3.7 0.2 convert_reduce_fusion
  3.9 0.1 fusion.2
  3.9 0.1 constant_dynamic-slice_fusion
  4.1 1.6 %collective-permute-start = (bf16[96,640]{1,0:T(8,128)(2,1)S(1)}, bf16[96,640]{1,0:T(8,128)(2,1)S(1)}, u32[]{:S(2)}, u32[]{:S(2)}) collective-permute-start(bf16[96,640]{1,0:T(8,128)(2,1)S(1)} %pad_maximum_fusion.1.refs_0_), channel_id=1, source_target_pairs={{0,8},{4,12},{8,24},{12,28},{16,0},{20,4},{24,16},{28,20},{1,9},{5... | collective-permute-start | bytes 368648 | tf_op jit(solution)/shard_map/ppermute | solution.py:45
  5.7 0.0 collective-permute-start.4
  5.7 1.2 %copy-done.3 = bf16[32,64,256]{2,1,0:T(8,128)(2,1)S(1)} copy-done((bf16[32,64,256]{2,1,0:T(8,128)(2,1)S(1)}, bf16[32,64,256]{2,1,0:T(8,128)(2,1)}, u32[]{:S(2)}) %copy-start.3) | copy-done | bytes 1048600
  6.9 1.2 %prepare.1 = (bf16[32,256]{1,0:T(8,128)(2,1)S(1)}, bf16[2,16,32,768]{3,2,1,0:T(8,128)(2,1)S(1)}, bf16[512,512]{1,0:T(8,128)(2,1)S(1)}, bf16[512,512]{1,0:T(8,128)(2,1)S(1)}) custom-call(bf16[32,64,256]{2,1,0:T(8,128)(2,1)S(1)} %copy-done.3, f32[16,32]{1,0:T(8,128)S(1)} %subtract_convert_fusion.label_ref), custom_call_target="tpu_custom_call" | custom-call | tf_op jit(solution)/shard_map/prepare/pallas_call | solution.py:57
  8.1 2.4 %collective-permute-start.7 = (bf16[32,256]{1,0:T(8,128)(2,1)S(1)}, bf16[32,256]{1,0:T(8,128)(2,1)S(1)}, u32[]{:S(2)}, u32[]{:S(2)}) collective-permute-start(bf16[32,256]{1,0:T(8,128)(2,1)S(1)} %get-tuple-element.36), channel_id=1, source_target_pairs={{0,1},{1,2},{2,3},{4,5},{5,6},{6,7},{8,9},{9,10},{10,11},{12,13},{... | collective-permute-start | bytes 49160 | tf_op jit(solution)/shard_map/ppermute | solution.py:34
  10.5 0.0 collective-permute-done.refs_1_
  10.6 2.6 %collective-permute-start.1 = (bf16[96,640]{1,0:T(8,128)(2,1)S(1)}, bf16[96,640]{1,0:T(8,128)(2,1)S(1)}, u32[]{:S(2)}, u32[]{:S(2)}) collective-permute-start(bf16[96,640]{1,0:T(8,128)(2,1)S(1)} %collective-permute-done.refs_1_), channel_id=1, source_target_pairs={{0,8},{4,12},{8,24},{12,28},{16,0},{20,4},{24,16},{28,20},{1,9},{5... | collective-permute-start | bytes 368648 | tf_op jit(solution)/shard_map/ppermute | solution.py:45
  13.2 0.0 collective-permute-done.5.w2
  13.2 0.0 collective-permute-start.6
  13.2 3.6 %collective-permute-done.1.refs_2_ = bf16[96,640]{1,0:T(8,128)(2,1)S(1)} collective-permute-done((bf16[96,640]{1,0:T(8,128)(2,1)S(1)}, bf16[96,640]{1,0:T(8,128)(2,1)S(1)}, u32[]{:S(2)}, u32[]{:S(2)}) %collective-permute-start.1) | collective-permute-done | bytes 122912 | tf_op jit(solution)/shard_map/ppermute | solution.py:45
  16.9 1.7 %collective-permute-start.2 = (bf16[96,640]{1,0:T(8,128)(2,1)S(1)}, bf16[96,640]{1,0:T(8,128)(2,1)S(1)}, u32[]{:S(2)}, u32[]{:S(2)}) collective-permute-start(bf16[96,640]{1,0:T(8,128)(2,1)S(1)} %collective-permute-done.1.refs_2_), channel_id=1, source_target_pairs={{0,8},{4,12},{8,24},{12,28},{16,0},{20,4},{24,16},{28,20},{1,9},{5... | collective-permute-start | bytes 368648 | tf_op jit(solution)/shard_map/ppermute | solution.py:45
  18.6 3.4 %collective-permute-start.8 = (bf16[80,256]{1,0:T(8,128)(2,1)S(1)}, bf16[80,256]{1,0:T(8,128)(2,1)S(1)}, u32[]{:S(2)}, u32[]{:S(2)}) collective-permute-start(bf16[80,256]{1,0:T(8,128)(2,1)S(1)} %pad_maximum_fusion.2), channel_id=1, source_target_pairs={{0,4},{4,8},{8,12},{12,16},{16,20},{20,24},{24,28},{1,5},{5,9},{9,... | collective-permute-start | bytes 122888 | tf_op jit(solution)/shard_map/ppermute | solution.py:34
  22.0 0.7 collective-permute-done.2.refs_3_
  22.7 1.0 %collective-permute-done.8.up_ref = bf16[80,256]{1,0:T(8,128)(2,1)S(1)} collective-permute-done((bf16[80,256]{1,0:T(8,128)(2,1)S(1)}, bf16[80,256]{1,0:T(8,128)(2,1)S(1)}, u32[]{:S(2)}, u32[]{:S(2)}) %collective-permute-start.8) | collective-permute-done | bytes 40992 | tf_op jit(solution)/shard_map/ppermute | solution.py:34
  23.7 0.0 collective-permute-done.4.w1
  23.7 0.0 collective-permute-done.6.w3
  23.7 1.0 %copy-done.1 = bf16[256,768]{1,0:T(8,128)(2,1)S(1)} copy-done((bf16[256,768]{1,0:T(8,128)(2,1)S(1)}, bf16[256,768]{1,0:T(8,128)(2,1)}, u32[]{:S(2)}) %copy-start.1) | copy-done | bytes 393240
  24.7 1.0 %copy-done.4 = bf16[576,256]{1,0:T(8,128)(2,1)S(1)} copy-done((bf16[576,256]{1,0:T(8,128)(2,1)S(1)}, bf16[576,256]{1,0:T(8,128)(2,1)}, u32[]{:S(2)}) %copy-start.4) | copy-done | bytes 294936
  25.6 0.7 copy-done.5
  26.3 3.0 %conv.1.f_ref.refs_0_ = bf16[512,256]{1,0:T(8,128)(2,1)S(1)} custom-call(bf16[2,16,32,768]{3,2,1,0:T(8,128)(2,1)S(1)} %get-tuple-element.34.z_hbm, bf16[576,256]{1,0:T(8,128)(2,1)S(1)} %copy-done.4, bf16[576,256]{1,0:T(8,128)(2,1)S(1)} %collective-permute-done.4.w1, bf16[576,256]{1,0:T(8,128)(2,1)S(1)} %collective-permute-done.5.w2, ...), custom_call_target="tpu_custom_call" | custom-call | tf_op jit(solution)/shard_map/conv/pallas_call | solution.py:57
  29.3 3.1 %collective-permute-start.12 = (bf16[512,256]{1,0:T(8,128)(2,1)S(1)}, bf16[512,256]{1,0:T(8,128)(2,1)S(1)}, u32[]{:S(2)}, u32[]{:S(2)}) collective-permute-start(bf16[512,256]{1,0:T(8,128)(2,1)S(1)} %conv.1.f_ref.refs_0_), channel_id=1, source_target_pairs={{0,8},{4,12},{8,24},{12,28},{16,0},{20,4},{24,16},{28,20},{1,9},{5... | collective-permute-start | bytes 786440 | tf_op jit(solution)/shard_map/ppermute | solution.py:45
  32.4 0.6 collective-permute-start.13
  33.0 0.2 copy.9
  33.2 1.0 %merge.1 = (f32[576,256]{1,0:T(8,128)S(1)}, bf16[16,128]{1,0:T(8,128)(2,1)S(1)}) custom-call(bf16[96,640]{1,0:T(8,128)(2,1)S(1)} %pad_maximum_fusion.1.refs_0_, bf16[96,640]{1,0:T(8,128)(2,1)S(1)} %collective-permute-done.refs_1_, bf16[96,640]{1,0:T(8,128)(2,1)S(1)} %collective-permute-done.1.refs_2_, bf16[96,640]{1,0:T(8,128)(2,1)S(1)} %collective-permute-done.2.refs_3_, ...), custom_call_target="tpu_custom_call" | custom-call | tf_op jit(solution)/shard_map/merge/pallas_call | solution.py:57
  34.2 2.9 %collective-permute-done.12.refs_1_ = bf16[512,256]{1,0:T(8,128)(2,1)S(1)} collective-permute-done((bf16[512,256]{1,0:T(8,128)(2,1)S(1)}, bf16[512,256]{1,0:T(8,128)(2,1)S(1)}, u32[]{:S(2)}, u32[]{:S(2)}) %collective-permute-start.12) | collective-permute-done | bytes 262176 | tf_op jit(solution)/shard_map/ppermute | solution.py:45
  37.1 2.1 %collective-permute-done.13.refs_4_ = bf16[512,256]{1,0:T(8,128)(2,1)S(1)} collective-permute-done((bf16[512,256]{1,0:T(8,128)(2,1)S(1)}, bf16[512,256]{1,0:T(8,128)(2,1)S(1)}, u32[]{:S(2)}, u32[]{:S(2)}) %collective-permute-start.13) | collective-permute-done | bytes 262176 | tf_op jit(solution)/shard_map/ppermute | solution.py:30
  39.2 0.3 collective-permute-start.14
  39.6 0.6 collective-permute-start.3
  40.1 1.6 %collective-permute-start.15 = (bf16[256,256]{1,0:T(8,128)(2,1)S(1)}, bf16[256,256]{1,0:T(8,128)(2,1)S(1)}, u32[]{:S(2)}, u32[]{:S(2)}) collective-permute-start(bf16[256,256]{1,0:T(8,128)(2,1)S(1)} %slice.27), channel_id=1, source_target_pairs={{0,4},{4,0},{8,12},{12,8},{16,20},{20,16},{24,28},{28,24},{1,5},{5... | collective-permute-start | bytes 393224 | tf_op jit(solution)/shard_map/ppermute | solution.py:30
  41.7 4.9 %collective-permute-done.3 = bf16[592,256]{1,0:T(8,128)(2,1)S(1)} collective-permute-done((bf16[592,256]{1,0:T(8,128)(2,1)S(1)}, bf16[592,256]{1,0:T(8,128)(2,1)S(1)}, u32[]{:S(2)}, u32[]{:S(2)}) %collective-permute-start.3) | collective-permute-done | bytes 303136 | tf_op jit(solution)/shard_map/ppermute | solution.py:30
  46.7 0.1 join.1
  46.8 1.1 %collective-permute-start.10 = (bf16[576,256]{1,0:T(8,128)(2,1)S(1)}, bf16[576,256]{1,0:T(8,128)(2,1)S(1)}, u32[]{:S(2)}, u32[]{:S(2)}) collective-permute-start(bf16[576,256]{1,0:T(8,128)(2,1)S(1)} %get-tuple-element.37.m0), channel_id=1, source_target_pairs={{0,2},{1,3},{2,0},{3,1},{4,6},{5,7},{6,4},{7,5},{8,10},{9,11},{10,... | collective-permute-start | bytes 884744 | tf_op jit(solution)/shard_map/ppermute | solution.py:30
  47.9 0.2 collective-permute-done.15.refs_5_
  48.1 0.6 collective-permute-done.14.refs_2_
  48.7 2.1 %collective-permute-start.16 = (bf16[512,256]{1,0:T(8,128)(2,1)S(1)}, bf16[512,256]{1,0:T(8,128)(2,1)S(1)}, u32[]{:S(2)}, u32[]{:S(2)}) collective-permute-start(bf16[512,256]{1,0:T(8,128)(2,1)S(1)} %slice.28), channel_id=1, source_target_pairs={{0,8},{4,12},{8,24},{12,28},{16,0},{20,4},{24,16},{28,20},{1,9},{5... | collective-permute-start | bytes 786440 | tf_op jit(solution)/shard_map/ppermute | solution.py:45
  50.7 0.0 collective-permute-start.17
  50.8 2.8 %collective-permute-done.10.m2 = bf16[576,256]{1,0:T(8,128)(2,1)S(1)} collective-permute-done((bf16[576,256]{1,0:T(8,128)(2,1)S(1)}, bf16[576,256]{1,0:T(8,128)(2,1)S(1)}, u32[]{:S(2)}, u32[]{:S(2)}) %collective-permute-start.10) | collective-permute-done | bytes 294944 | tf_op jit(solution)/shard_map/ppermute | solution.py:30
  53.5 3.2 %collective-permute-done.16.refs_3_ = bf16[512,256]{1,0:T(8,128)(2,1)S(1)} collective-permute-done((bf16[512,256]{1,0:T(8,128)(2,1)S(1)}, bf16[512,256]{1,0:T(8,128)(2,1)S(1)}, u32[]{:S(2)}, u32[]{:S(2)}) %collective-permute-start.16) | collective-permute-done | bytes 262176 | tf_op jit(solution)/shard_map/ppermute | solution.py:45
  56.8 0.8 %collective-permute-done.17.refs_6_ = bf16[512,256]{1,0:T(8,128)(2,1)S(1)} collective-permute-done((bf16[512,256]{1,0:T(8,128)(2,1)S(1)}, bf16[512,256]{1,0:T(8,128)(2,1)S(1)}, u32[]{:S(2)}, u32[]{:S(2)}) %collective-permute-start.17) | collective-permute-done | bytes 262176 | tf_op jit(solution)/shard_map/ppermute | solution.py:30
  57.5 0.7 collective-permute-start.18
  58.2 2.0 %queries.1 = (bf16[4,12,128,256]{3,2,1,0:T(8,128)(2,1)S(1)}, bf16[256,768]{1,0:T(8,128)(2,1)S(1)}) custom-call(bf16[512,256]{1,0:T(8,128)(2,1)S(1)} %conv.1.f_ref.refs_0_, bf16[576,256]{1,0:T(8,128)(2,1)S(1)} %get-tuple-element.37.m0, bf16[576,256]{1,0:T(8,128)(2,1)S(1)} %collective-permute-done.9.m1, bf16[576,256]{1,0:T(8,128)(2,1)S(1)} %collective-permute-done.10.m2, ...), custom_call_target="tpu_custom_call" | custom-call | tf_op jit(solution)/shard_map/queries/pallas_call | solution.py:57
  60.2 3.7 %collective-permute-done.18.refs_7_ = bf16[512,256]{1,0:T(8,128)(2,1)S(1)} collective-permute-done((bf16[512,256]{1,0:T(8,128)(2,1)S(1)}, bf16[512,256]{1,0:T(8,128)(2,1)S(1)}, u32[]{:S(2)}, u32[]{:S(2)}) %collective-permute-start.18) | collective-permute-done | bytes 262176 | tf_op jit(solution)/shard_map/ppermute | solution.py:30
  63.9 8.9 %attend.1 = bf16[512,768]{1,0:T(8,128)(2,1)} custom-call(s32[8,128]{1,0:T(8,128)S(1)} %get-tuple-element.33.counts_ref, bf16[4,12,128,256]{3,2,1,0:T(8,128)(2,1)S(1)} %get-tuple-element.38.q_hbm, bf16[256,768]{1,0:T(8,128)(2,1)S(1)} %get-tuple-element.39.v_hbm, bf16[512,512]{1,0:T(8,128)(2,1)S(1)} %get-tuple-element.40.back_hbm, ...), custom_call_target="tpu_custom_call" | custom-call | tf_op jit(solution)/shard_map/attend/pallas_call | solution.py:57
  (26 shorter events, 0.2 us)
Async XLA Ops:
  0.0 3.9 %copy-start = (bf16[96,2304]{1,0:T(8,128)(2,1)S(1)}, bf16[96,2304]{1,0:T(8,128)(2,1)}, u32[]{:S(2)}) copy-start(bf16[96,2304]{1,0:T(8,128)(2,1)} %param.11) | copy-start | bytes 1327108
  0.0 33.0 %copy-start.2 = (bf16[256,768]{1,0:T(8,128)(2,1)S(1)}, bf16[256,768]{1,0:T(8,128)(2,1)}, u32[]{:S(2)}) copy-start(bf16[256,768]{1,0:T(8,128)(2,1)} %proj_hbm.1) | copy-start | bytes 1179652
  0.0 13.2 %collective-permute-start.5 = (bf16[576,256]{1,0:T(8,128)(2,1)}, bf16[576,256]{1,0:T(8,128)(2,1)S(1)}, u32[]{:S(2)}, u32[]{:S(2)}) collective-permute-start(bf16[576,256]{1,0:T(8,128)(2,1)} %w0.1), channel_id=1, source_target_pairs={{0,2},{1,3},{2,0},{3,1},{4,6},{5,7},{6,4},{7,5},{8,10},{9,11},{10,... | collective-permute-start | bytes 884744 | tf_op jit(solution)/shard_map/ppermute | solution.py:30
  4.1 6.5 %collective-permute-start = (bf16[96,640]{1,0:T(8,128)(2,1)S(1)}, bf16[96,640]{1,0:T(8,128)(2,1)S(1)}, u32[]{:S(2)}, u32[]{:S(2)}) collective-permute-start(bf16[96,640]{1,0:T(8,128)(2,1)S(1)} %pad_maximum_fusion.1.refs_0_), channel_id=1, source_target_pairs={{0,8},{4,12},{8,24},{12,28},{16,0},{20,4},{24,16},{28,20},{1,9},{5... | collective-permute-start | bytes 368648 | tf_op jit(solution)/shard_map/ppermute | solution.py:45
  5.7 17.9 %collective-permute-start.4 = (bf16[576,256]{1,0:T(8,128)(2,1)}, bf16[576,256]{1,0:T(8,128)(2,1)S(1)}, u32[]{:S(2)}, u32[]{:S(2)}) collective-permute-start(bf16[576,256]{1,0:T(8,128)(2,1)} %w0.1), channel_id=1, source_target_pairs={{0,1},{1,0},{2,3},{3,2},{4,5},{5,4},{6,7},{7,6},{8,9},{9,8},{10,11... | collective-permute-start | bytes 884744 | tf_op jit(solution)/shard_map/ppermute | solution.py:30
  5.7 1.2 %copy-start.3 = (bf16[32,64,256]{2,1,0:T(8,128)(2,1)S(1)}, bf16[32,64,256]{2,1,0:T(8,128)(2,1)}, u32[]{:S(2)}) copy-start(bf16[32,64,256]{2,1,0:T(8,128)(2,1)} %x_ref.1) | copy-start | bytes 3145732
  8.1 5.1 %collective-permute-start.7 = (bf16[32,256]{1,0:T(8,128)(2,1)S(1)}, bf16[32,256]{1,0:T(8,128)(2,1)S(1)}, u32[]{:S(2)}, u32[]{:S(2)}) collective-permute-start(bf16[32,256]{1,0:T(8,128)(2,1)S(1)} %get-tuple-element.36), channel_id=1, source_target_pairs={{0,1},{1,2},{2,3},{4,5},{5,6},{6,7},{8,9},{9,10},{10,11},{12,13},{... | collective-permute-start | bytes 49160 | tf_op jit(solution)/shard_map/ppermute | solution.py:34
  10.6 6.3 %collective-permute-start.1 = (bf16[96,640]{1,0:T(8,128)(2,1)S(1)}, bf16[96,640]{1,0:T(8,128)(2,1)S(1)}, u32[]{:S(2)}, u32[]{:S(2)}) collective-permute-start(bf16[96,640]{1,0:T(8,128)(2,1)S(1)} %collective-permute-done.refs_1_), channel_id=1, source_target_pairs={{0,8},{4,12},{8,24},{12,28},{16,0},{20,4},{24,16},{28,20},{1,9},{5... | collective-permute-start | bytes 368648 | tf_op jit(solution)/shard_map/ppermute | solution.py:45
  13.2 10.5 %collective-permute-start.6 = (bf16[576,256]{1,0:T(8,128)(2,1)S(1)}, bf16[576,256]{1,0:T(8,128)(2,1)S(1)}, u32[]{:S(2)}, u32[]{:S(2)}) collective-permute-start(bf16[576,256]{1,0:T(8,128)(2,1)S(1)} %collective-permute-done.5.w2), channel_id=1, source_target_pairs={{0,1},{1,0},{2,3},{3,2},{4,5},{5,4},{6,7},{7,6},{8,9},{9,8},{10,11... | collective-permute-start | bytes 884744 | tf_op jit(solution)/shard_map/ppermute | solution.py:30
  16.9 5.8 %collective-permute-start.2 = (bf16[96,640]{1,0:T(8,128)(2,1)S(1)}, bf16[96,640]{1,0:T(8,128)(2,1)S(1)}, u32[]{:S(2)}, u32[]{:S(2)}) collective-permute-start(bf16[96,640]{1,0:T(8,128)(2,1)S(1)} %collective-permute-done.1.refs_2_), channel_id=1, source_target_pairs={{0,8},{4,12},{8,24},{12,28},{16,0},{20,4},{24,16},{28,20},{1,9},{5... | collective-permute-start | bytes 368648 | tf_op jit(solution)/shard_map/ppermute | solution.py:45
  18.6 5.1 %collective-permute-start.8 = (bf16[80,256]{1,0:T(8,128)(2,1)S(1)}, bf16[80,256]{1,0:T(8,128)(2,1)S(1)}, u32[]{:S(2)}, u32[]{:S(2)}) collective-permute-start(bf16[80,256]{1,0:T(8,128)(2,1)S(1)} %pad_maximum_fusion.2), channel_id=1, source_target_pairs={{0,4},{4,8},{8,12},{12,16},{16,20},{20,24},{24,28},{1,5},{5,9},{9,... | collective-permute-start | bytes 122888 | tf_op jit(solution)/shard_map/ppermute | solution.py:34
  23.7 1.0 %copy-start.1 = (bf16[256,768]{1,0:T(8,128)(2,1)S(1)}, bf16[256,768]{1,0:T(8,128)(2,1)}, u32[]{:S(2)}) copy-start(bf16[256,768]{1,0:T(8,128)(2,1)} %proj_hbm.1) | copy-start | bytes 1179652
  24.7 1.0 %copy-start.4 = (bf16[576,256]{1,0:T(8,128)(2,1)S(1)}, bf16[576,256]{1,0:T(8,128)(2,1)}, u32[]{:S(2)}) copy-start(bf16[576,256]{1,0:T(8,128)(2,1)} %w0.1) | copy-start | bytes 884740
  25.6 0.7 copy-start.5
  29.3 7.8 %collective-permute-start.12 = (bf16[512,256]{1,0:T(8,128)(2,1)S(1)}, bf16[512,256]{1,0:T(8,128)(2,1)S(1)}, u32[]{:S(2)}, u32[]{:S(2)}) collective-permute-start(bf16[512,256]{1,0:T(8,128)(2,1)S(1)} %conv.1.f_ref.refs_0_), channel_id=1, source_target_pairs={{0,8},{4,12},{8,24},{12,28},{16,0},{20,4},{24,16},{28,20},{1,9},{5... | collective-permute-start | bytes 786440 | tf_op jit(solution)/shard_map/ppermute | solution.py:45
  32.4 6.8 %collective-permute-start.13 = (bf16[512,256]{1,0:T(8,128)(2,1)S(1)}, bf16[512,256]{1,0:T(8,128)(2,1)S(1)}, u32[]{:S(2)}, u32[]{:S(2)}) collective-permute-start(bf16[512,256]{1,0:T(8,128)(2,1)S(1)} %conv.1.f_ref.refs_0_), channel_id=1, source_target_pairs={{0,4},{4,0},{8,12},{12,8},{16,20},{20,16},{24,28},{28,24},{1,5},{5... | collective-permute-start | bytes 786440 | tf_op jit(solution)/shard_map/ppermute | solution.py:30
  39.2 9.4 %collective-permute-start.14 = (bf16[768,256]{1,0:T(8,128)(2,1)S(1)}, bf16[768,256]{1,0:T(8,128)(2,1)S(1)}, u32[]{:S(2)}, u32[]{:S(2)}) collective-permute-start(bf16[768,256]{1,0:T(8,128)(2,1)S(1)} %pad_maximum_fusion), channel_id=1, source_target_pairs={{0,8},{4,12},{8,24},{12,28},{16,0},{20,4},{24,16},{28,20},{1,9},{5... | collective-permute-start | bytes 1179656 | tf_op jit(solution)/shard_map/ppermute | solution.py:45
  39.6 7.1 %collective-permute-start.3 = (bf16[592,256]{1,0:T(8,128)(2,1)S(1)}, bf16[592,256]{1,0:T(8,128)(2,1)S(1)}, u32[]{:S(2)}, u32[]{:S(2)}) collective-permute-start(bf16[592,256]{1,0:T(8,128)(2,1)S(1)} %fusion.1), channel_id=1, source_target_pairs={{0,4},{4,0},{8,12},{12,8},{16,20},{20,16},{24,28},{28,24},{1,5},{5... | collective-permute-start | bytes 909320 | tf_op jit(solution)/shard_map/ppermute | solution.py:30
  40.1 7.9 %collective-permute-start.15 = (bf16[256,256]{1,0:T(8,128)(2,1)S(1)}, bf16[256,256]{1,0:T(8,128)(2,1)S(1)}, u32[]{:S(2)}, u32[]{:S(2)}) collective-permute-start(bf16[256,256]{1,0:T(8,128)(2,1)S(1)} %slice.27), channel_id=1, source_target_pairs={{0,4},{4,0},{8,12},{12,8},{16,20},{20,16},{24,28},{28,24},{1,5},{5... | collective-permute-start | bytes 393224 | tf_op jit(solution)/shard_map/ppermute | solution.py:30
  46.8 6.8 %collective-permute-start.10 = (bf16[576,256]{1,0:T(8,128)(2,1)S(1)}, bf16[576,256]{1,0:T(8,128)(2,1)S(1)}, u32[]{:S(2)}, u32[]{:S(2)}) collective-permute-start(bf16[576,256]{1,0:T(8,128)(2,1)S(1)} %get-tuple-element.37.m0), channel_id=1, source_target_pairs={{0,2},{1,3},{2,0},{3,1},{4,6},{5,7},{6,4},{7,5},{8,10},{9,11},{10,... | collective-permute-start | bytes 884744 | tf_op jit(solution)/shard_map/ppermute | solution.py:30
  48.7 8.1 %collective-permute-start.16 = (bf16[512,256]{1,0:T(8,128)(2,1)S(1)}, bf16[512,256]{1,0:T(8,128)(2,1)S(1)}, u32[]{:S(2)}, u32[]{:S(2)}) collective-permute-start(bf16[512,256]{1,0:T(8,128)(2,1)S(1)} %slice.28), channel_id=1, source_target_pairs={{0,8},{4,12},{8,24},{12,28},{16,0},{20,4},{24,16},{28,20},{1,9},{5... | collective-permute-start | bytes 786440 | tf_op jit(solution)/shard_map/ppermute | solution.py:45
  50.7 6.8 %collective-permute-start.17 = (bf16[512,256]{1,0:T(8,128)(2,1)S(1)}, bf16[512,256]{1,0:T(8,128)(2,1)S(1)}, u32[]{:S(2)}, u32[]{:S(2)}) collective-permute-start(bf16[512,256]{1,0:T(8,128)(2,1)S(1)} %slice.28), channel_id=1, source_target_pairs={{0,4},{4,0},{8,12},{12,8},{16,20},{20,16},{24,28},{28,24},{1,5},{5... | collective-permute-start | bytes 786440 | tf_op jit(solution)/shard_map/ppermute | solution.py:30
  50.7 7.4 %collective-permute-start.9 = (bf16[576,256]{1,0:T(8,128)(2,1)S(1)}, bf16[576,256]{1,0:T(8,128)(2,1)S(1)}, u32[]{:S(2)}, u32[]{:S(2)}) collective-permute-start(bf16[576,256]{1,0:T(8,128)(2,1)S(1)} %get-tuple-element.37.m0), channel_id=1, source_target_pairs={{0,1},{1,0},{2,3},{3,2},{4,5},{5,4},{6,7},{7,6},{8,9},{9,8},{10,11... | collective-permute-start | bytes 884744 | tf_op jit(solution)/shard_map/ppermute | solution.py:30
  53.5 4.6 %collective-permute-start.11 = (bf16[576,256]{1,0:T(8,128)(2,1)S(1)}, bf16[576,256]{1,0:T(8,128)(2,1)S(1)}, u32[]{:S(2)}, u32[]{:S(2)}) collective-permute-start(bf16[576,256]{1,0:T(8,128)(2,1)S(1)} %collective-permute-done.10.m2), channel_id=1, source_target_pairs={{0,1},{1,0},{2,3},{3,2},{4,5},{5,4},{6,7},{7,6},{8,9},{9,8},{10,11... | collective-permute-start | bytes 884744 | tf_op jit(solution)/shard_map/ppermute | solution.py:30
  57.5 6.4 %collective-permute-start.18 = (bf16[512,256]{1,0:T(8,128)(2,1)S(1)}, bf16[512,256]{1,0:T(8,128)(2,1)S(1)}, u32[]{:S(2)}, u32[]{:S(2)}) collective-permute-start(bf16[512,256]{1,0:T(8,128)(2,1)S(1)} %collective-permute-done.16.refs_3_), channel_id=1, source_target_pairs={{0,4},{4,0},{8,12},{12,8},{16,20},{20,16},{24,28},{28,24},{1,5},{5... | collective-permute-start | bytes 786440 | tf_op jit(solution)/shard_map/ppermute | solution.py:30

commit v4 on v3

--- a/solution.py
+++ b/solution.py
@@ -118,23 +118,19 @@
 
 
 def conv_kernel(
-    z_hbm, w0, w1, w2, w3, proj_hbm, sort_hbm, left_ref, up_ref, bias_ref,
-    out_ref, z_ref, weight, proj_ref, sort_ref, edge, sems,
+    z_ref, w0, w1, w2, w3, proj_ref, sort_ref, left_ref, up_ref, bias_ref,
+    out_ref, weight, edge, sems,
 ):
     out_rows, out_cols, wide = z_ref.shape[1:]
     channels = wide // 3
     tokens = out_rows * out_cols
     shard = w0.shape[0]
     mine = lax.axis_index("col")
-    copies = [pltpu.make_async_copy(z_hbm, z_ref, sems.at[4])]
+    copies = []
     for j, ref in enumerate((w0, w1, w2, w3)):
         spot = pl.multiple_of((mine ^ j) * shard, 64)
         copies.append(pltpu.make_async_copy(ref, weight.at[pl.ds(spot, shard)], sems.at[j]))
-    later = [
-        pltpu.make_async_copy(proj_hbm, proj_ref, sems.at[5]),
-        pltpu.make_async_copy(sort_hbm, sort_ref, sems.at[6]),
-    ]
-    for copy in copies + later:
+    for copy in copies:
         copy.start()
     in_rows = left_ref.shape[0]
     corner = up_ref[0:16].astype(F32)
@@ -166,8 +162,6 @@
     grid = grid + jnp.where(first, side[:, None, :], 0.0)
     pre = grid.reshape(tokens, channels) + bias_ref[...]
     features = jax.nn.gelu(pre).astype(BF16)
-    for copy in later:
-        copy.wait()
     projected = dot(features, proj_ref[...])
     centred = projected - jnp.mean(projected, axis=1, keepdims=True)
     spread = jnp.mean(centred * centred, axis=1, keepdims=True)
@@ -210,35 +204,41 @@
     shard = m0.shape[0]
     width = 4 * shard // 3
     heads = width // HD
-    blocks, _, bucket, _ = q_ref.shape
+    phases = q_ref.shape[0]
     mine = lax.axis_index("col")
     copies = []
     for j, ref in enumerate((m0, m1, m2, m3)):
         spot = pl.multiple_of((mine ^ j) * shard, 64)
         copies.append(pltpu.make_async_copy(ref, merged.at[pl.ds(spot, shard)], sems.at[j]))
         copies[-1].start()
+    f = f_ref[...].astype(F32).T.astype(BF16)
+    bucket = f.shape[1] // phases
     for copy in copies:
         copy.wait()
-    f = f_ref[...]
     factor = math.log2(math.e) / math.sqrt(HD)
-    lanes = lax.broadcasted_iota(jnp.int32, (1, 2 * HD), 1)
+    rows = lax.broadcasted_iota(jnp.int32, (2 * HD, 1), 0)
     for pair in range(heads // 2):
         both = slice(pair * 2 * HD, (pair + 1) * 2 * HD)
-        queries = dot(f, merged[both], NT).astype(BF16).astype(F32)
+        queries = dot(merged[both], f).astype(BF16).astype(F32)
         keys = merged[width + pair * 2 * HD : width + (pair + 1) * 2 * HD]
         for h in range(2):
-            one = jnp.where(lanes // HD == h, queries, 0.0).astype(BF16)
-            wide = (dot(one, keys) * factor).astype(BF16)
-            q_ref[:, 2 * pair + h] = wide.reshape(blocks, bucket, wide.shape[1])
-    v_ref[...] = merged[2 * width :].astype(F32).T.astype(BF16)
-
-
-def attend_kernel(spare, counts_ref, q_hbm, v_hbm, back_hbm, *refs):
+            one = jnp.where(rows // HD == h, queries, 0.0).astype(BF16)
+            wide = (dot(keys, one, TN) * factor).astype(BF16)
+            for p in range(phases):
+                q_ref[p, pair, :, h * bucket : (h + 1) * bucket] = wide[:, p * bucket : (p + 1) * bucket]
+    v_ref[...] = merged[2 * width :]
+
+
+def attend_kernel(spare, counts_ref, q_ref, v_ref, back_ref, *refs):
     around, across = refs[:4], refs[4:8]
-    out_ref, rows32, keys, keys_t, mixed, q_ref, v_ref, back_ref, sems = refs[8:]
-    phases, heads, bucket, channels = q_ref.shape
+    out_ref, rows32, keys, keys_t, mixed, good = refs[8:]
+    phases, parts, channels, rows = q_ref.shape
+    bucket = back_ref.shape[0] // phases
     tokens = phases * bucket
     group = SEGMENT * bucket
+    few = group // 2
+    pack = rows // bucket
+    halves = range(channels // LANES)
 
     def part_of(j, p):
         step, side = j // 2, j % 2
@@ -248,15 +248,6 @@
             return across[step], p * bucket
         return around[2], tokens + (2 * p - phases) * bucket // 2
 
-    halves = range(channels // LANES)
-    parts = 6
-    share = heads // parts
-    copies = [
-        pltpu.make_async_copy(a, b, sems.at[i])
-        for i, (a, b) in enumerate(((q_hbm, q_ref), (v_hbm, v_ref), (back_hbm, back_ref)))
-    ]
-    for copy in copies:
-        copy.start()
     fills = []
     for p in range(phases):
         filled = 0
@@ -268,50 +259,74 @@
                 ].astype(F32)
             filled = filled + counts_ref[j, spare + p]
         for c in halves:
-            rows32[p, c, pl.ds(filled, group // 2), :] = jnp.zeros((group // 2, LANES), F32)
+            rows32[p, c, pl.ds(filled, few), :] = jnp.zeros((few, LANES), F32)
         fills.append(filled)
     most = functools.reduce(jnp.maximum, fills)
-    for copy in copies:
-        copy.wait()
-    for width in (group // 2, group):
-
-        @pl.when((most > width - group // 2) & (most <= width))
-        def _():
-            for p in range(phases):
-                if width == group:
-
-                    @pl.when(fills[p] < group // 2)
-                    def _(p=p):
-                        for c in halves:
-                            rows32[p, c, group // 2 : group, :] = jnp.zeros((group // 2, LANES), F32)
-
-                for c in halves:
-                    some = rows32[p, c, 0:width, :]
-                    keys[p, 0:width, c * LANES : (c + 1) * LANES] = some.astype(BF16)
-                    keys_t[p, c * LANES : (c + 1) * LANES, 0:width] = some.T.astype(BF16)
-                bias = jnp.where(
-                    lax.broadcasted_iota(jnp.int32, (1, width), 1) < fills[p], 0.0, -1e30
-                )
-                for part in range(parts):
-                    few = slice(part * share, (part + 1) * share)
-                    q = q_ref[p, few].reshape(share * bucket, channels)
-                    scores = dot(q, keys_t[p, :, 0:width]) + bias
-                    weights = jnp.exp2(scores - jnp.max(scores, axis=1, keepdims=True))
-                    total = jnp.sum(weights, axis=1, keepdims=True)
-                    mix = dot(weights.astype(BF16), keys[p, 0:width, :]) * (1.0 / total)
-                    mixed[p, few] = mix.astype(BF16).reshape(share, bucket, channels)
+
+    def arrange(p, width):
+        for c in halves:
+            some = rows32[p, c, 0:width, :]
+            keys[p, 0:width, c * LANES : (c + 1) * LANES] = some.astype(BF16)
+            keys_t[p, c * LANES : (c + 1) * LANES, 0:width] = some.T.astype(BF16)
+
+    def one_part(p, part, width, limit, shift):
+        place = lax.broadcasted_iota(jnp.int32, (width, rows), 0)
+        scores = dot(keys[p, 0:width, :], q_ref[p, part]) + jnp.where(place < limit, 0.0, -1e30)
+        if shift:
+            scores = scores - jnp.max(scores, axis=0, keepdims=True)
+        weights = jnp.exp2(scores)
+        total = jnp.sum(weights, axis=0, keepdims=True)
+        mix = (dot(keys_t[p, :, 0:width], weights.astype(BF16)) * (1.0 / total)).astype(BF16)
+        for h in range(pack):
+            mixed[p, part * pack + h] = mix[:, h * bucket : (h + 1) * bucket]
+        return total
+
+    good[0] = 0
+
+    @pl.when(most <= few)
+    def _():
+        least = greatest = None
+        for p in range(phases):
+            arrange(p, few)
+            for part in range(parts):
+                total = one_part(p, part, few, fills[p], False)
+                least = total if least is None else jnp.minimum(least, total)
+                greatest = total if greatest is None else jnp.maximum(greatest, total)
+        inside = jnp.where((least >= 2.0**-60) & (greatest <= 2.0**100), 1.0, 0.0)
+        good[0] = jnp.min(inside).astype(jnp.int32)
+
+    @pl.when(good[0] == 0)
+    def _():
+        def again(i, carry):
+            p, part = i // parts, lax.rem(i, parts)
+            limit = fills[0]
+            for k in range(1, phases):
+                limit = jnp.where(p == k, fills[k], limit)
+
+            @pl.when(part == 0)
+            def _():
+                @pl.when(limit < few)
+                def _():
+                    for c in halves:
+                        rows32[p, c, few:group, :] = jnp.zeros((group - few, LANES), F32)
+
+                arrange(p, group)
+
+            one_part(p, part, group, limit, True)
+            return carry
+
+        lax.fori_loop(0, phases * parts, again, 0)
 
     outs = []
-    lane = lax.broadcasted_iota(jnp.int32, (1, LANES), 1)
-    for pair in range(heads // 2):
-        some = v_ref[:, pair * LANES : (pair + 1) * LANES]
-        a = dot(mixed[:, 2 * pair].reshape(tokens, channels), some)
-        b = dot(mixed[:, 2 * pair + 1].reshape(tokens, channels), some)
-        outs.append(jnp.where(lane < HD, a, b))
-    spot = lax.broadcasted_iota(jnp.int32, (bucket, 1), 0)
-    live = jnp.concatenate([spot < counts_ref[0, spare + p] for p in range(phases)], axis=0)
-    ordered = jnp.where(live, jnp.concatenate(outs, axis=1), 0.0).astype(BF16)
-    out_ref[...] = dot(back_ref[...], ordered).astype(BF16)
+    for h in range(parts * pack):
+        side = jnp.concatenate([mixed[p, h] for p in range(phases)], axis=1)
+        outs.append(dot(v_ref[h * HD : (h + 1) * HD], side))
+    spot = lax.broadcasted_iota(jnp.int32, (1, bucket), 1)
+    live = jnp.concatenate(
+        [jnp.where(spot < counts_ref[0, spare + p], 1.0, 0.0) for p in range(phases)], axis=1
+    )
+    ordered = jnp.where(live > 0.5, jnp.concatenate(outs, axis=0), 0.0).astype(BF16)
+    out_ref[...] = dot(back_ref[...], ordered, NT).astype(BF16)
 
 
 def local(feat_in, conv_weight, conv_bias, proj_weight, qkv_weight, tissue, phase):
@@ -378,15 +393,12 @@
     mine = call(
         conv_kernel,
         jax.ShapeDtypeStruct((tokens, channels), BF16),
-        [ANY] * 7 + [VMEM] * 3,
+        [VMEM] + [ANY] * 4 + [VMEM] * 5,
         VMEM,
         [
-            VMEM(z.shape, BF16),
             VMEM((9 * channels, channels), BF16),
-            VMEM(proj_weight.shape, BF16),
-            VMEM((tokens, tokens), BF16),
             VMEM((2, channels // LANES, in_cols + 8, LANES), F32),
-            pltpu.SemaphoreType.DMA((7,)),
+            pltpu.SemaphoreType.DMA((4,)),
         ],
         (
             z, conv_weight, weight_core, weight_x, weight_far, proj_weight, sort, left, up,
@@ -443,8 +455,8 @@
     queries, values = call(
         query_kernel,
         (
-            jax.ShapeDtypeStruct((PHASES, heads, bucket, channels), BF16),
-            jax.ShapeDtypeStruct((channels, width), BF16),
+            jax.ShapeDtypeStruct((PHASES, heads // 2, channels, 2 * bucket), BF16),
+            jax.ShapeDtypeStruct((width, channels), BF16),
         ),
         [VMEM, ANY, ANY, ANY, ANY],
         (VMEM, VMEM),
@@ -457,17 +469,14 @@
     attended = call(
         functools.partial(attend_kernel, spare),
         jax.ShapeDtypeStruct((tokens, width), BF16),
-        [pltpu.SMEM, ANY, ANY, ANY] + [VMEM] * SEGMENT,
+        [pltpu.SMEM] + [VMEM] * (3 + SEGMENT),
         VMEM,
         [
             VMEM((PHASES, channels // LANES, group + group // 2, LANES), F32),
             VMEM((PHASES, group, channels), BF16),
             VMEM((PHASES, channels, group), BF16),
-            VMEM(queries.shape, BF16),
-            VMEM(queries.shape, BF16),
-            VMEM(values.shape, BF16),
-            VMEM((tokens, tokens), BF16),
-            pltpu.SemaphoreType.DMA((3,)),
+            VMEM((PHASES, heads, channels, bucket), BF16),
+            pltpu.SMEM((1,), jnp.int32),
         ],
         (counts, queries, values, back, *around, *across),
         "attend",

time: 74.2 us -> 95.2 us (1.28)
  Pallas kernels: 16.1 us -> 37.6 us
    pallas_call x6, Pallas kernels: 16.1 us -> 37.6 us  [call(): pl.pallas_call(kernel, out_shape=out_shape, in_specs=[pl.BlockSpec(memory...]
  transfers between devices with their start and end apart: 19 -> 19, of which waited for: 12 -> 12; matrix products, arithmetic and copies ran while one was open for 2% -> 1% of each run, Pallas kernels for 6% -> 5%
where the time goes in v4:
time: 95.2 us; the launch traced here: 94 us
  Pallas kernels  37.6 us (39%)
  waiting for transfers between devices  26.2 us (28%)
  starting transfers between devices  24.8 us (26%)
  local copies, waits for them, and re-layouts  4.21 us (4%)
  other arithmetic  1.1 us (1%)
    pallas_call x6, Pallas kernels, call(): pl.pallas_call(kernel, out_shape=out_shape, in_specs=[pl.BlockSpec(memory...  37.6 us
    ppermute x11, waiting for transfers between devices, flip(): lax.ppermute(array, axis, [(i, i ^ bits) for i in range(lax.axis_size(axi...  14.2 us
    ppermute x6, starting transfers between devices, ring(): return lax.ppermute(array, 'row', pairs)  11.4 us
    ppermute x6, waiting for transfers between devices, ring(): return lax.ppermute(array, 'row', pairs)  11 us
    ppermute x11, starting transfers between devices, flip(): lax.ppermute(array, axis, [(i, i ^ bits) for i in range(lax.axis_size(axi...  7.54 us
    ppermute x2, starting transfers between devices, shifted(): lax.ppermute(array, axis, [(i, i + 1) for i in range(lax.axis_size(axis)...  5.83 us
    unnamed x13, local copies, waits for them, and re-layouts  4.04 us
  transfers between devices with their start and end apart: 19, of which 12 were waited for; matrix products, arithmetic and copies ran while one was open for 1% of the time, Pallas kernels for 5%

profile of v4, /device:TPU:0, one launch (start us, length us, event | category | flops | bytes accessed | tf_op | source)
XLA Modules:
  0.0 94.0 jit_solution(2659703309758468193)
XLA Ops:
  0.0 2.9 %collective-permute-start.5 = (bf16[576,256]{1,0:T(8,128)(2,1)}, bf16[576,256]{1,0:T(8,128)(2,1)S(1)}, u32[]{:S(2)}, u32[]{:S(2)}) collective-permute-start(bf16[576,256]{1,0:T(8,128)(2,1)} %w0.1), channel_id=1, source_target_pairs={{0,2},{1,3},{2,0},{3,1},{4,6},{5,7},{6,4},{7,5},{8,10},{9,11},{10,... | collective-permute-start | bytes 884744 | tf_op jit(solution)/shard_map/ppermute | solution.py:30
  3.0 0.7 subtract_convert_fusion.label_ref
  3.7 0.2 convert_reduce_fusion
  3.9 0.1 fusion.2
  3.9 0.1 constant_dynamic-slice_fusion
  4.1 1.6 %collective-permute-start = (bf16[96,640]{1,0:T(8,128)(2,1)S(1)}, bf16[96,640]{1,0:T(8,128)(2,1)S(1)}, u32[]{:S(2)}, u32[]{:S(2)}) collective-permute-start(bf16[96,640]{1,0:T(8,128)(2,1)S(1)} %pad_maximum_fusion.1.refs_0_), channel_id=1, source_target_pairs={{0,8},{4,12},{8,24},{12,28},{16,0},{20,4},{24,16},{28,20},{1,9},{5... | collective-permute-start | bytes 368648 | tf_op jit(solution)/shard_map/ppermute | solution.py:45
  5.7 0.0 collective-permute-start.4
  5.7 1.2 %copy-done.3 = bf16[32,64,256]{2,1,0:T(8,128)(2,1)S(1)} copy-done((bf16[32,64,256]{2,1,0:T(8,128)(2,1)S(1)}, bf16[32,64,256]{2,1,0:T(8,128)(2,1)}, u32[]{:S(2)}) %copy-start.3) | copy-done | bytes 1048600
  6.9 1.2 %prepare.1 = (bf16[32,256]{1,0:T(8,128)(2,1)S(1)}, bf16[2,16,32,768]{3,2,1,0:T(8,128)(2,1)S(1)}, bf16[512,512]{1,0:T(8,128)(2,1)S(1)}, bf16[512,512]{1,0:T(8,128)(2,1)S(1)}) custom-call(bf16[32,64,256]{2,1,0:T(8,128)(2,1)S(1)} %copy-done.3, f32[16,32]{1,0:T(8,128)S(1)} %subtract_convert_fusion.label_ref), custom_call_target="tpu_custom_call" | custom-call | tf_op jit(solution)/shard_map/prepare/pallas_call | solution.py:57
  8.1 2.4 %collective-permute-start.7 = (bf16[32,256]{1,0:T(8,128)(2,1)S(1)}, bf16[32,256]{1,0:T(8,128)(2,1)S(1)}, u32[]{:S(2)}, u32[]{:S(2)}) collective-permute-start(bf16[32,256]{1,0:T(8,128)(2,1)S(1)} %get-tuple-element.36), channel_id=1, source_target_pairs={{0,1},{1,2},{2,3},{4,5},{5,6},{6,7},{8,9},{9,10},{10,11},{12,13},{... | collective-permute-start | bytes 49160 | tf_op jit(solution)/shard_map/ppermute | solution.py:34
  10.6 2.6 %collective-permute-start.1 = (bf16[96,640]{1,0:T(8,128)(2,1)S(1)}, bf16[96,640]{1,0:T(8,128)(2,1)S(1)}, u32[]{:S(2)}, u32[]{:S(2)}) collective-permute-start(bf16[96,640]{1,0:T(8,128)(2,1)S(1)} %collective-permute-done.refs_1_), channel_id=1, source_target_pairs={{0,8},{4,12},{8,24},{12,28},{16,0},{20,4},{24,16},{28,20},{1,9},{5... | collective-permute-start | bytes 368648 | tf_op jit(solution)/shard_map/ppermute | solution.py:45
  13.2 0.0 collective-permute-done.5.w2
  13.2 0.0 collective-permute-start.6
  13.2 0.0 collective-permute-done.7.left_ref
  13.2 3.6 %collective-permute-done.1.refs_2_ = bf16[96,640]{1,0:T(8,128)(2,1)S(1)} collective-permute-done((bf16[96,640]{1,0:T(8,128)(2,1)S(1)}, bf16[96,640]{1,0:T(8,128)(2,1)S(1)}, u32[]{:S(2)}, u32[]{:S(2)}) %collective-permute-start.1) | collective-permute-done | bytes 122912 | tf_op jit(solution)/shard_map/ppermute | solution.py:45
  16.9 1.7 %collective-permute-start.2 = (bf16[96,640]{1,0:T(8,128)(2,1)S(1)}, bf16[96,640]{1,0:T(8,128)(2,1)S(1)}, u32[]{:S(2)}, u32[]{:S(2)}) collective-permute-start(bf16[96,640]{1,0:T(8,128)(2,1)S(1)} %collective-permute-done.1.refs_2_), channel_id=1, source_target_pairs={{0,8},{4,12},{8,24},{12,28},{16,0},{20,4},{24,16},{28,20},{1,9},{5... | collective-permute-start | bytes 368648 | tf_op jit(solution)/shard_map/ppermute | solution.py:45
  18.6 3.4 %collective-permute-start.8 = (bf16[80,256]{1,0:T(8,128)(2,1)S(1)}, bf16[80,256]{1,0:T(8,128)(2,1)S(1)}, u32[]{:S(2)}, u32[]{:S(2)}) collective-permute-start(bf16[80,256]{1,0:T(8,128)(2,1)S(1)} %pad_maximum_fusion.2), channel_id=1, source_target_pairs={{0,4},{4,8},{8,12},{12,16},{16,20},{20,24},{24,28},{1,5},{5,9},{9,... | collective-permute-start | bytes 122888 | tf_op jit(solution)/shard_map/ppermute | solution.py:34
  22.0 0.7 collective-permute-done.2.refs_3_
  22.7 1.0 %collective-permute-done.8.up_ref = bf16[80,256]{1,0:T(8,128)(2,1)S(1)} collective-permute-done((bf16[80,256]{1,0:T(8,128)(2,1)S(1)}, bf16[80,256]{1,0:T(8,128)(2,1)S(1)}, u32[]{:S(2)}, u32[]{:S(2)}) %collective-permute-start.8) | collective-permute-done | bytes 40992 | tf_op jit(solution)/shard_map/ppermute | solution.py:34
  23.7 1.0 %copy-done.1 = bf16[256,768]{1,0:T(8,128)(2,1)S(1)} copy-done((bf16[256,768]{1,0:T(8,128)(2,1)S(1)}, bf16[256,768]{1,0:T(8,128)(2,1)}, u32[]{:S(2)}) %copy-start.1) | copy-done | bytes 393240
  24.7 1.0 %copy-done.4 = bf16[576,256]{1,0:T(8,128)(2,1)S(1)} copy-done((bf16[576,256]{1,0:T(8,128)(2,1)S(1)}, bf16[576,256]{1,0:T(8,128)(2,1)}, u32[]{:S(2)}) %copy-start.4) | copy-done | bytes 294936
  25.6 0.7 copy-done.5
  26.3 2.6 %conv.1.f_ref.refs_0_ = bf16[512,256]{1,0:T(8,128)(2,1)S(1)} custom-call(bf16[2,16,32,768]{3,2,1,0:T(8,128)(2,1)S(1)} %get-tuple-element.34.z_ref, bf16[576,256]{1,0:T(8,128)(2,1)S(1)} %copy-done.4, bf16[576,256]{1,0:T(8,128)(2,1)S(1)} %collective-permute-done.4.w1, bf16[576,256]{1,0:T(8,128)(2,1)S(1)} %collective-permute-done.5.w2, ...), custom_call_target="tpu_custom_call" | custom-call | tf_op jit(solution)/shard_map/conv/pallas_call | solution.py:57
  28.9 3.1 %collective-permute-start.12 = (bf16[512,256]{1,0:T(8,128)(2,1)S(1)}, bf16[512,256]{1,0:T(8,128)(2,1)S(1)}, u32[]{:S(2)}, u32[]{:S(2)}) collective-permute-start(bf16[512,256]{1,0:T(8,128)(2,1)S(1)} %conv.1.f_ref.refs_0_), channel_id=1, source_target_pairs={{0,8},{4,12},{8,24},{12,28},{16,0},{20,4},{24,16},{28,20},{1,9},{5... | collective-permute-start | bytes 786440 | tf_op jit(solution)/shard_map/ppermute | solution.py:45
  32.0 0.6 collective-permute-start.13
  32.6 0.2 copy.9
  32.8 1.0 %merge.1 = (f32[576,256]{1,0:T(8,128)S(1)}, bf16[16,128]{1,0:T(8,128)(2,1)S(1)}) custom-call(bf16[96,640]{1,0:T(8,128)(2,1)S(1)} %pad_maximum_fusion.1.refs_0_, bf16[96,640]{1,0:T(8,128)(2,1)S(1)} %collective-permute-done.refs_1_, bf16[96,640]{1,0:T(8,128)(2,1)S(1)} %collective-permute-done.1.refs_2_, bf16[96,640]{1,0:T(8,128)(2,1)S(1)} %collective-permute-done.2.refs_3_, ...), custom_call_target="tpu_custom_call" | custom-call | tf_op jit(solution)/shard_map/merge/pallas_call | solution.py:57
  33.8 2.9 %collective-permute-done.12.refs_1_ = bf16[512,256]{1,0:T(8,128)(2,1)S(1)} collective-permute-done((bf16[512,256]{1,0:T(8,128)(2,1)S(1)}, bf16[512,256]{1,0:T(8,128)(2,1)S(1)}, u32[]{:S(2)}, u32[]{:S(2)}) %collective-permute-start.12) | collective-permute-done | bytes 262176 | tf_op jit(solution)/shard_map/ppermute | solution.py:45
  36.7 2.1 %collective-permute-done.13.refs_4_ = bf16[512,256]{1,0:T(8,128)(2,1)S(1)} collective-permute-done((bf16[512,256]{1,0:T(8,128)(2,1)S(1)}, bf16[512,256]{1,0:T(8,128)(2,1)S(1)}, u32[]{:S(2)}, u32[]{:S(2)}) %collective-permute-start.13) | collective-permute-done | bytes 262176 | tf_op jit(solution)/shard_map/ppermute | solution.py:30
  38.9 0.3 collective-permute-start.14
  39.2 0.6 collective-permute-start.3
  39.7 1.6 %collective-permute-start.15 = (bf16[256,256]{1,0:T(8,128)(2,1)S(1)}, bf16[256,256]{1,0:T(8,128)(2,1)S(1)}, u32[]{:S(2)}, u32[]{:S(2)}) collective-permute-start(bf16[256,256]{1,0:T(8,128)(2,1)S(1)} %slice.27), channel_id=1, source_target_pairs={{0,4},{4,0},{8,12},{12,8},{16,20},{20,16},{24,28},{28,24},{1,5},{5... | collective-permute-start | bytes 393224 | tf_op jit(solution)/shard_map/ppermute | solution.py:30
  41.3 4.9 %collective-permute-done.3 = bf16[592,256]{1,0:T(8,128)(2,1)S(1)} collective-permute-done((bf16[592,256]{1,0:T(8,128)(2,1)S(1)}, bf16[592,256]{1,0:T(8,128)(2,1)S(1)}, u32[]{:S(2)}, u32[]{:S(2)}) %collective-permute-start.3) | collective-permute-done | bytes 303136 | tf_op jit(solution)/shard_map/ppermute | solution.py:30
  46.3 0.1 join.1
  46.4 1.1 %collective-permute-start.10 = (bf16[576,256]{1,0:T(8,128)(2,1)S(1)}, bf16[576,256]{1,0:T(8,128)(2,1)S(1)}, u32[]{:S(2)}, u32[]{:S(2)}) collective-permute-start(bf16[576,256]{1,0:T(8,128)(2,1)S(1)} %get-tuple-element.37.m0), channel_id=1, source_target_pairs={{0,2},{1,3},{2,0},{3,1},{4,6},{5,7},{6,4},{7,5},{8,10},{9,11},{10,... | collective-permute-start | bytes 884744 | tf_op jit(solution)/shard_map/ppermute | solution.py:30
  47.5 0.2 collective-permute-done.15.refs_5_
  47.7 0.6 collective-permute-done.14.refs_2_
  48.3 2.1 %collective-permute-start.16 = (bf16[512,256]{1,0:T(8,128)(2,1)S(1)}, bf16[512,256]{1,0:T(8,128)(2,1)S(1)}, u32[]{:S(2)}, u32[]{:S(2)}) collective-permute-start(bf16[512,256]{1,0:T(8,128)(2,1)S(1)} %slice.28), channel_id=1, source_target_pairs={{0,8},{4,12},{8,24},{12,28},{16,0},{20,4},{24,16},{28,20},{1,9},{5... | collective-permute-start | bytes 786440 | tf_op jit(solution)/shard_map/ppermute | solution.py:45
  50.4 0.0 collective-permute-start.17
  50.4 0.0 collective-permute-start.9
  50.4 2.8 %collective-permute-done.10.m2 = bf16[576,256]{1,0:T(8,128)(2,1)S(1)} collective-permute-done((bf16[576,256]{1,0:T(8,128)(2,1)S(1)}, bf16[576,256]{1,0:T(8,128)(2,1)S(1)}, u32[]{:S(2)}, u32[]{:S(2)}) %collective-permute-start.10) | collective-permute-done | bytes 294944 | tf_op jit(solution)/shard_map/ppermute | solution.py:30
  53.2 3.2 %collective-permute-done.16.refs_3_ = bf16[512,256]{1,0:T(8,128)(2,1)S(1)} collective-permute-done((bf16[512,256]{1,0:T(8,128)(2,1)S(1)}, bf16[512,256]{1,0:T(8,128)(2,1)S(1)}, u32[]{:S(2)}, u32[]{:S(2)}) %collective-permute-start.16) | collective-permute-done | bytes 262176 | tf_op jit(solution)/shard_map/ppermute | solution.py:45
  56.4 0.8 collective-permute-done.17.refs_6_
  57.1 0.7 collective-permute-start.18
  57.8 0.0 collective-permute-done.11.m3
  57.8 2.3 %queries.1 = (bf16[4,6,256,256]{3,2,1,0:T(8,128)(2,1)S(1)}, bf16[768,256]{1,0:T(8,128)(2,1)S(1)}) custom-call(bf16[512,256]{1,0:T(8,128)(2,1)S(1)} %conv.1.f_ref.refs_0_, bf16[576,256]{1,0:T(8,128)(2,1)S(1)} %get-tuple-element.37.m0, bf16[576,256]{1,0:T(8,128)(2,1)S(1)} %collective-permute-done.9.m1, bf16[576,256]{1,0:T(8,128)(2,1)S(1)} %collective-permute-done.10.m2, ...), custom_call_target="tpu_custom_call" | custom-call | tf_op jit(solution)/shard_map/queries/pallas_call | solution.py:57
  60.1 3.4 %collective-permute-done.18.refs_7_ = bf16[512,256]{1,0:T(8,128)(2,1)S(1)} collective-permute-done((bf16[512,256]{1,0:T(8,128)(2,1)S(1)}, bf16[512,256]{1,0:T(8,128)(2,1)S(1)}, u32[]{:S(2)}, u32[]{:S(2)}) %collective-permute-start.18) | collective-permute-done | bytes 262176 | tf_op jit(solution)/shard_map/ppermute | solution.py:30
  63.5 30.5 %attend.1 = bf16[512,768]{1,0:T(8,128)(2,1)} custom-call(s32[8,128]{1,0:T(8,128)S(1)} %get-tuple-element.33.counts_ref, bf16[4,6,256,256]{3,2,1,0:T(8,128)(2,1)S(1)} %get-tuple-element.38.q_ref, bf16[768,256]{1,0:T(8,128)(2,1)S(1)} %get-tuple-element.39.v_ref, bf16[512,512]{1,0:T(8,128)(2,1)S(1)} %get-tuple-element.40.back_ref, ...), custom_call_target="tpu_custom_call" | custom-call | tf_op jit(solution)/shard_map/attend/pallas_call | solution.py:57
  (26 shorter events, 0.2 us)
Async XLA Ops:
  0.0 3.9 %copy-start = (bf16[96,2304]{1,0:T(8,128)(2,1)S(1)}, bf16[96,2304]{1,0:T(8,128)(2,1)}, u32[]{:S(2)}) copy-start(bf16[96,2304]{1,0:T(8,128)(2,1)} %param.11) | copy-start | bytes 1327108
  0.0 32.6 %copy-start.2 = (bf16[256,768]{1,0:T(8,128)(2,1)S(1)}, bf16[256,768]{1,0:T(8,128)(2,1)}, u32[]{:S(2)}) copy-start(bf16[256,768]{1,0:T(8,128)(2,1)} %proj_ref.1) | copy-start | bytes 1179652
  0.0 13.2 %collective-permute-start.5 = (bf16[576,256]{1,0:T(8,128)(2,1)}, bf16[576,256]{1,0:T(8,128)(2,1)S(1)}, u32[]{:S(2)}, u32[]{:S(2)}) collective-permute-start(bf16[576,256]{1,0:T(8,128)(2,1)} %w0.1), channel_id=1, source_target_pairs={{0,2},{1,3},{2,0},{3,1},{4,6},{5,7},{6,4},{7,5},{8,10},{9,11},{10,... | collective-permute-start | bytes 884744 | tf_op jit(solution)/shard_map/ppermute | solution.py:30
  4.1 6.5 %collective-permute-start = (bf16[96,640]{1,0:T(8,128)(2,1)S(1)}, bf16[96,640]{1,0:T(8,128)(2,1)S(1)}, u32[]{:S(2)}, u32[]{:S(2)}) collective-permute-start(bf16[96,640]{1,0:T(8,128)(2,1)S(1)} %pad_maximum_fusion.1.refs_0_), channel_id=1, source_target_pairs={{0,8},{4,12},{8,24},{12,28},{16,0},{20,4},{24,16},{28,20},{1,9},{5... | collective-permute-start | bytes 368648 | tf_op jit(solution)/shard_map/ppermute | solution.py:45
  5.7 17.9 %collective-permute-start.4 = (bf16[576,256]{1,0:T(8,128)(2,1)}, bf16[576,256]{1,0:T(8,128)(2,1)S(1)}, u32[]{:S(2)}, u32[]{:S(2)}) collective-permute-start(bf16[576,256]{1,0:T(8,128)(2,1)} %w0.1), channel_id=1, source_target_pairs={{0,1},{1,0},{2,3},{3,2},{4,5},{5,4},{6,7},{7,6},{8,9},{9,8},{10,11... | collective-permute-start | bytes 884744 | tf_op jit(solution)/shard_map/ppermute | solution.py:30
  5.7 1.2 %copy-start.3 = (bf16[32,64,256]{2,1,0:T(8,128)(2,1)S(1)}, bf16[32,64,256]{2,1,0:T(8,128)(2,1)}, u32[]{:S(2)}) copy-start(bf16[32,64,256]{2,1,0:T(8,128)(2,1)} %x_ref.1) | copy-start | bytes 3145732
  8.1 5.1 %collective-permute-start.7 = (bf16[32,256]{1,0:T(8,128)(2,1)S(1)}, bf16[32,256]{1,0:T(8,128)(2,1)S(1)}, u32[]{:S(2)}, u32[]{:S(2)}) collective-permute-start(bf16[32,256]{1,0:T(8,128)(2,1)S(1)} %get-tuple-element.36), channel_id=1, source_target_pairs={{0,1},{1,2},{2,3},{4,5},{5,6},{6,7},{8,9},{9,10},{10,11},{12,13},{... | collective-permute-start | bytes 49160 | tf_op jit(solution)/shard_map/ppermute | solution.py:34
  10.6 6.3 %collective-permute-start.1 = (bf16[96,640]{1,0:T(8,128)(2,1)S(1)}, bf16[96,640]{1,0:T(8,128)(2,1)S(1)}, u32[]{:S(2)}, u32[]{:S(2)}) collective-permute-start(bf16[96,640]{1,0:T(8,128)(2,1)S(1)} %collective-permute-done.refs_1_), channel_id=1, source_target_pairs={{0,8},{4,12},{8,24},{12,28},{16,0},{20,4},{24,16},{28,20},{1,9},{5... | collective-permute-start | bytes 368648 | tf_op jit(solution)/shard_map/ppermute | solution.py:45
  13.2 10.5 %collective-permute-start.6 = (bf16[576,256]{1,0:T(8,128)(2,1)S(1)}, bf16[576,256]{1,0:T(8,128)(2,1)S(1)}, u32[]{:S(2)}, u32[]{:S(2)}) collective-permute-start(bf16[576,256]{1,0:T(8,128)(2,1)S(1)} %collective-permute-done.5.w2), channel_id=1, source_target_pairs={{0,1},{1,0},{2,3},{3,2},{4,5},{5,4},{6,7},{7,6},{8,9},{9,8},{10,11... | collective-permute-start | bytes 884744 | tf_op jit(solution)/shard_map/ppermute | solution.py:30
  16.9 5.8 %collective-permute-start.2 = (bf16[96,640]{1,0:T(8,128)(2,1)S(1)}, bf16[96,640]{1,0:T(8,128)(2,1)S(1)}, u32[]{:S(2)}, u32[]{:S(2)}) collective-permute-start(bf16[96,640]{1,0:T(8,128)(2,1)S(1)} %collective-permute-done.1.refs_2_), channel_id=1, source_target_pairs={{0,8},{4,12},{8,24},{12,28},{16,0},{20,4},{24,16},{28,20},{1,9},{5... | collective-permute-start | bytes 368648 | tf_op jit(solution)/shard_map/ppermute | solution.py:45
  18.6 5.1 %collective-permute-start.8 = (bf16[80,256]{1,0:T(8,128)(2,1)S(1)}, bf16[80,256]{1,0:T(8,128)(2,1)S(1)}, u32[]{:S(2)}, u32[]{:S(2)}) collective-permute-start(bf16[80,256]{1,0:T(8,128)(2,1)S(1)} %pad_maximum_fusion.2), channel_id=1, source_target_pairs={{0,4},{4,8},{8,12},{12,16},{16,20},{20,24},{24,28},{1,5},{5,9},{9,... | collective-permute-start | bytes 122888 | tf_op jit(solution)/shard_map/ppermute | solution.py:34
  23.7 1.0 %copy-start.1 = (bf16[256,768]{1,0:T(8,128)(2,1)S(1)}, bf16[256,768]{1,0:T(8,128)(2,1)}, u32[]{:S(2)}) copy-start(bf16[256,768]{1,0:T(8,128)(2,1)} %proj_ref.1) | copy-start | bytes 1179652
  24.7 1.0 %copy-start.4 = (bf16[576,256]{1,0:T(8,128)(2,1)S(1)}, bf16[576,256]{1,0:T(8,128)(2,1)}, u32[]{:S(2)}) copy-start(bf16[576,256]{1,0:T(8,128)(2,1)} %w0.1) | copy-start | bytes 884740
  25.6 0.7 copy-start.5
  28.9 7.8 %collective-permute-start.12 = (bf16[512,256]{1,0:T(8,128)(2,1)S(1)}, bf16[512,256]{1,0:T(8,128)(2,1)S(1)}, u32[]{:S(2)}, u32[]{:S(2)}) collective-permute-start(bf16[512,256]{1,0:T(8,128)(2,1)S(1)} %conv.1.f_ref.refs_0_), channel_id=1, source_target_pairs={{0,8},{4,12},{8,24},{12,28},{16,0},{20,4},{24,16},{28,20},{1,9},{5... | collective-permute-start | bytes 786440 | tf_op jit(solution)/shard_map/ppermute | solution.py:45
  32.0 6.8 %collective-permute-start.13 = (bf16[512,256]{1,0:T(8,128)(2,1)S(1)}, bf16[512,256]{1,0:T(8,128)(2,1)S(1)}, u32[]{:S(2)}, u32[]{:S(2)}) collective-permute-start(bf16[512,256]{1,0:T(8,128)(2,1)S(1)} %conv.1.f_ref.refs_0_), channel_id=1, source_target_pairs={{0,4},{4,0},{8,12},{12,8},{16,20},{20,16},{24,28},{28,24},{1,5},{5... | collective-permute-start | bytes 786440 | tf_op jit(solution)/shard_map/ppermute | solution.py:30
  38.9 9.4 %collective-permute-start.14 = (bf16[768,256]{1,0:T(8,128)(2,1)S(1)}, bf16[768,256]{1,0:T(8,128)(2,1)S(1)}, u32[]{:S(2)}, u32[]{:S(2)}) collective-permute-start(bf16[768,256]{1,0:T(8,128)(2,1)S(1)} %pad_maximum_fusion), channel_id=1, source_target_pairs={{0,8},{4,12},{8,24},{12,28},{16,0},{20,4},{24,16},{28,20},{1,9},{5... | collective-permute-start | bytes 1179656 | tf_op jit(solution)/shard_map/ppermute | solution.py:45
  39.2 7.1 %collective-permute-start.3 = (bf16[592,256]{1,0:T(8,128)(2,1)S(1)}, bf16[592,256]{1,0:T(8,128)(2,1)S(1)}, u32[]{:S(2)}, u32[]{:S(2)}) collective-permute-start(bf16[592,256]{1,0:T(8,128)(2,1)S(1)} %fusion.1), channel_id=1, source_target_pairs={{0,4},{4,0},{8,12},{12,8},{16,20},{20,16},{24,28},{28,24},{1,5},{5... | collective-permute-start | bytes 909320 | tf_op jit(solution)/shard_map/ppermute | solution.py:30
  39.7 7.9 %collective-permute-start.15 = (bf16[256,256]{1,0:T(8,128)(2,1)S(1)}, bf16[256,256]{1,0:T(8,128)(2,1)S(1)}, u32[]{:S(2)}, u32[]{:S(2)}) collective-permute-start(bf16[256,256]{1,0:T(8,128)(2,1)S(1)} %slice.27), channel_id=1, source_target_pairs={{0,4},{4,0},{8,12},{12,8},{16,20},{20,16},{24,28},{28,24},{1,5},{5... | collective-permute-start | bytes 393224 | tf_op jit(solution)/shard_map/ppermute | solution.py:30
  46.4 6.8 %collective-permute-start.10 = (bf16[576,256]{1,0:T(8,128)(2,1)S(1)}, bf16[576,256]{1,0:T(8,128)(2,1)S(1)}, u32[]{:S(2)}, u32[]{:S(2)}) collective-permute-start(bf16[576,256]{1,0:T(8,128)(2,1)S(1)} %get-tuple-element.37.m0), channel_id=1, source_target_pairs={{0,2},{1,3},{2,0},{3,1},{4,6},{5,7},{6,4},{7,5},{8,10},{9,11},{10,... | collective-permute-start | bytes 884744 | tf_op jit(solution)/shard_map/ppermute | solution.py:30
  48.3 8.1 %collective-permute-start.16 = (bf16[512,256]{1,0:T(8,128)(2,1)S(1)}, bf16[512,256]{1,0:T(8,128)(2,1)S(1)}, u32[]{:S(2)}, u32[]{:S(2)}) collective-permute-start(bf16[512,256]{1,0:T(8,128)(2,1)S(1)} %slice.28), channel_id=1, source_target_pairs={{0,8},{4,12},{8,24},{12,28},{16,0},{20,4},{24,16},{28,20},{1,9},{5... | collective-permute-start | bytes 786440 | tf_op jit(solution)/shard_map/ppermute | solution.py:45
  50.4 6.8 %collective-permute-start.17 = (bf16[512,256]{1,0:T(8,128)(2,1)S(1)}, bf16[512,256]{1,0:T(8,128)(2,1)S(1)}, u32[]{:S(2)}, u32[]{:S(2)}) collective-permute-start(bf16[512,256]{1,0:T(8,128)(2,1)S(1)} %slice.28), channel_id=1, source_target_pairs={{0,4},{4,0},{8,12},{12,8},{16,20},{20,16},{24,28},{28,24},{1,5},{5... | collective-permute-start | bytes 786440 | tf_op jit(solution)/shard_map/ppermute | solution.py:30
  50.4 7.4 %collective-permute-start.9 = (bf16[576,256]{1,0:T(8,128)(2,1)S(1)}, bf16[576,256]{1,0:T(8,128)(2,1)S(1)}, u32[]{:S(2)}, u32[]{:S(2)}) collective-permute-start(bf16[576,256]{1,0:T(8,128)(2,1)S(1)} %get-tuple-element.37.m0), channel_id=1, source_target_pairs={{0,1},{1,0},{2,3},{3,2},{4,5},{5,4},{6,7},{7,6},{8,9},{9,8},{10,11... | collective-permute-start | bytes 884744 | tf_op jit(solution)/shard_map/ppermute | solution.py:30
  53.1 4.6 %collective-permute-start.11 = (bf16[576,256]{1,0:T(8,128)(2,1)S(1)}, bf16[576,256]{1,0:T(8,128)(2,1)S(1)}, u32[]{:S(2)}, u32[]{:S(2)}) collective-permute-start(bf16[576,256]{1,0:T(8,128)(2,1)S(1)} %collective-permute-done.10.m2), channel_id=1, source_target_pairs={{0,1},{1,0},{2,3},{3,2},{4,5},{5,4},{6,7},{7,6},{8,9},{9,8},{10,11... | collective-permute-start | bytes 884744 | tf_op jit(solution)/shard_map/ppermute | solution.py:30
  57.1 6.4 %collective-permute-start.18 = (bf16[512,256]{1,0:T(8,128)(2,1)S(1)}, bf16[512,256]{1,0:T(8,128)(2,1)S(1)}, u32[]{:S(2)}, u32[]{:S(2)}) collective-permute-start(bf16[512,256]{1,0:T(8,128)(2,1)S(1)} %collective-permute-done.16.refs_3_), channel_id=1, source_target_pairs={{0,4},{4,0},{8,12},{12,8},{16,20},{20,16},{24,28},{28,24},{1,5},{5... | collective-permute-start | bytes 786440 | tf_op jit(solution)/shard_map/ppermute | solution.py:30

commit v5 on v4

--- a/solution.py
+++ b/solution.py
@@ -71,14 +71,13 @@
 
 
 def prepare_kernel(
-    x_ref, label_ref, left_ref, z_ref, sort_ref, back_ref, wide
+    x_ref, label_ref, z_ref, sort_ref, back_ref, wide
 ):
     rows, cols, channels = x_ref.shape
     out_rows, out_cols = label_ref.shape
     half = cols // 2
     tokens = out_rows * out_cols
     bucket = tokens // PHASES
-    left_ref[...] = x_ref[:, cols - 1, :]
     def one_row(r, carry):
         for c in range(channels // LANES):
             wide[r, c, pl.ds(0, 8), :] = jnp.zeros((8, LANES), F32)
@@ -118,16 +117,16 @@
 
 
 def conv_kernel(
-    z_ref, w0, w1, w2, w3, proj_ref, sort_ref, left_ref, up_ref, bias_ref,
+    z_ref, packed_ref, w1, w2, w3, sort_ref, left_ref, up_ref, bias_ref,
     out_ref, weight, edge, sems,
 ):
     out_rows, out_cols, wide = z_ref.shape[1:]
     channels = wide // 3
     tokens = out_rows * out_cols
-    shard = w0.shape[0]
+    shard = w1.shape[0]
     mine = lax.axis_index("col")
     copies = []
-    for j, ref in enumerate((w0, w1, w2, w3)):
+    for j, ref in enumerate((packed_ref.at[pl.ds(0, shard)], w1, w2, w3)):
         spot = pl.multiple_of((mine ^ j) * shard, 64)
         copies.append(pltpu.make_async_copy(ref, weight.at[pl.ds(spot, shard)], sems.at[j]))
     for copy in copies:
@@ -162,7 +161,13 @@
     grid = grid + jnp.where(first, side[:, None, :], 0.0)
     pre = grid.reshape(tokens, channels) + bias_ref[...]
     features = jax.nn.gelu(pre).astype(BF16)
-    projected = dot(features, proj_ref[...])
+    projected = jnp.concatenate(
+        [
+            dot(features, packed_ref[at : at + channels])
+            for at in range(shard, packed_ref.shape[0], channels)
+        ],
+        axis=1,
+    )
     centred = projected - jnp.mean(projected, axis=1, keepdims=True)
     spread = jnp.mean(centred * centred, axis=1, keepdims=True)
     scaled = (features.astype(F32) * lax.rsqrt(spread + 1e-05)).astype(BF16)
@@ -343,22 +348,21 @@
     weight_core = flip(conv_weight, "col", 1)
     weight_far = flip(weight_x, "col", 1)
     labels = (phase * 2 + 1 - tissue).astype(F32)
-    left, z, sort, back = call(
+    z, sort, back = call(
         prepare_kernel,
         (
-            jax.ShapeDtypeStruct((in_rows, channels), BF16),
             jax.ShapeDtypeStruct((2, out_rows, out_cols, 3 * channels), BF16),
             jax.ShapeDtypeStruct((tokens, tokens), BF16),
             jax.ShapeDtypeStruct((tokens, tokens), BF16),
         ),
         [VMEM] * 2,
-        (VMEM,) * 4,
+        (VMEM,) * 3,
         [VMEM((in_rows, channels // LANES, in_cols + 8, LANES), F32)],
         (feat_in, labels),
         "prepare",
         24,
     )
-    left = shifted(left, "col")
+    left = shifted(feat_in[:, in_cols - 1], "col")
     up = shifted(jnp.concatenate([left[in_rows - 16 :], feat_in[in_rows - 1]], axis=0), "row")
 
     here = labels[None] == 2.0 * jnp.arange(PHASES, dtype=F32)[:, None, None]
@@ -390,10 +394,14 @@
             pieces.append(ring(pieces[-1]))
         z, *pieces = lax.optimization_barrier((z, *pieces))
 
+    blocks = range(0, width, channels)
+    packed_weight = jnp.concatenate(
+        [conv_weight] + [proj_weight[:, at : at + channels] for at in blocks], axis=0
+    )
     mine = call(
         conv_kernel,
         jax.ShapeDtypeStruct((tokens, channels), BF16),
-        [VMEM] + [ANY] * 4 + [VMEM] * 5,
+        [VMEM, VMEM] + [ANY] * 3 + [VMEM] * 4,
         VMEM,
         [
             VMEM((9 * channels, channels), BF16),
@@ -401,7 +409,7 @@
             pltpu.SemaphoreType.DMA((4,)),
         ],
         (
-            z, conv_weight, weight_core, weight_x, weight_far, proj_weight, sort, left, up,
+            z, packed_weight, weight_core, weight_x, weight_far, sort, left, up,
             conv_bias.reshape(1, channels),
         ),
         "conv",

time: 95.2 us -> 89.6 us (0.941)
  waiting for transfers between devices: 26.2 us -> 23.3 us
  local copies, waits for them, and re-layouts: 4.21 us -> 2.37 us
    unnamed x13 -> x12, local copies, waits for them, and re-layouts: 4.04 us -> 0.2 us
    ppermute x11, starting transfers between devices: 7.54 us -> 10.6 us  [flip(): lax.ppermute(array, axis, [(i, i ^ bits) for i in range(lax.axis_size(axi...]
    ppermute x6, starting transfers between devices: 11.4 us -> 8.91 us  [ring(): return lax.ppermute(array, 'row', pairs)]
    slice x0 -> x2, local copies, waits for them, and re-layouts: none -> 2.01 us  [the longest x1 1.07 us: local(): proj_weight[:, at:at + channels]]
    ppermute x6, waiting for transfers between devices: 11 us -> 9.61 us  [ring(): return lax.ppermute(array, 'row', pairs)]
    ppermute x2, waiting for transfers between devices: 0.99 us -> 0.01 us  [shifted(): lax.ppermute(array, axis, [(i, i + 1) for i in range(lax.axis_size(axis)...]
  transfers between devices with their start and end apart: 19 -> 19, of which waited for: 12 -> 10; matrix products, arithmetic and copies ran while one was open for 1% -> 4% of each run, Pallas kernels for 5% -> 5%
where the time goes in v5:
time: 89.6 us; the launch traced here: 89.3 us
  Pallas kernels  37.5 us (42%)
  starting transfers between devices  24.7 us (28%)
  waiting for transfers between devices  23.3 us (26%)
  local copies, waits for them, and re-layouts  2.37 us (3%)
  other arithmetic  1.15 us (1%)
    pallas_call x6, Pallas kernels, call(): pl.pallas_call(kernel, out_shape=out_shape, in_specs=[pl.BlockSpec(memory...  37.5 us
    ppermute x11, waiting for transfers between devices, flip(): lax.ppermute(array, axis, [(i, i ^ bits) for i in range(lax.axis_size(axi...  13.7 us
    ppermute x11, starting transfers between devices, flip(): lax.ppermute(array, axis, [(i, i ^ bits) for i in range(lax.axis_size(axi...  10.6 us
    ppermute x6, waiting for transfers between devices, ring(): return lax.ppermute(array, 'row', pairs)  9.61 us
    ppermute x6, starting transfers between devices, ring(): return lax.ppermute(array, 'row', pairs)  8.91 us
    ppermute x2, starting transfers between devices, shifted(): lax.ppermute(array, axis, [(i, i + 1) for i in range(lax.axis_size(axis)...  5.2 us
  transfers between devices with their start and end apart: 19, of which 10 were waited for; matrix products, arithmetic and copies ran while one was open for 4% of the time, Pallas kernels for 5%

profile of v5, /device:TPU:0, one launch (start us, length us, event | category | flops | bytes accessed | tf_op | source)
XLA Modules:
  0.0 89.3 jit_solution(11805841475653375725)
XLA Ops:
  0.0 0.5 collective-permute-start.4
  0.5 2.6 %collective-permute-start.5 = (bf16[576,256]{1,0:T(8,128)(2,1)}, bf16[576,256]{1,0:T(8,128)(2,1)S(1)}, u32[]{:S(2)}, u32[]{:S(2)}) collective-permute-start(bf16[576,256]{1,0:T(8,128)(2,1)} %param.8), channel_id=1, source_target_pairs={{0,2},{1,3},{2,0},{3,1},{4,6},{5,7},{6,4},{7,5},{8,10},{9,11},{10,... | collective-permute-start | bytes 884744 | tf_op jit(solution)/shard_map/ppermute | solution.py:30
  3.1 0.7 subtract_convert_fusion.label_ref
  3.8 0.2 convert_reduce_fusion
  4.0 0.1 fusion.2
  4.1 0.1 constant_dynamic-slice_fusion
  4.2 1.6 %collective-permute-start = (bf16[96,640]{1,0:T(8,128)(2,1)S(1)}, bf16[96,640]{1,0:T(8,128)(2,1)S(1)}, u32[]{:S(2)}, u32[]{:S(2)}) collective-permute-start(bf16[96,640]{1,0:T(8,128)(2,1)S(1)} %pad_maximum_fusion.2.refs_0_), channel_id=1, source_target_pairs={{0,8},{4,12},{8,24},{12,28},{16,0},{20,4},{24,16},{28,20},{1,9},{5... | collective-permute-start | bytes 368648 | tf_op jit(solution)/shard_map/ppermute | solution.py:45
  5.9 0.9 %slice.39 = bf16[32,1,256]{2,1,0:T(2,128)(2,1)S(1)} slice(bf16[32,64,256]{2,1,0:T(8,128)(2,1)} %x_ref.1), slice={[0:32], [63:64], [0:256]} | slice | bytes 32768 | tf_op jit(solution)/shard_map/slice | solution.py:365
  6.8 1.8 %collective-permute-start.7 = (bf16[32,256]{1,0:T(8,128)(2,1)S(1)}, bf16[32,256]{1,0:T(8,128)(2,1)S(1)}, u32[]{:S(2)}, u32[]{:S(2)}) collective-permute-start(bf16[32,256]{1,0:T(8,128)(2,1)S(1)} %bitcast.10), channel_id=1, source_target_pairs={{0,1},{1,2},{2,3},{4,5},{5,6},{6,7},{8,9},{9,10},{10,11},{12,13},{... | collective-permute-start | bytes 49160 | tf_op jit(solution)/shard_map/ppermute | solution.py:34
  8.6 1.1 %fusion.3 = (bf16[256,256]{1,0:T(8,128)(2,1)S(1)}, bf16[256,256]{1,0:T(8,128)(2,1)S(1)}, bf16[256,256]{1,0:T(8,128)(2,1)S(1)}) fusion(bf16[256,768]{1,0:T(8,128)(2,1)} %param.10), kind=kLoop, calls=%fused_computation.15 | loop fusion | bytes 786432 | tf_op jit(solution)/shard_map/slice | solution.py:399
  9.7 0.0 copy-start.2
  9.7 0.9 collective-permute-done.refs_1_
  10.6 1.8 %collective-permute-start.1 = (bf16[96,640]{1,0:T(8,128)(2,1)S(1)}, bf16[96,640]{1,0:T(8,128)(2,1)S(1)}, u32[]{:S(2)}, u32[]{:S(2)}) collective-permute-start(bf16[96,640]{1,0:T(8,128)(2,1)S(1)} %collective-permute-done.refs_1_), channel_id=1, source_target_pairs={{0,8},{4,12},{8,24},{12,28},{16,0},{20,4},{24,16},{28,20},{1,9},{5... | collective-permute-start | bytes 368648 | tf_op jit(solution)/shard_map/ppermute | solution.py:45
  12.4 0.0 collective-permute-done.5.w2
  12.4 0.6 collective-permute-start.6
  12.9 3.4 %collective-permute-start.8 = (bf16[80,256]{1,0:T(8,128)(2,1)S(1)}, bf16[80,256]{1,0:T(8,128)(2,1)S(1)}, u32[]{:S(2)}, u32[]{:S(2)}) collective-permute-start(bf16[80,256]{1,0:T(8,128)(2,1)S(1)} %pad_maximum_fusion.3), channel_id=1, source_target_pairs={{0,4},{4,8},{8,12},{12,16},{16,20},{20,24},{24,28},{1,5},{5,9},{9,... | collective-permute-start | bytes 122888 | tf_op jit(solution)/shard_map/ppermute | solution.py:34
  16.4 0.3 collective-permute-done.1.refs_2_
  16.7 1.7 %collective-permute-start.2 = (bf16[96,640]{1,0:T(8,128)(2,1)S(1)}, bf16[96,640]{1,0:T(8,128)(2,1)S(1)}, u32[]{:S(2)}, u32[]{:S(2)}) collective-permute-start(bf16[96,640]{1,0:T(8,128)(2,1)S(1)} %collective-permute-done.1.refs_2_), channel_id=1, source_target_pairs={{0,8},{4,12},{8,24},{12,28},{16,0},{20,4},{24,16},{28,20},{1,9},{5... | collective-permute-start | bytes 368648 | tf_op jit(solution)/shard_map/ppermute | solution.py:45
  18.4 1.1 %prepare.1 = (bf16[2,16,32,768]{3,2,1,0:T(8,128)(2,1)S(1)}, bf16[512,512]{1,0:T(8,128)(2,1)S(1)}, bf16[512,512]{1,0:T(8,128)(2,1)S(1)}) custom-call(bf16[32,64,256]{2,1,0:T(8,128)(2,1)S(1)} %copy-done.1, f32[16,32]{1,0:T(8,128)S(1)} %subtract_convert_fusion.label_ref), custom_call_target="tpu_custom_call" | custom-call | tf_op jit(solution)/shard_map/prepare/pallas_call | solution.py:57
  19.6 2.9 %collective-permute-done.2.refs_3_ = bf16[96,640]{1,0:T(8,128)(2,1)S(1)} collective-permute-done((bf16[96,640]{1,0:T(8,128)(2,1)S(1)}, bf16[96,640]{1,0:T(8,128)(2,1)S(1)}, u32[]{:S(2)}, u32[]{:S(2)}) %collective-permute-start.2) | collective-permute-done | bytes 122912 | tf_op jit(solution)/shard_map/ppermute | solution.py:45
  22.4 0.0 collective-permute-done.8.up_ref
  22.4 0.0 collective-permute-done.4.w1
  22.5 0.0 copy-start.3
  22.5 2.6 %conv.1.f_ref.refs_0_ = bf16[512,256]{1,0:T(8,128)(2,1)S(1)} custom-call(bf16[2,16,32,768]{3,2,1,0:T(8,128)(2,1)S(1)} %get-tuple-element.33.z_ref, bf16[1344,256]{1,0:T(8,128)(2,1)S(1)} %pad_maximum_fusion.packed_ref, bf16[576,256]{1,0:T(8,128)(2,1)S(1)} %collective-permute-done.4.w1, bf16[576,256]{1,0:T(8,128)(2,1)S(1)} %collective-permute-done.5.w2, ...), custom_call_target="tpu_custom_call" | custom-call | tf_op jit(solution)/shard_map/conv/pallas_call | solution.py:57
  25.1 1.4 %collective-permute-start.12 = (bf16[512,256]{1,0:T(8,128)(2,1)S(1)}, bf16[512,256]{1,0:T(8,128)(2,1)S(1)}, u32[]{:S(2)}, u32[]{:S(2)}) collective-permute-start(bf16[512,256]{1,0:T(8,128)(2,1)S(1)} %conv.1.f_ref.refs_0_), channel_id=1, source_target_pairs={{0,8},{4,12},{8,24},{12,28},{16,0},{20,4},{24,16},{28,20},{1,9},{5... | collective-permute-start | bytes 786440 | tf_op jit(solution)/shard_map/ppermute | solution.py:45
  26.5 1.2 %collective-permute-start.13 = (bf16[512,256]{1,0:T(8,128)(2,1)S(1)}, bf16[512,256]{1,0:T(8,128)(2,1)S(1)}, u32[]{:S(2)}, u32[]{:S(2)}) collective-permute-start(bf16[512,256]{1,0:T(8,128)(2,1)S(1)} %conv.1.f_ref.refs_0_), channel_id=1, source_target_pairs={{0,4},{4,0},{8,12},{12,8},{16,20},{20,16},{24,28},{28,24},{1,5},{5... | collective-permute-start | bytes 786440 | tf_op jit(solution)/shard_map/ppermute | solution.py:30
  27.7 0.2 copy.10
  27.9 1.0 %merge.1 = (f32[576,256]{1,0:T(8,128)S(1)}, bf16[16,128]{1,0:T(8,128)(2,1)S(1)}) custom-call(bf16[96,640]{1,0:T(8,128)(2,1)S(1)} %pad_maximum_fusion.2.refs_0_, bf16[96,640]{1,0:T(8,128)(2,1)S(1)} %collective-permute-done.refs_1_, bf16[96,640]{1,0:T(8,128)(2,1)S(1)} %collective-permute-done.1.refs_2_, bf16[96,640]{1,0:T(8,128)(2,1)S(1)} %collective-permute-done.2.refs_3_, ...), custom_call_target="tpu_custom_call" | custom-call | tf_op jit(solution)/shard_map/merge/pallas_call | solution.py:57
  28.9 3.7 %collective-permute-done.12.refs_1_ = bf16[512,256]{1,0:T(8,128)(2,1)S(1)} collective-permute-done((bf16[512,256]{1,0:T(8,128)(2,1)S(1)}, bf16[512,256]{1,0:T(8,128)(2,1)S(1)}, u32[]{:S(2)}, u32[]{:S(2)}) %collective-permute-start.12) | collective-permute-done | bytes 262176 | tf_op jit(solution)/shard_map/ppermute | solution.py:45
  32.6 1.2 %collective-permute-done.13.refs_4_ = bf16[512,256]{1,0:T(8,128)(2,1)S(1)} collective-permute-done((bf16[512,256]{1,0:T(8,128)(2,1)S(1)}, bf16[512,256]{1,0:T(8,128)(2,1)S(1)}, u32[]{:S(2)}, u32[]{:S(2)}) %collective-permute-start.13) | collective-permute-done | bytes 262176 | tf_op jit(solution)/shard_map/ppermute | solution.py:30
  33.8 1.6 %collective-permute-start.14 = (bf16[768,256]{1,0:T(8,128)(2,1)S(1)}, bf16[768,256]{1,0:T(8,128)(2,1)S(1)}, u32[]{:S(2)}, u32[]{:S(2)}) collective-permute-start(bf16[768,256]{1,0:T(8,128)(2,1)S(1)} %pad_maximum_fusion.1), channel_id=1, source_target_pairs={{0,8},{4,12},{8,24},{12,28},{16,0},{20,4},{24,16},{28,20},{1,9},{5... | collective-permute-start | bytes 1179656 | tf_op jit(solution)/shard_map/ppermute | solution.py:45
  35.5 2.1 %collective-permute-start.3 = (bf16[592,256]{1,0:T(8,128)(2,1)S(1)}, bf16[592,256]{1,0:T(8,128)(2,1)S(1)}, u32[]{:S(2)}, u32[]{:S(2)}) collective-permute-start(bf16[592,256]{1,0:T(8,128)(2,1)S(1)} %fusion.1), channel_id=1, source_target_pairs={{0,4},{4,0},{8,12},{12,8},{16,20},{20,16},{24,28},{28,24},{1,5},{5... | collective-permute-start | bytes 909320 | tf_op jit(solution)/shard_map/ppermute | solution.py:30
  37.6 0.1 collective-permute-start.15
  37.7 5.5 %collective-permute-done.3 = bf16[592,256]{1,0:T(8,128)(2,1)S(1)} collective-permute-done((bf16[592,256]{1,0:T(8,128)(2,1)S(1)}, bf16[592,256]{1,0:T(8,128)(2,1)S(1)}, u32[]{:S(2)}, u32[]{:S(2)}) %collective-permute-start.3) | collective-permute-done | bytes 303136 | tf_op jit(solution)/shard_map/ppermute | solution.py:30
  43.3 0.1 join.1
  43.3 0.6 collective-permute-start.10
  43.9 0.7 collective-permute-done.15.refs_5_
  44.7 0.7 collective-permute-start.16
  45.4 1.2 %collective-permute-start.17 = (bf16[512,256]{1,0:T(8,128)(2,1)S(1)}, bf16[512,256]{1,0:T(8,128)(2,1)S(1)}, u32[]{:S(2)}, u32[]{:S(2)}) collective-permute-start(bf16[512,256]{1,0:T(8,128)(2,1)S(1)} %slice.44), channel_id=1, source_target_pairs={{0,4},{4,0},{8,12},{12,8},{16,20},{20,16},{24,28},{28,24},{1,5},{5... | collective-permute-start | bytes 786440 | tf_op jit(solution)/shard_map/ppermute | solution.py:30
  46.6 3.5 %collective-permute-done.10.m2 = bf16[576,256]{1,0:T(8,128)(2,1)S(1)} collective-permute-done((bf16[576,256]{1,0:T(8,128)(2,1)S(1)}, bf16[576,256]{1,0:T(8,128)(2,1)S(1)}, u32[]{:S(2)}, u32[]{:S(2)}) %collective-permute-start.10) | collective-permute-done | bytes 294944 | tf_op jit(solution)/shard_map/ppermute | solution.py:30
  50.1 0.0 collective-permute-start.11
  50.1 1.9 %collective-permute-done.16.refs_3_ = bf16[512,256]{1,0:T(8,128)(2,1)S(1)} collective-permute-done((bf16[512,256]{1,0:T(8,128)(2,1)S(1)}, bf16[512,256]{1,0:T(8,128)(2,1)S(1)}, u32[]{:S(2)}, u32[]{:S(2)}) %collective-permute-start.16) | collective-permute-done | bytes 262176 | tf_op jit(solution)/shard_map/ppermute | solution.py:45
  52.0 1.7 %collective-permute-start.18 = (bf16[512,256]{1,0:T(8,128)(2,1)S(1)}, bf16[512,256]{1,0:T(8,128)(2,1)S(1)}, u32[]{:S(2)}, u32[]{:S(2)}) collective-permute-start(bf16[512,256]{1,0:T(8,128)(2,1)S(1)} %collective-permute-done.16.refs_3_), channel_id=1, source_target_pairs={{0,4},{4,0},{8,12},{12,8},{16,20},{20,16},{24,28},{28,24},{1,5},{5... | collective-permute-start | bytes 786440 | tf_op jit(solution)/shard_map/ppermute | solution.py:30
  53.7 0.0 collective-permute-done.9.m1
  53.7 0.0 collective-permute-done.11.m3
  53.7 2.3 %queries.1 = (bf16[4,6,256,256]{3,2,1,0:T(8,128)(2,1)S(1)}, bf16[768,256]{1,0:T(8,128)(2,1)S(1)}) custom-call(bf16[512,256]{1,0:T(8,128)(2,1)S(1)} %conv.1.f_ref.refs_0_, bf16[576,256]{1,0:T(8,128)(2,1)S(1)} %get-tuple-element.35.m0, bf16[576,256]{1,0:T(8,128)(2,1)S(1)} %collective-permute-done.9.m1, bf16[576,256]{1,0:T(8,128)(2,1)S(1)} %collective-permute-done.10.m2, ...), custom_call_target="tpu_custom_call" | custom-call | tf_op jit(solution)/shard_map/queries/pallas_call | solution.py:57
  56.0 2.8 %collective-permute-done.18.refs_7_ = bf16[512,256]{1,0:T(8,128)(2,1)S(1)} collective-permute-done((bf16[512,256]{1,0:T(8,128)(2,1)S(1)}, bf16[512,256]{1,0:T(8,128)(2,1)S(1)}, u32[]{:S(2)}, u32[]{:S(2)}) %collective-permute-start.18) | collective-permute-done | bytes 262176 | tf_op jit(solution)/shard_map/ppermute | solution.py:30
  58.8 30.4 %attend.1 = bf16[512,768]{1,0:T(8,128)(2,1)} custom-call(s32[8,128]{1,0:T(8,128)S(1)} %get-tuple-element.32.counts_ref, bf16[4,6,256,256]{3,2,1,0:T(8,128)(2,1)S(1)} %get-tuple-element.36.q_ref, bf16[768,256]{1,0:T(8,128)(2,1)S(1)} %get-tuple-element.37.v_ref, bf16[512,512]{1,0:T(8,128)(2,1)S(1)} %get-tuple-element.38.back_ref, ...), custom_call_target="tpu_custom_call" | custom-call | tf_op jit(solution)/shard_map/attend/pallas_call | solution.py:57
  (28 shorter events, 0.3 us)
Async XLA Ops:
  0.0 4.1 %copy-start = (bf16[96,2304]{1,0:T(8,128)(2,1)S(1)}, bf16[96,2304]{1,0:T(8,128)(2,1)}, u32[]{:S(2)}) copy-start(bf16[96,2304]{1,0:T(8,128)(2,1)} %param.11) | copy-start | bytes 1327108
  0.0 18.4 %copy-start.4 = (bf16[576,256]{1,0:T(8,128)(2,1)S(1)}, bf16[576,256]{1,0:T(8,128)(2,1)}, u32[]{:S(2)}) copy-start(bf16[576,256]{1,0:T(8,128)(2,1)} %param.8) | copy-start | bytes 884740
  0.0 12.4 %copy-start.1 = (bf16[32,64,256]{2,1,0:T(8,128)(2,1)S(1)}, bf16[32,64,256]{2,1,0:T(8,128)(2,1)}, u32[]{:S(2)}) copy-start(bf16[32,64,256]{2,1,0:T(8,128)(2,1)} %x_ref.1) | copy-start | bytes 3145732
  0.0 22.4 %collective-permute-start.4 = (bf16[576,256]{1,0:T(8,128)(2,1)}, bf16[576,256]{1,0:T(8,128)(2,1)S(1)}, u32[]{:S(2)}, u32[]{:S(2)}) collective-permute-start(bf16[576,256]{1,0:T(8,128)(2,1)} %param.8), channel_id=1, source_target_pairs={{0,1},{1,0},{2,3},{3,2},{4,5},{5,4},{6,7},{7,6},{8,9},{9,8},{10,11... | collective-permute-start | bytes 884744 | tf_op jit(solution)/shard_map/ppermute | solution.py:30
  0.5 11.8 %collective-permute-start.5 = (bf16[576,256]{1,0:T(8,128)(2,1)}, bf16[576,256]{1,0:T(8,128)(2,1)S(1)}, u32[]{:S(2)}, u32[]{:S(2)}) collective-permute-start(bf16[576,256]{1,0:T(8,128)(2,1)} %param.8), channel_id=1, source_target_pairs={{0,2},{1,3},{2,0},{3,1},{4,6},{5,7},{6,4},{7,5},{8,10},{9,11},{10,... | collective-permute-start | bytes 884744 | tf_op jit(solution)/shard_map/ppermute | solution.py:30
  4.2 6.3 %collective-permute-start = (bf16[96,640]{1,0:T(8,128)(2,1)S(1)}, bf16[96,640]{1,0:T(8,128)(2,1)S(1)}, u32[]{:S(2)}, u32[]{:S(2)}) collective-permute-start(bf16[96,640]{1,0:T(8,128)(2,1)S(1)} %pad_maximum_fusion.2.refs_0_), channel_id=1, source_target_pairs={{0,8},{4,12},{8,24},{12,28},{16,0},{20,4},{24,16},{28,20},{1,9},{5... | collective-permute-start | bytes 368648 | tf_op jit(solution)/shard_map/ppermute | solution.py:45
  6.8 5.5 %collective-permute-start.7 = (bf16[32,256]{1,0:T(8,128)(2,1)S(1)}, bf16[32,256]{1,0:T(8,128)(2,1)S(1)}, u32[]{:S(2)}, u32[]{:S(2)}) collective-permute-start(bf16[32,256]{1,0:T(8,128)(2,1)S(1)} %bitcast.10), channel_id=1, source_target_pairs={{0,1},{1,2},{2,3},{4,5},{5,6},{6,7},{8,9},{9,10},{10,11},{12,13},{... | collective-permute-start | bytes 49160 | tf_op jit(solution)/shard_map/ppermute | solution.py:34
  9.7 12.8 %copy-start.2 = (f32[256]{0:T(256)S(1)}, f32[256]{0:T(256)}, u32[]{:S(2)}) copy-start(f32[256]{0:T(256)} %param.9) | copy-start | bytes 3076
  10.6 6.1 %collective-permute-start.1 = (bf16[96,640]{1,0:T(8,128)(2,1)S(1)}, bf16[96,640]{1,0:T(8,128)(2,1)S(1)}, u32[]{:S(2)}, u32[]{:S(2)}) collective-permute-start(bf16[96,640]{1,0:T(8,128)(2,1)S(1)} %collective-permute-done.refs_1_), channel_id=1, source_target_pairs={{0,8},{4,12},{8,24},{12,28},{16,0},{20,4},{24,16},{28,20},{1,9},{5... | collective-permute-start | bytes 368648 | tf_op jit(solution)/shard_map/ppermute | solution.py:45
  12.4 10.1 %collective-permute-start.6 = (bf16[576,256]{1,0:T(8,128)(2,1)S(1)}, bf16[576,256]{1,0:T(8,128)(2,1)S(1)}, u32[]{:S(2)}, u32[]{:S(2)}) collective-permute-start(bf16[576,256]{1,0:T(8,128)(2,1)S(1)} %collective-permute-done.5.w2), channel_id=1, source_target_pairs={{0,1},{1,0},{2,3},{3,2},{4,5},{5,4},{6,7},{7,6},{8,9},{9,8},{10,11... | collective-permute-start | bytes 884744 | tf_op jit(solution)/shard_map/ppermute | solution.py:30
  12.9 9.5 %collective-permute-start.8 = (bf16[80,256]{1,0:T(8,128)(2,1)S(1)}, bf16[80,256]{1,0:T(8,128)(2,1)S(1)}, u32[]{:S(2)}, u32[]{:S(2)}) collective-permute-start(bf16[80,256]{1,0:T(8,128)(2,1)S(1)} %pad_maximum_fusion.3), channel_id=1, source_target_pairs={{0,4},{4,8},{8,12},{12,16},{16,20},{20,24},{24,28},{1,5},{5,9},{9,... | collective-permute-start | bytes 122888 | tf_op jit(solution)/shard_map/ppermute | solution.py:34
  16.7 5.8 %collective-permute-start.2 = (bf16[96,640]{1,0:T(8,128)(2,1)S(1)}, bf16[96,640]{1,0:T(8,128)(2,1)S(1)}, u32[]{:S(2)}, u32[]{:S(2)}) collective-permute-start(bf16[96,640]{1,0:T(8,128)(2,1)S(1)} %collective-permute-done.1.refs_2_), channel_id=1, source_target_pairs={{0,8},{4,12},{8,24},{12,28},{16,0},{20,4},{24,16},{28,20},{1,9},{5... | collective-permute-start | bytes 368648 | tf_op jit(solution)/shard_map/ppermute | solution.py:45
  22.5 5.2 %copy-start.3 = (bf16[256,768]{1,0:T(8,128)(2,1)S(1)}, bf16[256,768]{1,0:T(8,128)(2,1)}, u32[]{:S(2)}) copy-start(bf16[256,768]{1,0:T(8,128)(2,1)} %param.10) | copy-start | bytes 1179652
  25.1 7.5 %collective-permute-start.12 = (bf16[512,256]{1,0:T(8,128)(2,1)S(1)}, bf16[512,256]{1,0:T(8,128)(2,1)S(1)}, u32[]{:S(2)}, u32[]{:S(2)}) collective-permute-start(bf16[512,256]{1,0:T(8,128)(2,1)S(1)} %conv.1.f_ref.refs_0_), channel_id=1, source_target_pairs={{0,8},{4,12},{8,24},{12,28},{16,0},{20,4},{24,16},{28,20},{1,9},{5... | collective-permute-start | bytes 786440 | tf_op jit(solution)/shard_map/ppermute | solution.py:45
  26.5 7.3 %collective-permute-start.13 = (bf16[512,256]{1,0:T(8,128)(2,1)S(1)}, bf16[512,256]{1,0:T(8,128)(2,1)S(1)}, u32[]{:S(2)}, u32[]{:S(2)}) collective-permute-start(bf16[512,256]{1,0:T(8,128)(2,1)S(1)} %conv.1.f_ref.refs_0_), channel_id=1, source_target_pairs={{0,4},{4,0},{8,12},{12,8},{16,20},{20,16},{24,28},{28,24},{1,5},{5... | collective-permute-start | bytes 786440 | tf_op jit(solution)/shard_map/ppermute | solution.py:30
  33.8 10.8 %collective-permute-start.14 = (bf16[768,256]{1,0:T(8,128)(2,1)S(1)}, bf16[768,256]{1,0:T(8,128)(2,1)S(1)}, u32[]{:S(2)}, u32[]{:S(2)}) collective-permute-start(bf16[768,256]{1,0:T(8,128)(2,1)S(1)} %pad_maximum_fusion.1), channel_id=1, source_target_pairs={{0,8},{4,12},{8,24},{12,28},{16,0},{20,4},{24,16},{28,20},{1,9},{5... | collective-permute-start | bytes 1179656 | tf_op jit(solution)/shard_map/ppermute | solution.py:45
  35.5 7.7 %collective-permute-start.3 = (bf16[592,256]{1,0:T(8,128)(2,1)S(1)}, bf16[592,256]{1,0:T(8,128)(2,1)S(1)}, u32[]{:S(2)}, u32[]{:S(2)}) collective-permute-start(bf16[592,256]{1,0:T(8,128)(2,1)S(1)} %fusion.1), channel_id=1, source_target_pairs={{0,4},{4,0},{8,12},{12,8},{16,20},{20,16},{24,28},{28,24},{1,5},{5... | collective-permute-start | bytes 909320 | tf_op jit(solution)/shard_map/ppermute | solution.py:30
  37.6 7.0 %collective-permute-start.15 = (bf16[256,256]{1,0:T(8,128)(2,1)S(1)}, bf16[256,256]{1,0:T(8,128)(2,1)S(1)}, u32[]{:S(2)}, u32[]{:S(2)}) collective-permute-start(bf16[256,256]{1,0:T(8,128)(2,1)S(1)} %slice.43), channel_id=1, source_target_pairs={{0,4},{4,0},{8,12},{12,8},{16,20},{20,16},{24,28},{28,24},{1,5},{5... | collective-permute-start | bytes 393224 | tf_op jit(solution)/shard_map/ppermute | solution.py:30
  43.3 6.8 %collective-permute-start.10 = (bf16[576,256]{1,0:T(8,128)(2,1)S(1)}, bf16[576,256]{1,0:T(8,128)(2,1)S(1)}, u32[]{:S(2)}, u32[]{:S(2)}) collective-permute-start(bf16[576,256]{1,0:T(8,128)(2,1)S(1)} %get-tuple-element.35.m0), channel_id=1, source_target_pairs={{0,2},{1,3},{2,0},{3,1},{4,6},{5,7},{6,4},{7,5},{8,10},{9,11},{10,... | collective-permute-start | bytes 884744 | tf_op jit(solution)/shard_map/ppermute | solution.py:30
  44.7 7.3 %collective-permute-start.16 = (bf16[512,256]{1,0:T(8,128)(2,1)S(1)}, bf16[512,256]{1,0:T(8,128)(2,1)S(1)}, u32[]{:S(2)}, u32[]{:S(2)}) collective-permute-start(bf16[512,256]{1,0:T(8,128)(2,1)S(1)} %slice.44), channel_id=1, source_target_pairs={{0,8},{4,12},{8,24},{12,28},{16,0},{20,4},{24,16},{28,20},{1,9},{5... | collective-permute-start | bytes 786440 | tf_op jit(solution)/shard_map/ppermute | solution.py:45
  45.4 6.6 %collective-permute-start.17 = (bf16[512,256]{1,0:T(8,128)(2,1)S(1)}, bf16[512,256]{1,0:T(8,128)(2,1)S(1)}, u32[]{:S(2)}, u32[]{:S(2)}) collective-permute-start(bf16[512,256]{1,0:T(8,128)(2,1)S(1)} %slice.44), channel_id=1, source_target_pairs={{0,4},{4,0},{8,12},{12,8},{16,20},{20,16},{24,28},{28,24},{1,5},{5... | collective-permute-start | bytes 786440 | tf_op jit(solution)/shard_map/ppermute | solution.py:30
  46.6 7.1 %collective-permute-start.9 = (bf16[576,256]{1,0:T(8,128)(2,1)S(1)}, bf16[576,256]{1,0:T(8,128)(2,1)S(1)}, u32[]{:S(2)}, u32[]{:S(2)}) collective-permute-start(bf16[576,256]{1,0:T(8,128)(2,1)S(1)} %get-tuple-element.35.m0), channel_id=1, source_target_pairs={{0,1},{1,0},{2,3},{3,2},{4,5},{5,4},{6,7},{7,6},{8,9},{9,8},{10,11... | collective-permute-start | bytes 884744 | tf_op jit(solution)/shard_map/ppermute | solution.py:30
  50.1 3.6 %collective-permute-start.11 = (bf16[576,256]{1,0:T(8,128)(2,1)S(1)}, bf16[576,256]{1,0:T(8,128)(2,1)S(1)}, u32[]{:S(2)}, u32[]{:S(2)}) collective-permute-start(bf16[576,256]{1,0:T(8,128)(2,1)S(1)} %collective-permute-done.10.m2), channel_id=1, source_target_pairs={{0,1},{1,0},{2,3},{3,2},{4,5},{5,4},{6,7},{7,6},{8,9},{9,8},{10,11... | collective-permute-start | bytes 884744 | tf_op jit(solution)/shard_map/ppermute | solution.py:30
  52.0 6.9 %collective-permute-start.18 = (bf16[512,256]{1,0:T(8,128)(2,1)S(1)}, bf16[512,256]{1,0:T(8,128)(2,1)S(1)}, u32[]{:S(2)}, u32[]{:S(2)}) collective-permute-start(bf16[512,256]{1,0:T(8,128)(2,1)S(1)} %collective-permute-done.16.refs_3_), channel_id=1, source_target_pairs={{0,4},{4,0},{8,12},{12,8},{16,20},{20,16},{24,28},{28,24},{1,5},{5... | collective-permute-start | bytes 786440 | tf_op jit(solution)/shard_map/ppermute | solution.py:30
